TPU v7x, 256 devices: a whole 4x4x8 slice. The times are simulated.
256 devices in a mesh: adapter: 32 (over y, z), tensor: 8 (over x, core).
Axes of the slice: x: 4, y: 4, z: 8, core: 2. Of those that a mesh axis runs over, the one named last changes fastest.
Arguments:
- queries: bfloat16 [1536, 8192], P('adapter', 'tensor'), may hold values from -2000 to 2000
- cache_keys: bfloat16 [1536, 8, 32, 128], P('adapter', 'tensor'), may hold values from -6 to 6
- cache_values: bfloat16 [1536, 8, 32, 128], P('adapter', 'tensor'), may hold values from -6 to 6
- new_keys: bfloat16 [1536, 1024], P('adapter', 'tensor'), may hold values from -7 to 7
- new_values: bfloat16 [1536, 1024], P('adapter', 'tensor'), may hold values from -6 to 6
- cache_lengths: int32 [1536], P('adapter'), may hold values from 1 to 32, as said below
- out_weight: bfloat16 [8192, 4096], P('tensor'), may hold values from -0.0625 to 0.0625
- adapter_down: bfloat16 [8192, 32768], P('tensor', 'adapter'), may hold values from -0.0625 to 0.0625
- adapter_up: bfloat16 [32768, 4096], P('adapter', 'tensor'), may hold values from -0.75 to 0.75
- adapter_ids: int32 [1536, 4], P('adapter'), may hold values from 0 to 511, as said below
- hub_weights: float32 [1536, 4], P('adapter'), may hold values from -1.5 to 1.5
Outputs:
- layer_out: bfloat16 [1536, 4096], P('adapter', 'tensor')
Inputs may be any that keep to these rules, and one draw needn't show every extreme that they name: `adapter_ids`: the 4 adapters of a row are distinct; adapter a is held by index a // 16 of the adapter axis. Among the 192 row-adapter pairs of one device's rows at most 24 name adapters held by one index, and in every draw one index takes exactly 24 pairs from every device. `cache_lengths`: among each device's 48 rows at least one has length 32.
All inputs are finite; a program needn't handle non-finite values.
Results may differ from a plain program's by a relative error of at most 0.011.
Values may be sent and summed in bfloat16 or wider, within the bound.
No kernel may reach another device: no remote copies, remote signals or barrier semaphores. Data moves between devices by JAX's collectives and lax.ppermute only.
A program may use at most 128 MiB of HBM per device.

v0:
```python
import functools
import math

import jax
import jax.numpy as jnp
from jax import lax
from jax.sharding import PartitionSpec as P

HEADS = 64
KV_HEADS = 8
HEAD_DIM = 128
RANK = 64
ADP_DEV = 16
TOPA = 4
CAP = 24


def slot_positions(flat_ids, owner_count):
    owners = flat_ids // ADP_DEV
    marks = (owners[:, None] == jnp.arange(owner_count)[None, :]).astype(jnp.int32)
    earlier = jnp.cumsum(marks, axis=0) - marks
    places = jnp.sum(earlier * marks, axis=1)
    return (owners, places)


def local(
    queries,
    cache_keys,
    cache_values,
    new_keys,
    new_values,
    cache_lengths,
    out_weight,
    adapter_down,
    adapter_up,
    adapter_ids,
    hub_weights,
):
    rows_here = queries.shape[0]
    feats_here = queries.shape[1]
    kv_here = cache_keys.shape[1]
    cache_len = cache_keys.shape[2]
    group_size = HEADS // KV_HEADS
    owner_count = lax.axis_size("adapter")
    own_index = lax.axis_index("adapter")
    query_heads = queries.reshape(rows_here, kv_here, group_size, HEAD_DIM)
    scale_factor = 1.0 / math.sqrt(HEAD_DIM)
    cached_scores = (
        jnp.einsum("rkgd,rkld->rkgl", query_heads, cache_keys, preferred_element_type=jnp.float32)
        * scale_factor
    )
    fresh_keys = new_keys.reshape(rows_here, kv_here, HEAD_DIM)
    new_scores = (
        jnp.einsum("rkgd,rkd->rkg", query_heads, fresh_keys, preferred_element_type=jnp.float32)
        * scale_factor
    )
    usable = (jnp.arange(cache_len)[None, :] < cache_lengths[:, None])[:, None, None, :]
    cached_scores = jnp.where(usable, cached_scores, -jnp.inf)
    highest = jnp.maximum(jnp.max(cached_scores, axis=-1), new_scores)
    cached_probs = jnp.where(usable, jnp.exp(cached_scores - highest[..., None]), 0.0)
    new_probs = jnp.exp(new_scores - highest)
    totals = jnp.sum(cached_probs, axis=-1) + new_probs
    new_weights = lax.optimization_barrier(new_probs.astype(jnp.bfloat16))
    summed = jnp.einsum(
        "rkgl,rkld->rkgd",
        cached_probs.astype(jnp.bfloat16),
        cache_values,
        preferred_element_type=jnp.float32,
    )
    fresh_values = new_values.reshape(rows_here, kv_here, 1, HEAD_DIM).astype(jnp.float32)
    summed = summed + new_weights.astype(jnp.float32)[..., None] * fresh_values
    attended = (summed / totals[..., None]).astype(jnp.bfloat16).reshape(rows_here, feats_here)
    flat_ids = adapter_ids.reshape(-1)
    owners, places = slot_positions(flat_ids, owner_count)
    home_slots = owners * CAP + places
    pair_rows = jnp.arange(flat_ids.shape[0]) // TOPA
    every_rows, every_ids = (
        lax.all_gather(attended, "adapter", axis=0, tiled=True),
        lax.all_gather(adapter_ids, "adapter", axis=0, tiled=True),
    )
    projected = jnp.dot(every_rows, adapter_down, preferred_element_type=jnp.float32).reshape(
        -1, ADP_DEV, RANK
    )
    every_local = every_ids % ADP_DEV
    selector = (every_local[..., None] == jnp.arange(ADP_DEV)).astype(jnp.float32)
    pair_ranks = jnp.einsum("nak,nja->njk", projected, selector, precision=lax.Precision.HIGHEST)
    every_owners, every_places = jax.vmap(
        functools.partial(slot_positions, owner_count=owner_count)
    )(every_ids.reshape(owner_count, -1))
    targets = jnp.where(
        every_owners == own_index,
        jnp.arange(owner_count)[:, None] * CAP + every_places,
        owner_count * CAP,
    ).reshape(-1)
    rank_buffer = (
        jnp.zeros((owner_count * CAP, RANK), jnp.float32)
        .at[targets]
        .set(pair_ranks.reshape(-1, RANK), mode="drop")
    )
    rank_buffer = rank_buffer.reshape(owner_count, CAP, RANK)
    owner_ids = (
        jnp.full((owner_count * CAP,), -1, jnp.int32)
        .at[targets]
        .set(every_local.reshape(-1), mode="drop")
    )
    owner_ids = owner_ids.reshape(owner_count, CAP)
    rank_buffer = lax.psum(rank_buffer, "tensor")
    rank_home = lax.all_to_all(
        rank_buffer.reshape(owner_count, CAP * RANK),
        "adapter",
        split_axis=0,
        concat_axis=0,
        tiled=True,
    )
    rank_home = rank_home.reshape(owner_count * CAP, RANK)
    pair_lowered = rank_home[home_slots].reshape(rows_here, TOPA, RANK)
    folded = jnp.sum(hub_weights[:, :, None] * pair_lowered, axis=1)
    mixed = folded.astype(jnp.bfloat16)
    mixed_send = (
        jnp.zeros((owner_count * CAP, RANK), jnp.bfloat16).at[home_slots].set(mixed[pair_rows])
    )
    mixed_recv = lax.all_to_all(
        mixed_send.reshape(owner_count, CAP * RANK),
        "adapter",
        split_axis=0,
        concat_axis=0,
        tiled=True,
    )
    mixed_recv = mixed_recv.reshape(owner_count * CAP, RANK)
    picker_up = (owner_ids.reshape(-1)[:, None] == jnp.arange(ADP_DEV)[None, :]).astype(
        jnp.bfloat16
    )
    expanded = (picker_up[:, :, None] * mixed_recv[:, None, :]).reshape(
        owner_count * CAP, ADP_DEV * RANK
    )
    raised = jnp.dot(expanded, adapter_up, preferred_element_type=jnp.float32).astype(jnp.bfloat16)
    raised = raised.reshape(owner_count, CAP, -1)
    raised_home = lax.all_to_all(raised, "adapter", split_axis=0, concat_axis=0, tiled=True)
    raised_home = raised_home.reshape(owner_count * CAP, -1)
    pair_raised = raised_home[home_slots].reshape(rows_here, TOPA, -1).astype(jnp.float32)
    delta = jnp.sum(hub_weights[:, :, None] * pair_raised, axis=1)
    frozen_part = jnp.dot(attended, out_weight, preferred_element_type=jnp.float32)
    frozen_share = lax.psum_scatter(frozen_part, "tensor", scatter_dimension=1, tiled=True)
    return (frozen_share + delta).astype(jnp.bfloat16)


def solution(mesh):
    return jax.shard_map(
        local,
        mesh=mesh,
        in_specs=(
            P("adapter", "tensor"),
            P("adapter", "tensor", None, None),
            P("adapter", "tensor", None, None),
            P("adapter", "tensor"),
            P("adapter", "tensor"),
            P("adapter"),
            P("tensor", None),
            P("tensor", "adapter"),
            P("adapter", "tensor"),
            P("adapter", None),
            P("adapter", None),
        ),
        out_specs=P("adapter", "tensor"),
        check_vma=False,
    )
```

profile of v0, /device:TPU:32, one launch (start us, length us, event | category | flops | bytes accessed | tf_op | source)
XLA Modules:
  0.0 333.5 jit_solution(3575160576000059676)
XLA Ops:
  6.5 0.9 iota_compare_fusion.7
  7.4 0.9 copy.61
  8.3 0.9 fusion.28
  9.2 1.4 fusion.35
  11.6 1.3 fusion.4
  13.6 51.2 %all-gather = s32[32,48,4]{1,2,0:T(4,128)S(1)} all-gather(s32[1,48,4]{1,2,0:T(4,128)S(1)} %bitcast.89), channel_id=1, replica_groups=mesh['adapter'=32,'tensor'=8] {'adapter'}, dimensions={0}, use_global_device_ids=true | all-gather | bytes 25344 | tf_op jit(solution)/shard_map/all_gather | solution.py:79
  65.0 1.2 copy.35
  66.6 1.2 copy.44
  68.1 1.1 copy_bitcast_fusion
  69.3 32.3 %reduce-window.14 = s32[32,32,2,128]{3,1,2,0:T(8,128)S(1)} reduce-window(s32[32,32,2,128]{3,1,2,0:T(8,128)} %copy_bitcast_fusion, s32[]{:T(128)} %constant.76.clone.1), window={size=1x1x1x128 pad=0_0x0_0x0_0x127_0}, to_apply=%region_3.4 | reduce-window | flops 33292288 | bytes 2097156 | tf_op jit(solution)/shard_map/reduce-window
  101.6 1.3 slice.30
  102.9 1.7 copy.40
  105.5 1.7 reshape.466
  108.3 7.3 %fusion.36 = f32[1536,1024]{0,1:T(8,128)} fusion(bf16[1536,1024]{1,0:T(8,128)(2,1)} %all-gather.3.cloned.1.call-done, bf16[1024,1024]{1,0:T(8,128)(2,1)S(1)} %copy-done), kind=kOutput, calls=%fused_computation.104 | convolution fusion | flops 3221225472 | bytes 11534336 | tf_op jit(solution)/shard_map/dot_general | solution.py:81
  115.6 11.3 %copy.51 = f32[1536,16,64]{2,1,0:T(8,128)} copy(f32[1536,16,64]{0,2,1:T(8,128)} %bitcast.73) | data formatting | bytes 12582912 | tf_op jit(solution)/shard_map/reshape | solution.py:81
  127.0 11.0 %fusion = f32[1536,4,64]{2,1,0:T(4,128)} fusion(f32[1536,16,64]{2,1,0:T(8,128)} %copy.51, s32[1536,4]{1,0:T(8,128)S(1)} %copy-done.1), kind=kOutput, calls=%fused_computation.7 | convolution fusion | flops 75595776 | bytes 7888896 | tf_op jit(solution)/shard_map/nak,nja->njk/dot_general | solution.py:86
  138.0 16.0 %scatter_custom_fusion.1 = f32[768,64]{1,0:T(8,128)S(1)} fusion(s32[6144]{0:T(1024)S(1)} %bitcast.87, f32[6144,64]{1,0:T(8,128)} %bitcast.74, f32[]{:T(128)} %constant.73.clone.1), kind=kCustom, calls=%fused_computation.28 | custom fusion | bytes 197120 | tf_op jit(solution)/shard_map/scatter | solution.py:98
  154.8 63.0 %all-reduce.4.cloned.1.call-done = f32[32,1,1536]{2,0,1:T(8,128)} async-done(((f32[32,1,1536]{2,0,1:T(8,128)}), f32[32,1,1536]{2,0,1:T(8,128)}) %all-reduce.4.cloned.1.call-update) | async-done | bytes 196624 | tf_op jit(solution)/shard_map/psum | solution.py:107
  217.8 1.8 copy.52
  219.7 10.1 %all-to-all-start = ((f32[32,1,1536]{2,1,0:T(1,128)}), f32[32,1,1536]{2,1,0:T(1,128)S(1)}, u32[]{:S(2)}, u32[]{:S(2)}) async-start(f32[32,1,1536]{2,1,0:T(1,128)} %copy.52), calls=%async_computation.1 | async-start | bytes 393216 | tf_op jit(solution)/shard_map/all_to_all | solution.py:108
  230.3 23.0 %scatter_custom_fusion = s32[768]{0:T(1024)S(1)} fusion(s32[6144]{0:T(1024)S(1)} %bitcast.88, s32[6144]{0:T(1024)S(1)} %reshape.515, s32[]{:T(128)} %constant.74.clone.1), kind=kCustom, calls=%fused_computation.94 | custom fusion | bytes 3076 | tf_op jit(solution)/shard_map/scatter | solution.py:104
  254.8 1.6 scatter_custom_fusion.2
  257.0 1.2 reduce.8
  258.8 9.8 %all-to-all-start.1 = ((bf16[32,2,768]{2,1,0:T(2,128)(2,1)}), bf16[32,2,768]{2,1,0:T(2,128)(2,1)S(1)}, u32[]{:S(2)}, u32[]{:S(2)}) async-start(bf16[32,2,768]{2,1,0:T(2,128)(2,1)} %reshape.554), calls=%async_computation.2 | async-start | bytes 196608 | tf_op jit(solution)/shard_map/all_to_all | solution.py:122
  268.6 9.4 %all-to-all-done.1 = bf16[32,2,768]{2,1,0:T(2,128)(2,1)S(1)} async-done(((bf16[32,2,768]{2,1,0:T(2,128)(2,1)}), bf16[32,2,768]{2,1,0:T(2,128)(2,1)S(1)}, u32[]{:S(2)}, u32[]{:S(2)}) %all-to-all-start.1) | async-done | bytes 98336 | tf_op jit(solution)/shard_map/all_to_all | solution.py:122
  279.1 3.1 convolution_convert_fusion
  282.3 4.5 %all-to-all-start.2 = ((bf16[32,24,512]{2,1,0:T(8,128)(2,1)}), bf16[32,24,512]{2,1,0:T(8,128)(2,1)S(1)}, u32[]{:S(2)}, u32[]{:S(2)}) async-start(bf16[32,24,512]{2,1,0:T(8,128)(2,1)} %bitcast.76), calls=%async_computation.3 | async-start | bytes 1572864 | tf_op jit(solution)/shard_map/all_to_all | solution.py:138
  286.9 5.8 %fusion.34 = f32[48,4096]{1,0:T(8,128)} fusion(bf16[1024,4096]{1,0:T(8,128)(2,1)} %param.17, bf16[6,8,8,128]{3,2,1,0:T(8,128)(2,1)S(1)} %bitcast.78), kind=kOutput, calls=%fused_computation.102 | convolution fusion | flops 402653184 | bytes 9273344 | tf_op jit(solution)/shard_map/dot_general | solution.py:142
  292.7 13.6 %all-to-all-done.2 = bf16[32,24,512]{2,1,0:T(8,128)(2,1)S(1)} async-done(((bf16[32,24,512]{2,1,0:T(8,128)(2,1)}), bf16[32,24,512]{2,1,0:T(8,128)(2,1)S(1)}, u32[]{:S(2)}, u32[]{:S(2)}) %all-to-all-start.2) | async-done | bytes 786464 | tf_op jit(solution)/shard_map/all_to_all | solution.py:138
  306.3 1.0 gather_fusion.1
  307.7 17.7 %reduce-scatter.2.cloned.1.call-done = f32[48,512]{1,0:T(8,128)} async-done(((f32[48,4096]{1,0:T(8,128)}), f32[48,512]{1,0:T(8,128)}) %reduce-scatter.2.cloned.1.call-update) | async-done | bytes 98320 | tf_op jit(solution)/shard_map/reduce_scatter | solution.py:143
  325.4 1.5 add_convert_fusion
  (72 shorter events, 10.1 us)
Async XLA Ops:
  6.5 101.8 %copy-start = (bf16[1024,1024]{1,0:T(8,128)(2,1)S(1)}, bf16[1024,1024]{1,0:T(8,128)(2,1)}, u32[]{:S(2)}) copy-start(bf16[1024,1024]{1,0:T(8,128)(2,1)} %param.18) | copy-start | bytes 6291460
  6.5 7.1 %copy-start.2 = (s32[48,4]{0,1:T(4,128)S(1)}, s32[48,4]{0,1:T(4,128)}, u32[]{:S(2)}) copy-start(s32[48,4]{0,1:T(4,128)} %param.20) | copy-start | bytes 2308
  6.5 101.8 %all-gather.3.cloned.1.call-start = ((), (), s32[]{:S(2)}) async-start(), calls=%async_computation.5 | async-start | bytes 3244032 | tf_op jit(solution)/shard_map/all_gather | solution.py:78
  13.6 204.3 %all-reduce.4.cloned.1.call-start = ((), (), s32[]{:S(2)}) async-start(), calls=%async_computation.6 | async-start | bytes 393216 | tf_op jit(solution)/shard_map/psum | solution.py:107
  115.6 11.3 %copy-start.1 = (s32[1536,4]{1,0:T(8,128)S(1)}, s32[1536,4]{1,0:T(8,128)}, u32[]{:S(2)}) copy-start(s32[1536,4]{1,0:T(8,128)} %copy.44) | copy-start | bytes 73732
  127.0 103.2 %copy-start.3 = (f32[48,4]{0,1:T(4,128)S(1)}, f32[48,4]{0,1:T(4,128)}, u32[]{:S(2)}) copy-start(f32[48,4]{0,1:T(4,128)} %param.21) | copy-start | bytes 2308
  219.7 33.7 %all-to-all-start = ((f32[32,1,1536]{2,1,0:T(1,128)}), f32[32,1,1536]{2,1,0:T(1,128)S(1)}, u32[]{:S(2)}, u32[]{:S(2)}) async-start(f32[32,1,1536]{2,1,0:T(1,128)} %copy.52), calls=%async_computation.1 | async-start | bytes 393216 | tf_op jit(solution)/shard_map/all_to_all | solution.py:108
  258.8 19.2 %all-to-all-start.1 = ((bf16[32,2,768]{2,1,0:T(2,128)(2,1)}), bf16[32,2,768]{2,1,0:T(2,128)(2,1)S(1)}, u32[]{:S(2)}, u32[]{:S(2)}) async-start(bf16[32,2,768]{2,1,0:T(2,128)(2,1)} %reshape.554), calls=%async_computation.2 | async-start | bytes 196608 | tf_op jit(solution)/shard_map/all_to_all | solution.py:122
  282.3 24.0 %all-to-all-start.2 = ((bf16[32,24,512]{2,1,0:T(8,128)(2,1)}), bf16[32,24,512]{2,1,0:T(8,128)(2,1)S(1)}, u32[]{:S(2)}, u32[]{:S(2)}) async-start(bf16[32,24,512]{2,1,0:T(8,128)(2,1)} %bitcast.76), calls=%async_computation.3 | async-start | bytes 1572864 | tf_op jit(solution)/shard_map/all_to_all | solution.py:138
  286.8 38.6 %reduce-scatter.2.cloned.1.call-start = ((), (), s32[]{:S(2)}) async-start(), calls=%async_computation.4 | async-start | bytes 884736 | tf_op jit(solution)/shard_map/reduce_scatter | solution.py:143
Sparse Core Ops, SparseCore 0:
  13.7 81.8 all-gather.2
  154.9 62.8 all-reduce.3
  292.8 32.5 reduce-scatter.1
where the time goes:
time: 337 us; the launch traced here: 333 us
  waiting for transfers between devices  104 us (31%)
  local copies, waits for them, and re-layouts  68.1 us (20%)
  blocking collectives  51.2 us (15%)
  other arithmetic  41.5 us (12%)
  matrix products  30.9 us (9%)
  starting transfers between devices  24.5 us (7%)
  between operations  13.5 us (4%)
    psum x1, waiting for transfers between devices, local(): rank_buffer = lax.psum(rank_buffer, 'tensor')  63 us
    all_gather x1, blocking collectives, local(): lax.all_gather(adapter_ids, 'adapter', axis=0, tiled=True)  51.2 us
    another operation x8, other arithmetic  34.6 us
    scatter x1, local copies, waits for them, and re-layouts, local(): owner_ids = jnp.full((owner_count * CAP,), -1, jnp.int32).at[targets].set...  23 us
    reduce_scatter x1, waiting for transfers between devices, local(): lax.psum_scatter(frozen_part, 'tensor', scatter_dimension=1, tiled=True)  17.7 us
    scatter x1, local copies, waits for them, and re-layouts, local(): rank_buffer = jnp.zeros((owner_count * CAP, RANK), jnp.float32).at[target...  16 us
    all_to_all x1, waiting for transfers between devices, local(): lax.all_to_all(raised, 'adapter', split_axis=0, concat_axis=0, tiled=True)  13.6 us
    reshape x1, local copies, waits for them, and re-layouts, local(): jnp.dot(every_rows, adapter_down, preferred_element_type=jnp.float32)  11.3 us
  transfers between devices with their start and end apart: 6, of which 4 were waited for; matrix products, arithmetic and copies ran while one was open for 22% of the time, Pallas kernels for 0%

commit v1 on v0

v1 whole, which is shorter than its diff:
```python
import functools
import math

import jax
import jax.numpy as jnp
from jax import lax
from jax.experimental import pallas as pl
from jax.experimental.pallas import tpu as pltpu
from jax.sharding import PartitionSpec as P

HEADS = 64
KV_HEADS = 8
GROUP = HEADS // KV_HEADS
HEAD_DIM = 128
RANK = 64
ADP_DEV = 16
TOPA = 4
CAP = 24
ROWS = 48
OWNERS = 32
PART = 8
PARTS = CAP // PART
LINES = OWNERS * PART
FEATS = GROUP * HEAD_DIM
COLS = 512
TENSOR = 8
CHUNK = 16
BF = jnp.bfloat16
F32 = jnp.float32


def iota(shape, dim):
    return lax.broadcasted_iota(jnp.int32, shape, dim)


def dot(a, b, contract=((1,), (0,))):
    return lax.dot_general(a, b, (contract, ((), ())), preferred_element_type=F32)


def split_parts(x):
    high = x.astype(BF)
    low = (x - high.astype(F32)).astype(BF)
    return high, low


def attend_kernel(q, ck, cv, nk, nv, lens, ids, hub, att, picks, pay):
    scale = 1.0 / math.sqrt(HEAD_DIM)
    keys = CHUNK * 32
    wide = CHUNK * GROUP
    row_of = iota((wide, keys), 0) & (CHUNK - 1)
    col = iota((wide, keys), 1)
    for c in range(ROWS // CHUNK):
        rows = pl.ds(c * CHUNK, CHUNK)
        qc = q[rows, :]
        qs = jnp.concatenate([qc[:, h * HEAD_DIM : (h + 1) * HEAD_DIM] for h in range(GROUP)], axis=0)
        kc = ck[pl.ds(c * keys, keys), :]
        vc = cv[pl.ds(c * keys, keys), :]
        scores = dot(qs, kc, ((1,), (1,))) * scale
        held = jnp.concatenate([lens[rows, :]] * GROUP, axis=0)
        usable = (row_of == (col >> 5)) & ((col & 31) < held)
        scores = jnp.where(usable, scores, -jnp.inf)
        fresh_k = jnp.concatenate([nk[rows, :].astype(F32)] * GROUP, axis=0)
        fresh_v = jnp.concatenate([nv[rows, :].astype(F32)] * GROUP, axis=0)
        new_scores = jnp.sum(qs.astype(F32) * fresh_k, axis=1, keepdims=True) * scale
        highest = jnp.maximum(jnp.max(scores, axis=1, keepdims=True), new_scores)
        probs = jnp.exp(scores - highest)
        new_probs = jnp.exp(new_scores - highest)
        totals = jnp.sum(probs, axis=1, keepdims=True) + new_probs
        summed = dot(probs.astype(BF), vc) + new_probs.astype(BF).astype(F32) * fresh_v
        out = (summed / totals).astype(BF)
        for h in range(GROUP):
            att[rows, h * HEAD_DIM : (h + 1) * HEAD_DIM] = out[h * CHUNK : (h + 1) * CHUNK, :]

    owner_of_line = iota((ROWS, LINES), 1) >> 3
    named = jnp.zeros((ROWS, LINES), jnp.bool_)
    adapter_of_col = iota((ROWS, OWNERS * ADP_DEV), 1)
    coef = jnp.zeros((ROWS, OWNERS * ADP_DEV), F32)
    for j in range(TOPA):
        idj = ids[:, j : j + 1]
        named = named | ((idj >> 4) == owner_of_line)
        coef = coef + jnp.where(idj == adapter_of_col, hub[:, j : j + 1], 0.0)
    earlier = (iota((ROWS, ROWS), 1) < iota((ROWS, ROWS), 0)).astype(BF)
    place = dot(earlier, named.astype(BF)).astype(jnp.int32)
    place = jnp.where(named, place, -1)
    spot = iota((ROWS, LINES), 1) & (PART - 1)
    high, low = split_parts(coef)
    shape = (LINES, OWNERS * ADP_DEV)
    mine = (iota(shape, 0) >> 3) == (iota(shape, 1) >> 4)
    fold_shape = (OWNERS * ADP_DEV, 128)
    within = iota(fold_shape, 0) & (ADP_DEV - 1)
    lane = iota(fold_shape, 1)
    meta = jnp.zeros((LINES, 128), F32)
    everything = att[...]
    for g in range(PARTS):
        pick = (place == spot + g * PART).astype(BF)
        picks[pl.ds(g * ROWS, ROWS), :] = pick
        pay[:, g * FEATS : (g + 1) * FEATS] = dot(pick, everything, ((0,), (0,))).astype(BF)
        for k, piece in enumerate((high, low)):
            spread = jnp.where(mine, dot(pick, piece, ((0,), (0,))), 0.0).astype(BF)
            fold = (lane == within + (g * 32 + k * ADP_DEV)).astype(BF)
            meta = meta + dot(spread, fold)
    pay[:, PARTS * FEATS :] = meta.astype(BF)


def coefs_of(meta, g):
    shape = (128, ADP_DEV * RANK)
    line = iota(shape, 0)
    adapter = iota(shape, 1) >> 6
    spread = (line == adapter + g * 32) | (line == adapter + (g * 32 + ADP_DEV))
    return dot(meta, spread.astype(BF))


def join_parts(pieces):
    lane = iota((pieces[0].shape[0], 128), 1)
    first = jnp.where(lane < RANK, pieces[0], pieces[1])
    second = jnp.where(lane < RANK, pieces[2], 0.0)
    return jnp.concatenate([first, second], axis=1)


def lower_kernel(got, down, out):
    meta = got[:, PARTS * FEATS :]
    weights = down[...]
    pieces = []
    for g in range(PARTS):
        lowered = dot(got[:, g * FEATS : (g + 1) * FEATS], weights) * coefs_of(meta, g)
        total = lowered[:, :128]
        for p in range(1, ADP_DEV * RANK // 128):
            total = total + lowered[:, p * 128 : (p + 1) * 128]
        pieces.append(total + pltpu.roll(total, RANK, 1))
    out[...] = join_parts(pieces).astype(BF)


def home_kernel(got, picks, out):
    lane = iota((ROWS, 256), 1)
    total = jnp.zeros((ROWS, 256), F32)
    for g in range(PARTS):
        part = dot(picks[pl.ds(g * ROWS, ROWS), :], got[...])
        total = total + jnp.where((lane >> 6) == g, part, 0.0)
    folded = total[:, :128] + total[:, 128:]
    folded = folded + pltpu.roll(folded, RANK, 1)
    for t in range(TENSOR):
        out[pl.ds(t * ROWS, ROWS), :] = folded


def mix_kernel(got, picks, out):
    total = got[pl.ds(0, ROWS), :]
    for t in range(1, TENSOR):
        total = total + got[pl.ds(t * ROWS, ROWS), :]
    mixed = total.astype(BF)
    pieces = [dot(picks[pl.ds(g * ROWS, ROWS), :], mixed, ((0,), (0,))) for g in range(PARTS)]
    out[...] = join_parts(pieces).astype(BF)


def raise_kernel(got, meta, up, out):
    shape = (256, ADP_DEV * RANK)
    line = iota(shape, 0)
    rank = iota(shape, 1) & (RANK - 1)
    for g in range(PARTS):
        tiled = dot(got[...], (line == rank + g * RANK).astype(BF))
        expanded = (tiled * coefs_of(meta[...], g)).astype(BF)
        out[:, g * COLS : (g + 1) * COLS] = dot(expanded, up[...]).astype(BF)


def final_kernel(got, picks, frozen, out):
    total = frozen[...]
    for g in range(PARTS):
        total = total + dot(picks[pl.ds(g * ROWS, ROWS), :], got[:, g * COLS : (g + 1) * COLS])
    out[...] = total.astype(BF)


def call(kernel, out_shape, *args):
    return pl.pallas_call(
        kernel,
        out_shape=out_shape,
        compiler_params=pltpu.CompilerParams(vmem_limit_bytes=48 * 1024 * 1024),
    )(*args)


def shape_of(*shape, dtype=BF):
    return jax.ShapeDtypeStruct(shape, dtype)


def swap(x, axis):
    return lax.all_to_all(x, axis, split_axis=0, concat_axis=0, tiled=True)


def local(
    queries,
    cache_keys,
    cache_values,
    new_keys,
    new_values,
    cache_lengths,
    out_weight,
    adapter_down,
    adapter_up,
    adapter_ids,
    hub_weights,
):
    attended, picks, payload = call(
        attend_kernel,
        (
            shape_of(ROWS, FEATS),
            shape_of(PARTS * ROWS, LINES),
            shape_of(LINES, PARTS * FEATS + 128),
        ),
        queries,
        cache_keys.reshape(-1, HEAD_DIM),
        cache_values.reshape(-1, HEAD_DIM),
        new_keys,
        new_values,
        cache_lengths.reshape(ROWS, 1),
        adapter_ids,
        hub_weights,
    )
    got = swap(payload, "adapter")
    frozen_part = jnp.dot(attended, out_weight, preferred_element_type=F32)
    got, frozen_part = lax.optimization_barrier((got, frozen_part))
    frozen = lax.psum_scatter(frozen_part, "tensor", scatter_dimension=1, tiled=True)
    lowered = call(lower_kernel, shape_of(LINES, 256), got, adapter_down)
    lowered = swap(lowered, "adapter")
    share = call(home_kernel, shape_of(TENSOR * ROWS, 128, dtype=F32), lowered, picks)
    share = swap(share, "tensor")
    mixed = call(mix_kernel, shape_of(LINES, 256), share, picks)
    mixed = swap(mixed, "adapter")
    meta = got[:, PARTS * FEATS :]
    raised = call(raise_kernel, shape_of(LINES, PARTS * COLS), mixed, meta, adapter_up)
    raised = swap(raised, "adapter")
    return call(final_kernel, shape_of(ROWS, COLS), raised, picks, frozen)


def solution(mesh):
    return jax.shard_map(
        local,
        mesh=mesh,
        in_specs=(
            P("adapter", "tensor"),
            P("adapter", "tensor", None, None),
            P("adapter", "tensor", None, None),
            P("adapter", "tensor"),
            P("adapter", "tensor"),
            P("adapter"),
            P("tensor", None),
            P("tensor", "adapter"),
            P("adapter", "tensor"),
            P("adapter", None),
            P("adapter", None),
        ),
        out_specs=P("adapter", "tensor"),
        check_vma=False,
    )
```

time: 337 us -> 154 us (0.46)
  local copies, waits for them, and re-layouts: 68.1 us -> 9.06 us
  other arithmetic: 41.5 us -> 0 us
  waiting for transfers between devices: 104 us -> 66.3 us
  matrix products: 30.9 us -> 5.93 us
  blocking collectives: 51.2 us -> 26.5 us
  Pallas kernels: 0 us -> 12 us
  starting transfers between devices: 24.5 us -> 20.1 us
    psum x1 -> x0, waiting for transfers between devices: 63 us -> none  [local(): rank_buffer = lax.psum(rank_buffer, 'tensor')]
    all_gather x1 -> x0, blocking collectives: 51.2 us -> none  [local(): lax.all_gather(adapter_ids, 'adapter', axis=0, tiled=True)]
    scatter x3 -> x0, local copies, waits for them, and re-layouts: 40.5 us -> none  [the longest x1 23 us: local(): owner_ids = jnp.full((owner_count * CAP,), -1, jnp.int32).at[targets].set...]
    another operation x8 -> x0, other arithmetic: 34.6 us -> none
    all_to_all x0 -> x2, blocking collectives: none -> 26.5 us  [swap(): return lax.all_to_all(x, axis, split_axis=0, concat_axis=0, tiled=True)]
    dot_general x7 -> x1, matrix products: 30.9 us -> 5.93 us  [local(): frozen_part = jnp.dot(attended, out_weight, preferred_element_type=F32)]
    all_to_all x3, waiting for transfers between devices: 23 us -> 46 us  [swap(): return lax.all_to_all(x, axis, split_axis=0, concat_axis=0, tiled=True)]
    reshape x6 -> x1, local copies, waits for them, and re-layouts: 13.7 us -> 0.74 us  [local(): cache_lengths.reshape(ROWS, 1)]
  transfers between devices with their start and end apart: 6 -> 4, of which waited for: 4 -> 4; matrix products, arithmetic and copies ran while one was open for 22% -> 4% of each run, Pallas kernels for 0% -> 2%
where the time goes in v1:
time: 154 us; the launch traced here: 153 us
  waiting for transfers between devices  66.3 us (43%)
  blocking collectives  26.5 us (17%)
  starting transfers between devices  20.1 us (13%)
  between operations  13.5 us (9%)
  Pallas kernels  12 us (8%)
  local copies, waits for them, and re-layouts  9.06 us (6%)
  matrix products  5.93 us (4%)
    all_to_all x3, waiting for transfers between devices, swap(): return lax.all_to_all(x, axis, split_axis=0, concat_axis=0, tiled=True)  46 us
    all_to_all x2, blocking collectives, swap(): return lax.all_to_all(x, axis, split_axis=0, concat_axis=0, tiled=True)  26.5 us
    all_to_all x3, starting transfers between devices, swap(): return lax.all_to_all(x, axis, split_axis=0, concat_axis=0, tiled=True)  20.1 us
    reduce_scatter x1, waiting for transfers between devices, local(): lax.psum_scatter(frozen_part, 'tensor', scatter_dimension=1, tiled=True)  19.6 us
    pallas_call x6, Pallas kernels, call(): pl.pallas_call(kernel, out_shape=out_shape, compiler_params=pltpu.Compile...  12 us
    unnamed x18, local copies, waits for them, and re-layouts  8.32 us
    dot_general x1, matrix products, local(): frozen_part = jnp.dot(attended, out_weight, preferred_element_type=F32)  5.93 us
  transfers between devices with their start and end apart: 4, of which 4 were waited for; matrix products, arithmetic and copies ran while one was open for 4% of the time, Pallas kernels for 2%

profile of v1, /device:TPU:32, one launch (start us, length us, event | category | flops | bytes accessed | tf_op | source)
XLA Modules:
  0.0 153.4 jit_solution(15087000985758833218)
XLA Ops:
  6.5 0.7 copy.12.lens
  7.3 0.8 copy.13.ids
  8.0 0.8 copy.14.hub
  8.8 0.0 copy-start.2
  8.8 1.0 copy-done.2
  9.8 0.0 copy-start.3
  9.8 1.0 copy-done.3
  10.8 0.9 copy-done.4
  11.7 0.7 copy-done.6
  12.4 0.7 copy-done.7
  13.1 4.1 %shard_map.109 = (bf16[48,1024]{1,0:T(8,128)(2,1)S(1)}, bf16[144,256]{1,0:T(8,128)(2,1)S(1)}, bf16[256,3200]{1,0:T(8,128)(2,1)}) custom-call(bf16[48,1024]{1,0:T(8,128)(2,1)S(1)} %copy-done.4, bf16[1536,128]{1,0:T(8,128)(2,1)S(1)} %bitcast.23, bf16[1536,128]{1,0:T(8,128)(2,1)S(1)} %bitcast.24, bf16[48,128]{1,0:T(8,128)(2,1)S(1)} %copy-done.6, ...), custom_call_target="tpu_custom_call" | custom-call | tf_op jit(solution)/shard_map/pallas_call | solution.py:172
  17.2 11.4 %all-to-all-start = ((bf16[32,8,3200]{2,1,0:T(8,128)(2,1)}), bf16[32,8,3200]{2,1,0:T(8,128)(2,1)S(1)}, u32[]{:S(2)}, u32[]{:S(2)}) async-start(bf16[32,8,3200]{2,1,0:T(8,128)(2,1)} %bitcast.3), calls=%async_computation | async-start | bytes 3276800 | tf_op jit(solution)/shard_map/all_to_all | solution.py:184
  28.5 0.0 copy-start.1
  28.5 5.9 %fusion = f32[48,4096]{1,0:T(8,128)} fusion(bf16[48,1024]{1,0:T(8,128)(2,1)S(1)} %get-tuple-element.11, bf16[1024,4096]{1,0:T(8,128)(2,1)} %param.17), kind=kOutput, calls=%fused_computation | convolution fusion | flops 402653184 | bytes 9273344 | tf_op jit(solution)/shard_map/dot_general | solution.py:217
  34.5 34.3 %all-to-all-done = bf16[32,8,3200]{2,1,0:T(8,128)(2,1)S(1)} async-done(((bf16[32,8,3200]{2,1,0:T(8,128)(2,1)}), bf16[32,8,3200]{2,1,0:T(8,128)(2,1)S(1)}, u32[]{:S(2)}, u32[]{:S(2)}) %all-to-all-start) | async-done | bytes 1638432 | tf_op jit(solution)/shard_map/all_to_all | solution.py:184
  68.8 1.6 %copy-done = bf16[1024,1024]{1,0:T(8,128)(2,1)S(1)} copy-done((bf16[1024,1024]{1,0:T(8,128)(2,1)S(1)}, bf16[1024,1024]{1,0:T(8,128)(2,1)}, u32[]{:S(2)}) %copy-start) | copy-done | bytes 2097176
  70.4 2.8 %shard_map.110 = bf16[256,256]{1,0:T(8,128)(2,1)S(1)} custom-call(bf16[256,3200]{1,0:T(8,128)(2,1)S(1)} %bitcast.15, bf16[1024,1024]{1,0:T(8,128)(2,1)S(1)} %copy-done), custom_call_target="tpu_custom_call" | custom-call | tf_op jit(solution)/shard_map/pallas_call | solution.py:172
  73.2 15.6 %all_to_all.56 = bf16[32,8,256]{2,1,0:T(8,128)(2,1)S(1)} all-to-all(bf16[32,8,256]{2,1,0:T(8,128)(2,1)S(1)} %bitcast.22), channel_id=1, replica_groups=mesh['adapter'=32,'tensor'=8] {'adapter'}, dimensions={0} | all-to-all | bytes 262144 | tf_op jit(solution)/shard_map/all_to_all | solution.py:184
  88.8 0.3 shard_map.111
  89.0 10.9 %all_to_all.57 = f32[8,48,128]{2,1,0:T(8,128)S(1)} all-to-all(f32[8,48,128]{2,1,0:T(8,128)S(1)} %bitcast.18), channel_id=1, replica_groups=mesh['adapter'=32,'tensor'=8] {'tensor'}, dimensions={0} | all-to-all | bytes 393216 | tf_op jit(solution)/shard_map/all_to_all | solution.py:184
  100.0 0.9 shard_map.112
  100.9 4.4 %all-to-all-start.3 = ((bf16[32,8,256]{2,1,0:T(8,128)(2,1)}), bf16[32,8,256]{2,1,0:T(8,128)(2,1)S(1)}, u32[]{:S(2)}, u32[]{:S(2)}) async-start(bf16[32,8,256]{2,1,0:T(8,128)(2,1)} %bitcast.9), calls=%async_computation.3 | async-start | bytes 262144 | tf_op jit(solution)/shard_map/all_to_all | solution.py:184
  105.3 0.0 reduce-scatter.2.cloned.1.call-start
  105.3 0.7 reduce-scatter.2.cloned.1.call-update
  106.0 9.1 %all-to-all-done.3 = bf16[32,8,256]{2,1,0:T(8,128)(2,1)S(1)} async-done(((bf16[32,8,256]{2,1,0:T(8,128)(2,1)}), bf16[32,8,256]{2,1,0:T(8,128)(2,1)S(1)}, u32[]{:S(2)}, u32[]{:S(2)}) %all-to-all-start.3) | async-done | bytes 131104 | tf_op jit(solution)/shard_map/all_to_all | solution.py:184
  115.2 0.0 copy-done.1
  115.2 3.1 %shard_map.113 = bf16[256,1536]{1,0:T(8,128)(2,1)} custom-call(bf16[256,256]{1,0:T(8,128)(2,1)S(1)} %bitcast.20, bf16[256,128]{1,0:T(8,128)(2,1)S(1)} %slice.3.meta, bf16[1024,512]{1,0:T(8,128)(2,1)S(1)} %copy-done.1), custom_call_target="tpu_custom_call" | custom-call | tf_op jit(solution)/shard_map/pallas_call | solution.py:172
  118.3 4.3 %all-to-all-start.4 = ((bf16[32,8,1536]{2,1,0:T(8,128)(2,1)}), bf16[32,8,1536]{2,1,0:T(8,128)(2,1)S(1)}, u32[]{:S(2)}, u32[]{:S(2)}) async-start(bf16[32,8,1536]{2,1,0:T(8,128)(2,1)} %bitcast.11), calls=%async_computation.4 | async-start | bytes 1572864 | tf_op jit(solution)/shard_map/all_to_all | solution.py:184
  122.6 19.6 %reduce-scatter.2.cloned.1.call-done.frozen = f32[48,512]{1,0:T(8,128)} async-done(((f32[48,4096]{1,0:T(8,128)}), f32[48,512]{1,0:T(8,128)}) %reduce-scatter.2.cloned.1.call-update) | async-done | bytes 98320 | tf_op jit(solution)/shard_map/reduce_scatter | solution.py:219
  142.2 2.5 %all-to-all-done.4 = bf16[32,8,1536]{2,1,0:T(8,128)(2,1)S(1)} async-done(((bf16[32,8,1536]{2,1,0:T(8,128)(2,1)}), bf16[32,8,1536]{2,1,0:T(8,128)(2,1)S(1)}, u32[]{:S(2)}, u32[]{:S(2)}) %all-to-all-start.4) | async-done | bytes 786464 | tf_op jit(solution)/shard_map/all_to_all | solution.py:184
  144.8 0.9 copy-done.5
  145.7 0.9 shard_map.114
  (6 shorter events, 0.0 us)
Async XLA Ops:
  8.8 1.0 copy-start.2
  9.8 1.0 copy-start.3
  10.8 0.9 copy-start.4
  11.7 0.7 copy-start.6
  12.4 0.7 copy-start.7
  17.2 51.6 %all-to-all-start = ((bf16[32,8,3200]{2,1,0:T(8,128)(2,1)}), bf16[32,8,3200]{2,1,0:T(8,128)(2,1)S(1)}, u32[]{:S(2)}, u32[]{:S(2)}) async-start(bf16[32,8,3200]{2,1,0:T(8,128)(2,1)} %bitcast.3), calls=%async_computation | async-start | bytes 3276800 | tf_op jit(solution)/shard_map/all_to_all | solution.py:184
  28.5 86.7 %copy-start.1 = (bf16[1024,512]{1,0:T(8,128)(2,1)S(1)}, bf16[1024,512]{1,0:T(8,128)(2,1)}, u32[]{:S(2)}) copy-start(bf16[1024,512]{1,0:T(8,128)(2,1)} %up.1) | copy-start | bytes 3145732
  68.8 1.6 %copy-start = (bf16[1024,1024]{1,0:T(8,128)(2,1)S(1)}, bf16[1024,1024]{1,0:T(8,128)(2,1)}, u32[]{:S(2)}) copy-start(bf16[1024,1024]{1,0:T(8,128)(2,1)} %down.1) | copy-start | bytes 6291460
  100.9 14.3 %all-to-all-start.3 = ((bf16[32,8,256]{2,1,0:T(8,128)(2,1)}), bf16[32,8,256]{2,1,0:T(8,128)(2,1)S(1)}, u32[]{:S(2)}, u32[]{:S(2)}) async-start(bf16[32,8,256]{2,1,0:T(8,128)(2,1)} %bitcast.9), calls=%async_computation.3 | async-start | bytes 262144 | tf_op jit(solution)/shard_map/all_to_all | solution.py:184
  105.3 36.9 %reduce-scatter.2.cloned.1.call-start = ((), (), s32[]{:S(2)}) async-start(), calls=%async_computation.6 | async-start | bytes 884736 | tf_op jit(solution)/shard_map/reduce_scatter | solution.py:219
  118.3 26.4 %all-to-all-start.4 = ((bf16[32,8,1536]{2,1,0:T(8,128)(2,1)}), bf16[32,8,1536]{2,1,0:T(8,128)(2,1)S(1)}, u32[]{:S(2)}, u32[]{:S(2)}) async-start(bf16[32,8,1536]{2,1,0:T(8,128)(2,1)} %bitcast.11), calls=%async_computation.4 | async-start | bytes 1572864 | tf_op jit(solution)/shard_map/all_to_all | solution.py:184
  144.8 0.9 copy-start.5
Sparse Core Ops, SparseCore 0:
  108.7 33.5 reduce-scatter.1

commit v2 on v1

--- a/solution.py
+++ b/solution.py
@@ -24,6 +24,9 @@
 FEATS = GROUP * HEAD_DIM
 COLS = 512
 TENSOR = 8
+CORES = 2
+CHIPS = 4
+DOWN_STEPS = 4
 CHUNK = 16
 BF = jnp.bfloat16
 F32 = jnp.float32
@@ -43,7 +46,55 @@
     return high, low
 
 
-def attend_kernel(q, ck, cv, nk, nv, lens, ids, hub, att, picks, pay):
+def attend_kernel(
+    q_hbm, ck_hbm, cv_hbm, nk_hbm, nv_hbm, lens_hbm, ids_hbm, hub_hbm,
+    att, picks, pay,
+    q, ck, cv, nk, nv, lens, ids, hub, sems,
+):
+    copies = []
+    sources = (ids_hbm, hub_hbm, lens_hbm, q_hbm, ck_hbm, nk_hbm, nv_hbm, cv_hbm)
+    for n, (src, dst) in enumerate(zip(sources, (ids, hub, lens, q, ck, nk, nv, cv))):
+        copies.append(pltpu.make_async_copy(src, dst, sems.at[n]))
+        copies[-1].start()
+
+    diagonal = iota((ROWS, ROWS), 0) == iota((ROWS, ROWS), 1)
+
+    def column(line):
+        return jnp.sum(jnp.where(diagonal, line, 0.0), axis=1, keepdims=True)
+
+    copies[0].wait()
+    copies[1].wait()
+    owner_of_line = iota((ROWS, LINES), 1) >> 3
+    named = jnp.zeros((ROWS, LINES), jnp.bool_)
+    adapter_of_col = iota((ROWS, OWNERS * ADP_DEV), 1)
+    coef = jnp.zeros((ROWS, OWNERS * ADP_DEV), F32)
+    for j in range(TOPA):
+        idj = column(ids[j : j + 1, :].astype(F32)).astype(jnp.int32)
+        named = named | ((idj >> 4) == owner_of_line)
+        coef = coef + jnp.where(idj == adapter_of_col, column(hub[j : j + 1, :]), 0.0)
+    earlier = (iota((ROWS, ROWS), 1) < iota((ROWS, ROWS), 0)).astype(BF)
+    place = dot(earlier, named.astype(BF)).astype(jnp.int32)
+    place = jnp.where(named, place, -1)
+    spot = iota((ROWS, LINES), 1) & (PART - 1)
+    high, low = split_parts(coef)
+    shape = (LINES, OWNERS * ADP_DEV)
+    mine = (iota(shape, 0) >> 3) == (iota(shape, 1) >> 4)
+    fold_shape = (OWNERS * ADP_DEV, 128)
+    within = iota(fold_shape, 0) & (ADP_DEV - 1)
+    lane = iota(fold_shape, 1)
+    meta = jnp.zeros((LINES, 128), F32)
+    for g in range(PARTS):
+        pick = (place == spot + g * PART).astype(BF)
+        picks[pl.ds(g * ROWS, ROWS), :] = pick
+        for k, piece in enumerate((high, low)):
+            spread = jnp.where(mine, dot(pick, piece, ((0,), (0,))), 0.0).astype(BF)
+            fold = (lane == within + (g * 32 + k * ADP_DEV)).astype(BF)
+            meta = meta + dot(spread, fold)
+    pay[:, PARTS * FEATS :] = meta.astype(BF)
+
+    for copy in copies[2:]:
+        copy.wait()
+    lengths = column(lens[...].astype(F32)).astype(jnp.int32)
     scale = 1.0 / math.sqrt(HEAD_DIM)
     keys = CHUNK * 32
     wide = CHUNK * GROUP
@@ -56,7 +107,7 @@
         kc = ck[pl.ds(c * keys, keys), :]
         vc = cv[pl.ds(c * keys, keys), :]
         scores = dot(qs, kc, ((1,), (1,))) * scale
-        held = jnp.concatenate([lens[rows, :]] * GROUP, axis=0)
+        held = jnp.concatenate([lengths[c * CHUNK : (c + 1) * CHUNK, :]] * GROUP, axis=0)
         usable = (row_of == (col >> 5)) & ((col & 31) < held)
         scores = jnp.where(usable, scores, -jnp.inf)
         fresh_k = jnp.concatenate([nk[rows, :].astype(F32)] * GROUP, axis=0)
@@ -70,42 +121,16 @@
         out = (summed / totals).astype(BF)
         for h in range(GROUP):
             att[rows, h * HEAD_DIM : (h + 1) * HEAD_DIM] = out[h * CHUNK : (h + 1) * CHUNK, :]
-
-    owner_of_line = iota((ROWS, LINES), 1) >> 3
-    named = jnp.zeros((ROWS, LINES), jnp.bool_)
-    adapter_of_col = iota((ROWS, OWNERS * ADP_DEV), 1)
-    coef = jnp.zeros((ROWS, OWNERS * ADP_DEV), F32)
-    for j in range(TOPA):
-        idj = ids[:, j : j + 1]
-        named = named | ((idj >> 4) == owner_of_line)
-        coef = coef + jnp.where(idj == adapter_of_col, hub[:, j : j + 1], 0.0)
-    earlier = (iota((ROWS, ROWS), 1) < iota((ROWS, ROWS), 0)).astype(BF)
-    place = dot(earlier, named.astype(BF)).astype(jnp.int32)
-    place = jnp.where(named, place, -1)
-    spot = iota((ROWS, LINES), 1) & (PART - 1)
-    high, low = split_parts(coef)
-    shape = (LINES, OWNERS * ADP_DEV)
-    mine = (iota(shape, 0) >> 3) == (iota(shape, 1) >> 4)
-    fold_shape = (OWNERS * ADP_DEV, 128)
-    within = iota(fold_shape, 0) & (ADP_DEV - 1)
-    lane = iota(fold_shape, 1)
-    meta = jnp.zeros((LINES, 128), F32)
     everything = att[...]
     for g in range(PARTS):
-        pick = (place == spot + g * PART).astype(BF)
-        picks[pl.ds(g * ROWS, ROWS), :] = pick
+        pick = picks[pl.ds(g * ROWS, ROWS), :]
         pay[:, g * FEATS : (g + 1) * FEATS] = dot(pick, everything, ((0,), (0,))).astype(BF)
-        for k, piece in enumerate((high, low)):
-            spread = jnp.where(mine, dot(pick, piece, ((0,), (0,))), 0.0).astype(BF)
-            fold = (lane == within + (g * 32 + k * ADP_DEV)).astype(BF)
-            meta = meta + dot(spread, fold)
-    pay[:, PARTS * FEATS :] = meta.astype(BF)
-
-
-def coefs_of(meta, g):
-    shape = (128, ADP_DEV * RANK)
+
+
+def coefs_of(meta, g, first=0, count=ADP_DEV):
+    shape = (128, count * RANK)
     line = iota(shape, 0)
-    adapter = iota(shape, 1) >> 6
+    adapter = (iota(shape, 1) >> 6) + first
     spread = (line == adapter + g * 32) | (line == adapter + (g * 32 + ADP_DEV))
     return dot(meta, spread.astype(BF))
 
@@ -117,16 +142,24 @@
     return jnp.concatenate([first, second], axis=1)
 
 
-def lower_kernel(got, down, out):
+def lower_kernel(got, down, out, weights, sems):
+    width = down.shape[1] // DOWN_STEPS
+    held = ADP_DEV // DOWN_STEPS
+    copies = []
+    for n in range(DOWN_STEPS):
+        cols = pl.ds(n * width, width)
+        copies.append(pltpu.make_async_copy(down.at[:, cols], weights.at[:, cols], sems.at[n]))
+        copies[-1].start()
     meta = got[:, PARTS * FEATS :]
-    weights = down[...]
-    pieces = []
-    for g in range(PARTS):
-        lowered = dot(got[:, g * FEATS : (g + 1) * FEATS], weights) * coefs_of(meta, g)
-        total = lowered[:, :128]
-        for p in range(1, ADP_DEV * RANK // 128):
-            total = total + lowered[:, p * 128 : (p + 1) * 128]
-        pieces.append(total + pltpu.roll(total, RANK, 1))
+    totals = [jnp.zeros((LINES, 128), F32)] * PARTS
+    for n in range(DOWN_STEPS):
+        copies[n].wait()
+        for g in range(PARTS):
+            lowered = dot(got[:, g * FEATS : (g + 1) * FEATS], weights[:, n * width : (n + 1) * width])
+            lowered = lowered * coefs_of(meta, g, n * held, held)
+            for p in range(width // 128):
+                totals[g] = totals[g] + lowered[:, p * 128 : (p + 1) * 128]
+    pieces = [total + pltpu.roll(total, RANK, 1) for total in totals]
     out[...] = join_parts(pieces).astype(BF)
 
 
@@ -138,15 +171,23 @@
         total = total + jnp.where((lane >> 6) == g, part, 0.0)
     folded = total[:, :128] + total[:, 128:]
     folded = folded + pltpu.roll(folded, RANK, 1)
+    half = ROWS // 2
+    lane = iota((half, 128), 1)
+    packed = jnp.where(lane < RANK, folded[:half, :], folded[half:, :])
     for t in range(TENSOR):
-        out[pl.ds(t * ROWS, ROWS), :] = folded
+        out[pl.ds(t * half, half), :] = packed
 
 
 def mix_kernel(got, picks, out):
-    total = got[pl.ds(0, ROWS), :]
+    half = ROWS // 2
+    total = got[pl.ds(0, half), :]
     for t in range(1, TENSOR):
-        total = total + got[pl.ds(t * ROWS, ROWS), :]
-    mixed = total.astype(BF)
+        total = total + got[pl.ds(t * half, half), :]
+    other = pltpu.roll(total, RANK, 1)
+    lane = iota((half, 128), 1)
+    first = jnp.where(lane < RANK, total, other)
+    second = jnp.where(lane < RANK, other, total)
+    mixed = jnp.concatenate([first, second], axis=0).astype(BF)
     pieces = [dot(picks[pl.ds(g * ROWS, ROWS), :], mixed, ((0,), (0,))) for g in range(PARTS)]
     out[...] = join_parts(pieces).astype(BF)
 
@@ -168,11 +209,39 @@
     out[...] = total.astype(BF)
 
 
+def attend(*args):
+    return pl.pallas_call(
+        attend_kernel,
+        out_shape=(
+            shape_of(ROWS, FEATS),
+            shape_of(PARTS * ROWS, LINES),
+            shape_of(LINES, PARTS * FEATS + 128),
+        ),
+        in_specs=[pl.BlockSpec(memory_space=pltpu.HBM)] * len(args),
+        scratch_shapes=[pltpu.VMEM(x.shape, x.dtype) for x in args]
+        + [pltpu.SemaphoreType.DMA((len(args),))],
+        compiler_params=pltpu.CompilerParams(vmem_limit_bytes=32 * 1024 * 1024),
+    )(*[pltpu.with_memory_space_constraint(x, pltpu.HBM) for x in args])
+
+
+def lower(got, down):
+    return pl.pallas_call(
+        lower_kernel,
+        out_shape=shape_of(LINES, 256),
+        in_specs=[pl.BlockSpec(memory_space=pltpu.VMEM), pl.BlockSpec(memory_space=pltpu.HBM)],
+        scratch_shapes=[
+            pltpu.VMEM(down.shape, down.dtype),
+            pltpu.SemaphoreType.DMA((DOWN_STEPS,)),
+        ],
+        compiler_params=pltpu.CompilerParams(vmem_limit_bytes=24 * 1024 * 1024),
+    )(got, pltpu.with_memory_space_constraint(down, pltpu.HBM))
+
+
 def call(kernel, out_shape, *args):
     return pl.pallas_call(
         kernel,
         out_shape=out_shape,
-        compiler_params=pltpu.CompilerParams(vmem_limit_bytes=48 * 1024 * 1024),
+        compiler_params=pltpu.CompilerParams(vmem_limit_bytes=24 * 1024 * 1024),
     )(*args)
 
 
@@ -182,6 +251,24 @@
 
 def swap(x, axis):
     return lax.all_to_all(x, axis, split_axis=0, concat_axis=0, tiled=True)
+
+
+def frozen_sum(attended, out_weight):
+    index = lax.axis_index("tensor")
+    chip, core = index // CORES, index % CORES
+    part = jnp.dot(attended, out_weight, preferred_element_type=F32)
+    part = part.reshape(ROWS, CHIPS, CORES, COLS)
+    kept = jnp.where(core == 0, part[:, :, 0], part[:, :, 1])
+    sent = jnp.where(core == 0, part[:, :, 1], part[:, :, 0]).astype(BF)
+    came = lax.ppermute(sent, "tensor", [(i, i ^ 1) for i in range(TENSOR)])
+    pair = (kept + came.astype(F32)).reshape(ROWS, CHIPS * COLS)
+    rounded = pair.astype(BF)
+    total = lax.dynamic_slice_in_dim(pair, chip * COLS, COLS, 1)
+    for step in range(1, CHIPS):
+        block = lax.dynamic_slice_in_dim(rounded, ((chip + step) % CHIPS) * COLS, COLS, 1)
+        pairs = [(i, (i + step * CORES) % TENSOR) for i in range(TENSOR)]
+        total = total + lax.ppermute(block, "tensor", pairs).astype(F32)
+    return total
 
 
 def local(
@@ -197,29 +284,22 @@
     adapter_ids,
     hub_weights,
 ):
-    attended, picks, payload = call(
-        attend_kernel,
-        (
-            shape_of(ROWS, FEATS),
-            shape_of(PARTS * ROWS, LINES),
-            shape_of(LINES, PARTS * FEATS + 128),
-        ),
+    attended, picks, payload = attend(
         queries,
         cache_keys.reshape(-1, HEAD_DIM),
         cache_values.reshape(-1, HEAD_DIM),
         new_keys,
         new_values,
-        cache_lengths.reshape(ROWS, 1),
-        adapter_ids,
-        hub_weights,
+        cache_lengths.reshape(1, ROWS),
+        adapter_ids.T,
+        hub_weights.T,
     )
     got = swap(payload, "adapter")
-    frozen_part = jnp.dot(attended, out_weight, preferred_element_type=F32)
-    got, frozen_part = lax.optimization_barrier((got, frozen_part))
-    frozen = lax.psum_scatter(frozen_part, "tensor", scatter_dimension=1, tiled=True)
-    lowered = call(lower_kernel, shape_of(LINES, 256), got, adapter_down)
+    frozen = frozen_sum(attended, out_weight)
+    got, frozen = lax.optimization_barrier((got, frozen))
+    lowered = lower(got, adapter_down)
     lowered = swap(lowered, "adapter")
-    share = call(home_kernel, shape_of(TENSOR * ROWS, 128, dtype=F32), lowered, picks)
+    share = call(home_kernel, shape_of(TENSOR * ROWS // 2, 128, dtype=F32), lowered, picks)
     share = swap(share, "tensor")
     mixed = call(mix_kernel, shape_of(LINES, 256), share, picks)
     mixed = swap(mixed, "adapter")

time: 154 us -> 132 us (0.86)
  waiting for transfers between devices: 66.3 us -> 33.6 us
  blocking collectives: 26.5 us -> 52.1 us
  between operations: 13.5 us -> 0.12 us
  local copies, waits for them, and re-layouts: 9.06 us -> 3.88 us
  other arithmetic: 0 us -> 2.04 us
  Pallas kernels: 12 us -> 13.8 us
    all_to_all x2 -> x3, blocking collectives: 26.5 us -> 52.1 us  [swap(): return lax.all_to_all(x, axis, split_axis=0, concat_axis=0, tiled=True)]
    reduce_scatter x1 -> x0, waiting for transfers between devices: 19.6 us -> none  [local(): lax.psum_scatter(frozen_part, 'tensor', scatter_dimension=1, tiled=True)]
    all_to_all x3 -> x2, waiting for transfers between devices: 46 us -> 29.1 us  [swap(): return lax.all_to_all(x, axis, split_axis=0, concat_axis=0, tiled=True)]
    pallas_call x0 -> x2, Pallas kernels: none -> 9.5 us  [the longest x1 5.15 us: attend(): pl.pallas_call(attend_kernel, out_shape=(shape_of(ROWS, FEATS), shape_of(...]
    unnamed x18 -> x3, local copies, waits for them, and re-layouts: 8.32 us -> 0.13 us
    pallas_call x6 -> x4, Pallas kernels: 12 us -> 4.26 us  [call(): pl.pallas_call(kernel, out_shape=out_shape, compiler_params=pltpu.Compile...]
    ppermute x0 -> x4, starting transfers between devices: none -> 5.74 us  [the longest x3 5.74 us: frozen_sum(): total = total + lax.ppermute(block, 'tensor', pairs).astype(F32)]
    ppermute x0 -> x4, waiting for transfers between devices: none -> 4.43 us  [the longest x3 2.65 us: frozen_sum(): total = total + lax.ppermute(block, 'tensor', pairs).astype(F32)]
  transfers between devices with their start and end apart: 4 -> 6, of which waited for: 4 -> 5; matrix products, arithmetic and copies ran while one was open for 4% -> 8% of each run, Pallas kernels for 2% -> 0%
where the time goes in v2:
time: 132 us
  blocking collectives  52.1 us (39%)
  waiting for transfers between devices  33.6 us (25%)
  starting transfers between devices  21.5 us (16%)
  Pallas kernels  13.8 us (10%)
  matrix products  4.95 us (4%)
  local copies, waits for them, and re-layouts  3.88 us (3%)
  other arithmetic  2.04 us (2%)
    all_to_all x3, blocking collectives, swap(): return lax.all_to_all(x, axis, split_axis=0, concat_axis=0, tiled=True)  52.1 us
    all_to_all x2, waiting for transfers between devices, swap(): return lax.all_to_all(x, axis, split_axis=0, concat_axis=0, tiled=True)  29.1 us
    all_to_all x2, starting transfers between devices, swap(): return lax.all_to_all(x, axis, split_axis=0, concat_axis=0, tiled=True)  15.8 us
    ppermute x3, starting transfers between devices, frozen_sum(): total = total + lax.ppermute(block, 'tensor', pairs).astype(F32)  5.74 us
    pallas_call x1, Pallas kernels, attend(): pl.pallas_call(attend_kernel, out_shape=(shape_of(ROWS, FEATS), shape_of(...  5.15 us
    dot_general x1, matrix products, frozen_sum(): part = jnp.dot(attended, out_weight, preferred_element_type=F32)  4.95 us
    pallas_call x1, Pallas kernels, lower(): pl.pallas_call(lower_kernel, out_shape=shape_of(LINES, 256), in_specs=[pl...  4.35 us
    pallas_call x4, Pallas kernels, call(): pl.pallas_call(kernel, out_shape=out_shape, compiler_params=pltpu.Compile...  4.26 us
  transfers between devices with their start and end apart: 6, of which 5 were waited for; matrix products, arithmetic and copies ran while one was open for 8% of the time, Pallas kernels for 0%

profile of v2, /device:TPU:32, one launch (start us, length us, event | category | flops | bytes accessed | tf_op | source)
XLA Modules:
  0.0 131.9 jit_solution(7020925799291914078)
XLA Ops:
  0.0 5.1 %shard_map.109 = (bf16[48,1024]{1,0:T(8,128)(2,1)S(1)}, bf16[144,256]{1,0:T(8,128)(2,1)S(1)}, bf16[256,3200]{1,0:T(8,128)(2,1)}) custom-call(bf16[48,1024]{1,0:T(8,128)(2,1)} %q_hbm.1, bf16[1536,128]{1,0:T(8,128)(2,1)} %bitcast.35, bf16[1536,128]{1,0:T(8,128)(2,1)} %bitcast.36, bf16[48,128]{1,0:T(8,128)(2,1)} %nk_hbm.1, bf16[48,128]{1,0:T(8,128)(2,1)} %nv_hbm.1, ...), custom_call_target="tpu_custom_call" | custom-call | tf_op jit(solution)/shard_map/pallas_call | solution.py:213
  5.2 11.4 %all-to-all-start = ((bf16[32,8,3200]{2,1,0:T(8,128)(2,1)}), bf16[32,8,3200]{2,1,0:T(8,128)(2,1)S(1)}, u32[]{:S(2)}, u32[]{:S(2)}) async-start(bf16[32,8,3200]{2,1,0:T(8,128)(2,1)} %bitcast.5), calls=%async_computation | async-start | bytes 3276800 | tf_op jit(solution)/shard_map/all_to_all | solution.py:253
  16.5 5.0 %fusion.2 = f32[48,4096]{1,0:T(8,128)S(1)} fusion(bf16[48,1024]{1,0:T(8,128)(2,1)S(1)} %get-tuple-element.11, bf16[1024,4096]{1,0:T(8,128)(2,1)} %param.17), kind=kOutput, calls=%fused_computation.8 | convolution fusion | flops 402653184 | bytes 9273344 | tf_op jit(solution)/shard_map/dot_general | solution.py:259
  21.5 0.0 copy-start
  21.5 1.5 %reshape.33 = f32[48,4,2,512]{3,2,1,0:T(2,128)} reshape(f32[48,4096]{1,0:T(8,128)S(1)} %fusion.2) | data formatting | bytes 1572864 | tf_op jit(solution)/shard_map/reshape | solution.py:260
  23.1 2.2 %fusion.1 = (f32[48,4,1,512]{3,2,1,0:T(1,128)S(1)}, f32[48,4,1,512]{3,2,1,0:T(1,128)S(1)}) fusion(f32[48,4,2,512]{3,2,1,0:T(2,128)} %reshape.33), kind=kLoop, calls=%fused_computation.7 | loop fusion | bytes 1572864 | tf_op jit(solution)/shard_map/slice | solution.py:261
  25.2 0.8 fusion
  26.1 0.0 collective-permute-start
  26.1 1.8 %collective-permute-done = bf16[48,4,512]{2,1,0:T(4,128)(2,1)} collective-permute-done((bf16[48,4,512]{2,1,0:T(4,128)(2,1)}, bf16[48,4,512]{2,1,0:T(4,128)(2,1)}, u32[]{:S(2)}, u32[]{:S(2)}) %collective-permute-start) | collective-permute-done | bytes 196640 | tf_op jit(solution)/shard_map/ppermute | solution.py:263
  27.9 1.2 bitcast_add_fusion
  29.0 0.1 copy.16
  29.2 1.6 %collective-permute-start.1 = (bf16[48,512]{1,0:T(8,128)(2,1)S(1)}, bf16[48,512]{1,0:T(8,128)(2,1)S(1)}, u32[]{:S(2)}, u32[]{:S(2)}) collective-permute-start(bf16[48,512]{1,0:T(8,128)(2,1)S(1)} %get-tuple-element.17), channel_id=1, source_target_pairs={{0,2},{1,3},{2,4},{3,5},{4,6},{5,7},{6,0},{7,1},{8,10},{9,11},{10,... | collective-permute-start | bytes 147464 | tf_op jit(solution)/shard_map/ppermute | solution.py:270
  30.8 2.7 %collective-permute-start.2 = (bf16[48,512]{1,0:T(8,128)(2,1)S(1)}, bf16[48,512]{1,0:T(8,128)(2,1)S(1)}, u32[]{:S(2)}, u32[]{:S(2)}) collective-permute-start(bf16[48,512]{1,0:T(8,128)(2,1)S(1)} %get-tuple-element.19), channel_id=1, source_target_pairs={{0,4},{1,5},{2,6},{3,7},{4,0},{5,1},{6,2},{7,3},{8,12},{9,13},{10,... | collective-permute-start | bytes 147464 | tf_op jit(solution)/shard_map/ppermute | solution.py:270
  33.5 1.4 %collective-permute-start.3 = (bf16[48,512]{1,0:T(8,128)(2,1)S(1)}, bf16[48,512]{1,0:T(8,128)(2,1)S(1)}, u32[]{:S(2)}, u32[]{:S(2)}) collective-permute-start(bf16[48,512]{1,0:T(8,128)(2,1)S(1)} %get-tuple-element.18), channel_id=1, source_target_pairs={{0,6},{1,7},{2,0},{3,1},{4,2},{5,3},{6,4},{7,5},{8,14},{9,15},{10,... | collective-permute-start | bytes 147464 | tf_op jit(solution)/shard_map/ppermute | solution.py:270
  34.9 0.0 collective-permute-done.1
  35.0 1.4 %collective-permute-done.2 = bf16[48,512]{1,0:T(8,128)(2,1)S(1)} collective-permute-done((bf16[48,512]{1,0:T(8,128)(2,1)S(1)}, bf16[48,512]{1,0:T(8,128)(2,1)S(1)}, u32[]{:S(2)}, u32[]{:S(2)}) %collective-permute-start.2) | collective-permute-done | bytes 49184 | tf_op jit(solution)/shard_map/ppermute | solution.py:270
  36.4 1.2 collective-permute-done.3
  37.6 19.2 %all-to-all-done = bf16[32,8,3200]{2,1,0:T(8,128)(2,1)S(1)} async-done(((bf16[32,8,3200]{2,1,0:T(8,128)(2,1)}), bf16[32,8,3200]{2,1,0:T(8,128)(2,1)S(1)}, u32[]{:S(2)}, u32[]{:S(2)}) %all-to-all-start) | async-done | bytes 1638432 | tf_op jit(solution)/shard_map/all_to_all | solution.py:253
  56.8 4.3 %shard_map.110 = bf16[256,256]{1,0:T(8,128)(2,1)S(1)} custom-call(bf16[256,3200]{1,0:T(8,128)(2,1)S(1)} %bitcast.23, bf16[1024,1024]{1,0:T(8,128)(2,1)} %down.1), custom_call_target="tpu_custom_call" | custom-call | tf_op jit(solution)/shard_map/pallas_call | solution.py:228
  61.1 15.6 %all_to_all.56 = bf16[32,8,256]{2,1,0:T(8,128)(2,1)S(1)} all-to-all(bf16[32,8,256]{2,1,0:T(8,128)(2,1)S(1)} %bitcast.29), channel_id=1, replica_groups=mesh['adapter'=32,'tensor'=8] {'adapter'}, dimensions={0} | all-to-all | bytes 262144 | tf_op jit(solution)/shard_map/all_to_all | solution.py:253
  76.8 0.3 shard_map.111
  77.0 9.9 %all_to_all.57 = f32[8,24,128]{2,1,0:T(8,128)S(1)} all-to-all(f32[8,24,128]{2,1,0:T(8,128)S(1)} %bitcast.30), channel_id=1, replica_groups=mesh['adapter'=32,'tensor'=8] {'tensor'}, dimensions={0} | all-to-all | bytes 196608 | tf_op jit(solution)/shard_map/all_to_all | solution.py:253
  86.9 0.9 shard_map.112
  87.8 4.4 %all-to-all-start.3 = ((bf16[32,8,256]{2,1,0:T(8,128)(2,1)}), bf16[32,8,256]{2,1,0:T(8,128)(2,1)S(1)}, u32[]{:S(2)}, u32[]{:S(2)}) async-start(bf16[32,8,256]{2,1,0:T(8,128)(2,1)} %bitcast.13), calls=%async_computation.3 | async-start | bytes 262144 | tf_op jit(solution)/shard_map/all_to_all | solution.py:253
  92.3 10.0 %all-to-all-done.3 = bf16[32,8,256]{2,1,0:T(8,128)(2,1)S(1)} async-done(((bf16[32,8,256]{2,1,0:T(8,128)(2,1)}), bf16[32,8,256]{2,1,0:T(8,128)(2,1)S(1)}, u32[]{:S(2)}, u32[]{:S(2)}) %all-to-all-start.3) | async-done | bytes 131104 | tf_op jit(solution)/shard_map/all_to_all | solution.py:253
  102.2 0.0 copy-done
  102.2 2.2 %shard_map.113 = bf16[256,1536]{1,0:T(8,128)(2,1)S(1)} custom-call(bf16[256,256]{1,0:T(8,128)(2,1)S(1)} %bitcast.27, bf16[256,128]{1,0:T(8,128)(2,1)S(1)} %slice.13.meta, bf16[1024,512]{1,0:T(8,128)(2,1)S(1)} %copy-done), custom_call_target="tpu_custom_call" | custom-call | tf_op jit(solution)/shard_map/pallas_call | solution.py:241
  104.5 26.5 %all_to_all.58 = bf16[32,8,1536]{2,1,0:T(8,128)(2,1)S(1)} all-to-all(bf16[32,8,1536]{2,1,0:T(8,128)(2,1)S(1)} %bitcast.26), channel_id=1, replica_groups=mesh['adapter'=32,'tensor'=8] {'adapter'}, dimensions={0} | all-to-all | bytes 1572864 | tf_op jit(solution)/shard_map/all_to_all | solution.py:253
  131.0 0.9 shard_map.114
  (4 shorter events, 0.1 us)
Async XLA Ops:
  5.2 51.6 %all-to-all-start = ((bf16[32,8,3200]{2,1,0:T(8,128)(2,1)}), bf16[32,8,3200]{2,1,0:T(8,128)(2,1)S(1)}, u32[]{:S(2)}, u32[]{:S(2)}) async-start(bf16[32,8,3200]{2,1,0:T(8,128)(2,1)} %bitcast.5), calls=%async_computation | async-start | bytes 3276800 | tf_op jit(solution)/shard_map/all_to_all | solution.py:253
  21.5 80.7 %copy-start = (bf16[1024,512]{1,0:T(8,128)(2,1)S(1)}, bf16[1024,512]{1,0:T(8,128)(2,1)}, u32[]{:S(2)}) copy-start(bf16[1024,512]{1,0:T(8,128)(2,1)} %up.1) | copy-start | bytes 3145732
  26.1 1.8 %collective-permute-start = (bf16[48,4,512]{2,1,0:T(4,128)(2,1)}, bf16[48,4,512]{2,1,0:T(4,128)(2,1)}, u32[]{:S(2)}, u32[]{:S(2)}) collective-permute-start(bf16[48,4,512]{2,1,0:T(4,128)(2,1)} %fusion), channel_id=1, source_target_pairs={{0,1},{1,0},{2,3},{3,2},{4,5},{5,4},{6,7},{7,6},{8,9},{9,8},{10,11... | collective-permute-start | bytes 589832 | tf_op jit(solution)/shard_map/ppermute | solution.py:263
  29.2 5.7 %collective-permute-start.1 = (bf16[48,512]{1,0:T(8,128)(2,1)S(1)}, bf16[48,512]{1,0:T(8,128)(2,1)S(1)}, u32[]{:S(2)}, u32[]{:S(2)}) collective-permute-start(bf16[48,512]{1,0:T(8,128)(2,1)S(1)} %get-tuple-element.17), channel_id=1, source_target_pairs={{0,2},{1,3},{2,4},{3,5},{4,6},{5,7},{6,0},{7,1},{8,10},{9,11},{10,... | collective-permute-start | bytes 147464 | tf_op jit(solution)/shard_map/ppermute | solution.py:270
  30.8 5.6 %collective-permute-start.2 = (bf16[48,512]{1,0:T(8,128)(2,1)S(1)}, bf16[48,512]{1,0:T(8,128)(2,1)S(1)}, u32[]{:S(2)}, u32[]{:S(2)}) collective-permute-start(bf16[48,512]{1,0:T(8,128)(2,1)S(1)} %get-tuple-element.19), channel_id=1, source_target_pairs={{0,4},{1,5},{2,6},{3,7},{4,0},{5,1},{6,2},{7,3},{8,12},{9,13},{10,... | collective-permute-start | bytes 147464 | tf_op jit(solution)/shard_map/ppermute | solution.py:270
  33.5 4.1 %collective-permute-start.3 = (bf16[48,512]{1,0:T(8,128)(2,1)S(1)}, bf16[48,512]{1,0:T(8,128)(2,1)S(1)}, u32[]{:S(2)}, u32[]{:S(2)}) collective-permute-start(bf16[48,512]{1,0:T(8,128)(2,1)S(1)} %get-tuple-element.18), channel_id=1, source_target_pairs={{0,6},{1,7},{2,0},{3,1},{4,2},{5,3},{6,4},{7,5},{8,14},{9,15},{10,... | collective-permute-start | bytes 147464 | tf_op jit(solution)/shard_map/ppermute | solution.py:270
  87.8 14.4 %all-to-all-start.3 = ((bf16[32,8,256]{2,1,0:T(8,128)(2,1)}), bf16[32,8,256]{2,1,0:T(8,128)(2,1)S(1)}, u32[]{:S(2)}, u32[]{:S(2)}) async-start(bf16[32,8,256]{2,1,0:T(8,128)(2,1)} %bitcast.13), calls=%async_computation.3 | async-start | bytes 262144 | tf_op jit(solution)/shard_map/all_to_all | solution.py:253

commit v3 on v2

--- a/solution.py
+++ b/solution.py
@@ -40,6 +40,11 @@
     return lax.dot_general(a, b, (contract, ((), ())), preferred_element_type=F32)
 
 
+def column(line):
+    diagonal = iota((ROWS, ROWS), 0) == iota((ROWS, ROWS), 1)
+    return jnp.sum(jnp.where(diagonal, line, 0.0), axis=1, keepdims=True)
+
+
 def split_parts(x):
     high = x.astype(BF)
     low = (x - high.astype(F32)).astype(BF)
@@ -49,48 +54,48 @@
 def attend_kernel(
     q_hbm, ck_hbm, cv_hbm, nk_hbm, nv_hbm, lens_hbm, ids_hbm, hub_hbm,
     att, picks, pay,
-    q, ck, cv, nk, nv, lens, ids, hub, sems,
+    q, ck, cv, nk, nv, lens, ids, hub, sems, made, out_sems,
 ):
+    def leave(g, start, width):
+        cols = pl.ds(start, width)
+        copy = pltpu.make_async_copy(made.at[:, cols], pay.at[:, cols], out_sems.at[g])
+        copy.start()
+        return copy
+
     copies = []
     sources = (ids_hbm, hub_hbm, lens_hbm, q_hbm, ck_hbm, nk_hbm, nv_hbm, cv_hbm)
     for n, (src, dst) in enumerate(zip(sources, (ids, hub, lens, q, ck, nk, nv, cv))):
         copies.append(pltpu.make_async_copy(src, dst, sems.at[n]))
         copies[-1].start()
 
-    diagonal = iota((ROWS, ROWS), 0) == iota((ROWS, ROWS), 1)
-
-    def column(line):
-        return jnp.sum(jnp.where(diagonal, line, 0.0), axis=1, keepdims=True)
-
     copies[0].wait()
     copies[1].wait()
-    owner_of_line = iota((ROWS, LINES), 1) >> 3
-    named = jnp.zeros((ROWS, LINES), jnp.bool_)
-    adapter_of_col = iota((ROWS, OWNERS * ADP_DEV), 1)
-    coef = jnp.zeros((ROWS, OWNERS * ADP_DEV), F32)
+    shape = (LINES, ROWS)
+    owner_of_line = iota(shape, 0) >> 3
+    hits = [(ids[j : j + 1, :] >> 4) == owner_of_line for j in range(TOPA)]
+    named = (hits[0] | hits[1]) | (hits[2] | hits[3])
+    earlier = (iota((ROWS, ROWS), 0) < iota((ROWS, ROWS), 1)).astype(BF)
+    place = dot(named.astype(BF), earlier).astype(jnp.int32)
+    place = jnp.where(named, place, -1)
+    spot = iota(shape, 0) & (PART - 1)
+    line = iota((128, ROWS), 0)
+    spreads = []
     for j in range(TOPA):
-        idj = column(ids[j : j + 1, :].astype(F32)).astype(jnp.int32)
-        named = named | ((idj >> 4) == owner_of_line)
-        coef = coef + jnp.where(idj == adapter_of_col, column(hub[j : j + 1, :]), 0.0)
-    earlier = (iota((ROWS, ROWS), 1) < iota((ROWS, ROWS), 0)).astype(BF)
-    place = dot(earlier, named.astype(BF)).astype(jnp.int32)
-    place = jnp.where(named, place, -1)
-    spot = iota((ROWS, LINES), 1) & (PART - 1)
-    high, low = split_parts(coef)
-    shape = (LINES, OWNERS * ADP_DEV)
-    mine = (iota(shape, 0) >> 3) == (iota(shape, 1) >> 4)
-    fold_shape = (OWNERS * ADP_DEV, 128)
-    within = iota(fold_shape, 0) & (ADP_DEV - 1)
-    lane = iota(fold_shape, 1)
+        within = ids[j : j + 1, :] & (ADP_DEV - 1)
+        high, low = split_parts(hub[j : j + 1, :])
+        spread = jnp.where(line == within, high.astype(F32), 0.0)
+        spread = jnp.where(line == within + ADP_DEV, low.astype(F32), spread)
+        spreads.append(spread.astype(BF))
     meta = jnp.zeros((LINES, 128), F32)
     for g in range(PARTS):
-        pick = (place == spot + g * PART).astype(BF)
-        picks[pl.ds(g * ROWS, ROWS), :] = pick
-        for k, piece in enumerate((high, low)):
-            spread = jnp.where(mine, dot(pick, piece, ((0,), (0,))), 0.0).astype(BF)
-            fold = (lane == within + (g * 32 + k * ADP_DEV)).astype(BF)
-            meta = meta + dot(spread, fold)
-    pay[:, PARTS * FEATS :] = meta.astype(BF)
+        pick = place == spot + g * PART
+        picks[pl.ds(g * LINES, LINES), :] = pick.astype(BF)
+        coefs = jnp.zeros((LINES, 128), F32)
+        for j in range(TOPA):
+            coefs = coefs + dot((pick & hits[j]).astype(BF), spreads[j], ((1,), (1,)))
+        meta = meta + (pltpu.roll(coefs, g * 2 * ADP_DEV, 1) if g else coefs)
+    made[:, PARTS * FEATS :] = meta.astype(BF)
+    leaving = [leave(PARTS, PARTS * FEATS, 128)]
 
     for copy in copies[2:]:
         copy.wait()
@@ -123,8 +128,11 @@
             att[rows, h * HEAD_DIM : (h + 1) * HEAD_DIM] = out[h * CHUNK : (h + 1) * CHUNK, :]
     everything = att[...]
     for g in range(PARTS):
-        pick = picks[pl.ds(g * ROWS, ROWS), :]
-        pay[:, g * FEATS : (g + 1) * FEATS] = dot(pick, everything, ((0,), (0,))).astype(BF)
+        pick = picks[pl.ds(g * LINES, LINES), :]
+        made[:, g * FEATS : (g + 1) * FEATS] = dot(pick, everything).astype(BF)
+        leaving.append(leave(g, g * FEATS, FEATS))
+    for copy in leaving:
+        copy.wait()
 
 
 def coefs_of(meta, g, first=0, count=ADP_DEV):
@@ -144,23 +152,38 @@
 
 def lower_kernel(got, down, out, weights, sems):
     width = down.shape[1] // DOWN_STEPS
-    held = ADP_DEV // DOWN_STEPS
     copies = []
     for n in range(DOWN_STEPS):
         cols = pl.ds(n * width, width)
         copies.append(pltpu.make_async_copy(down.at[:, cols], weights.at[:, cols], sems.at[n]))
         copies[-1].start()
     meta = got[:, PARTS * FEATS :]
+    coefs = [coefs_of(meta, g) for g in range(PARTS)]
     totals = [jnp.zeros((LINES, 128), F32)] * PARTS
     for n in range(DOWN_STEPS):
         copies[n].wait()
+        block = weights[:, n * width : (n + 1) * width]
         for g in range(PARTS):
-            lowered = dot(got[:, g * FEATS : (g + 1) * FEATS], weights[:, n * width : (n + 1) * width])
-            lowered = lowered * coefs_of(meta, g, n * held, held)
+            lowered = dot(got[:, g * FEATS : (g + 1) * FEATS], block)
+            lowered = lowered * coefs[g][:, n * width : (n + 1) * width]
             for p in range(width // 128):
                 totals[g] = totals[g] + lowered[:, p * 128 : (p + 1) * 128]
     pieces = [total + pltpu.roll(total, RANK, 1) for total in totals]
     out[...] = join_parts(pieces).astype(BF)
+
+
+def pick_kernel(ids, after, picks):
+    owner_of_line = iota((ROWS, LINES), 1) >> 3
+    named = jnp.zeros((ROWS, LINES), jnp.bool_)
+    for j in range(TOPA):
+        owner = column(ids[j : j + 1, :].astype(F32)).astype(jnp.int32) >> 4
+        named = named | (owner == owner_of_line)
+    earlier = (iota((ROWS, ROWS), 1) < iota((ROWS, ROWS), 0)).astype(BF)
+    place = dot(earlier, named.astype(BF)).astype(jnp.int32)
+    place = jnp.where(named, place, -1)
+    spot = iota((ROWS, LINES), 1) & (PART - 1)
+    for g in range(PARTS):
+        picks[pl.ds(g * ROWS, ROWS), :] = (place == spot + g * PART).astype(BF)
 
 
 def home_kernel(got, picks, out):
@@ -173,33 +196,46 @@
     folded = folded + pltpu.roll(folded, RANK, 1)
     half = ROWS // 2
     lane = iota((half, 128), 1)
-    packed = jnp.where(lane < RANK, folded[:half, :], folded[half:, :])
-    for t in range(TENSOR):
-        out[pl.ds(t * half, half), :] = packed
-
-
-def mix_kernel(got, picks, out):
+    out[...] = jnp.where(lane < RANK, folded[:half, :], folded[half:, :])
+
+
+def mix_kernel(own, ahead, behind, across, picks, out):
     half = ROWS // 2
-    total = got[pl.ds(0, half), :]
-    for t in range(1, TENSOR):
-        total = total + got[pl.ds(t * half, half), :]
+    total = (own[...] + ahead[...]) + (behind[...] + across[...])
     other = pltpu.roll(total, RANK, 1)
     lane = iota((half, 128), 1)
     first = jnp.where(lane < RANK, total, other)
     second = jnp.where(lane < RANK, other, total)
     mixed = jnp.concatenate([first, second], axis=0).astype(BF)
-    pieces = [dot(picks[pl.ds(g * ROWS, ROWS), :], mixed, ((0,), (0,))) for g in range(PARTS)]
+    pieces = [dot(picks[pl.ds(g * LINES, LINES), :], mixed) for g in range(PARTS)]
     out[...] = join_parts(pieces).astype(BF)
 
 
 def raise_kernel(got, meta, up, out):
-    shape = (256, ADP_DEV * RANK)
-    line = iota(shape, 0)
-    rank = iota(shape, 1) & (RANK - 1)
-    for g in range(PARTS):
-        tiled = dot(got[...], (line == rank + g * RANK).astype(BF))
-        expanded = (tiled * coefs_of(meta[...], g)).astype(BF)
-        out[:, g * COLS : (g + 1) * COLS] = dot(expanded, up[...]).astype(BF)
+    lane = iota((LINES, 128), 1)
+    first = got[:, :128].astype(F32)
+    second = got[:, 128:].astype(F32)
+    turned = pltpu.roll(first, RANK, 1)
+    pairs = (
+        jnp.where(lane < RANK, first, turned),
+        jnp.where(lane < RANK, turned, first),
+        jnp.where(lane < RANK, second, pltpu.roll(second, RANK, 1)),
+    )
+    blocks = []
+    for g in range(PARTS):
+        coefs = coefs_of(meta[...], g)
+        blocks.append(
+            jnp.concatenate(
+                [
+                    (coefs[:, p * 128 : (p + 1) * 128] * pairs[g]).astype(BF)
+                    for p in range(ADP_DEV * RANK // 128)
+                ],
+                axis=1,
+            )
+        )
+    raised = dot(jnp.concatenate(blocks, axis=0), up[...]).astype(BF)
+    for g in range(PARTS):
+        out[:, g * COLS : (g + 1) * COLS] = raised[g * LINES : (g + 1) * LINES, :]
 
 
 def final_kernel(got, picks, frozen, out):
@@ -214,12 +250,21 @@
         attend_kernel,
         out_shape=(
             shape_of(ROWS, FEATS),
-            shape_of(PARTS * ROWS, LINES),
+            shape_of(PARTS * LINES, ROWS),
             shape_of(LINES, PARTS * FEATS + 128),
         ),
         in_specs=[pl.BlockSpec(memory_space=pltpu.HBM)] * len(args),
+        out_specs=(
+            pl.BlockSpec(memory_space=pltpu.VMEM),
+            pl.BlockSpec(memory_space=pltpu.VMEM),
+            pl.BlockSpec(memory_space=pltpu.HBM),
+        ),
         scratch_shapes=[pltpu.VMEM(x.shape, x.dtype) for x in args]
-        + [pltpu.SemaphoreType.DMA((len(args),))],
+        + [
+            pltpu.SemaphoreType.DMA((len(args),)),
+            pltpu.VMEM((LINES, PARTS * FEATS + 128), BF),
+            pltpu.SemaphoreType.DMA((PARTS + 1,)),
+        ],
         compiler_params=pltpu.CompilerParams(vmem_limit_bytes=32 * 1024 * 1024),
     )(*[pltpu.with_memory_space_constraint(x, pltpu.HBM) for x in args])
 
@@ -253,6 +298,13 @@
     return lax.all_to_all(x, axis, split_axis=0, concat_axis=0, tiled=True)
 
 
+def turn(x, chips, cores):
+    pairs = [
+        (i, (i // CORES + chips) % CHIPS * CORES + (i + cores) % CORES) for i in range(TENSOR)
+    ]
+    return lax.ppermute(x, "tensor", pairs)
+
+
 def frozen_sum(attended, out_weight):
     index = lax.axis_index("tensor")
     chip, core = index // CORES, index % CORES
@@ -260,14 +312,13 @@
     part = part.reshape(ROWS, CHIPS, CORES, COLS)
     kept = jnp.where(core == 0, part[:, :, 0], part[:, :, 1])
     sent = jnp.where(core == 0, part[:, :, 1], part[:, :, 0]).astype(BF)
-    came = lax.ppermute(sent, "tensor", [(i, i ^ 1) for i in range(TENSOR)])
+    came = turn(sent, 0, 1)
     pair = (kept + came.astype(F32)).reshape(ROWS, CHIPS * COLS)
     rounded = pair.astype(BF)
     total = lax.dynamic_slice_in_dim(pair, chip * COLS, COLS, 1)
     for step in range(1, CHIPS):
         block = lax.dynamic_slice_in_dim(rounded, ((chip + step) % CHIPS) * COLS, COLS, 1)
-        pairs = [(i, (i + step * CORES) % TENSOR) for i in range(TENSOR)]
-        total = total + lax.ppermute(block, "tensor", pairs).astype(F32)
+        total = total + turn(block, step, 0).astype(F32)
     return total
 
 
@@ -284,7 +335,7 @@
     adapter_ids,
     hub_weights,
 ):
-    attended, picks, payload = attend(
+    attended, picks_out, payload = attend(
         queries,
         cache_keys.reshape(-1, HEAD_DIM),
         cache_values.reshape(-1, HEAD_DIM),
@@ -296,12 +347,14 @@
     )
     got = swap(payload, "adapter")
     frozen = frozen_sum(attended, out_weight)
-    got, frozen = lax.optimization_barrier((got, frozen))
+    picks = call(pick_kernel, shape_of(PARTS * ROWS, LINES), adapter_ids.T, attended)
+    got, frozen, picks = lax.optimization_barrier((got, frozen, picks))
     lowered = lower(got, adapter_down)
     lowered = swap(lowered, "adapter")
-    share = call(home_kernel, shape_of(TENSOR * ROWS // 2, 128, dtype=F32), lowered, picks)
-    share = swap(share, "tensor")
-    mixed = call(mix_kernel, shape_of(LINES, 256), share, picks)
+    share = call(home_kernel, shape_of(ROWS // 2, 128, dtype=F32), lowered, picks)
+    share = share + turn(share, 0, 1)
+    shares = [turn(share, step, 0) for step in (1, CHIPS - 1, 2)]
+    mixed = call(mix_kernel, shape_of(LINES, 256), share, *shares, picks_out)
     mixed = swap(mixed, "adapter")
     meta = got[:, PARTS * FEATS :]
     raised = call(raise_kernel, shape_of(LINES, PARTS * COLS), mixed, meta, adapter_up)

time: 132 us -> 129 us (0.977)
  blocking collectives: 52.1 us -> 40.8 us
  starting transfers between devices: 21.5 us -> 25.5 us
  local copies, waits for them, and re-layouts: 3.88 us -> 6.48 us
  Pallas kernels: 13.8 us -> 12 us
    all_to_all x3 -> x2, blocking collectives: 52.1 us -> 40.8 us  [swap(): return lax.all_to_all(x, axis, split_axis=0, concat_axis=0, tiled=True)]
    ppermute x4 -> x8, waiting for transfers between devices: 4.43 us -> 10.6 us  [turn(): return lax.ppermute(x, 'tensor', pairs)]
    all_to_all x2, waiting for transfers between devices: 29.1 us -> 23.9 us  [swap(): return lax.all_to_all(x, axis, split_axis=0, concat_axis=0, tiled=True)]
    ppermute x4 -> x8, starting transfers between devices: 5.74 us -> 9.72 us  [turn(): return lax.ppermute(x, 'tensor', pairs)]
    pallas_call x4 -> x5, Pallas kernels: 4.26 us -> 4.01 us  [call(): pl.pallas_call(kernel, out_shape=out_shape, compiler_params=pltpu.Compile...]
  transfers between devices with their start and end apart: 6 -> 10, of which waited for: 5 -> 9; matrix products, arithmetic and copies ran while one was open for 8% -> 11% of each run, Pallas kernels for 0% -> 0%
where the time goes in v3:
time: 129 us; the launch traced here: 128 us
  blocking collectives  40.8 us (32%)
  waiting for transfers between devices  34.5 us (27%)
  starting transfers between devices  25.5 us (20%)
  Pallas kernels  12 us (9%)
  local copies, waits for them, and re-layouts  6.48 us (5%)
  matrix products  5.83 us (5%)
  other arithmetic  3.04 us (2%)
    all_to_all x2, blocking collectives, swap(): return lax.all_to_all(x, axis, split_axis=0, concat_axis=0, tiled=True)  40.8 us
    all_to_all x2, waiting for transfers between devices, swap(): return lax.all_to_all(x, axis, split_axis=0, concat_axis=0, tiled=True)  23.9 us
    all_to_all x2, starting transfers between devices, swap(): return lax.all_to_all(x, axis, split_axis=0, concat_axis=0, tiled=True)  15.8 us
    ppermute x8, waiting for transfers between devices, turn(): return lax.ppermute(x, 'tensor', pairs)  10.6 us
    ppermute x8, starting transfers between devices, turn(): return lax.ppermute(x, 'tensor', pairs)  9.72 us
    dot_general x1, matrix products, frozen_sum(): part = jnp.dot(attended, out_weight, preferred_element_type=F32)  5.83 us
    pallas_call x5, Pallas kernels, call(): pl.pallas_call(kernel, out_shape=out_shape, compiler_params=pltpu.Compile...  4.01 us
    pallas_call x1, Pallas kernels, lower(): pl.pallas_call(lower_kernel, out_shape=shape_of(LINES, 256), in_specs=[pl...  4 us
  transfers between devices with their start and end apart: 10, of which 9 were waited for; matrix products, arithmetic and copies ran while one was open for 11% of the time, Pallas kernels for 0%

profile of v3, /device:TPU:32, one launch (start us, length us, event | category | flops | bytes accessed | tf_op | source)
XLA Modules:
  0.0 128.2 jit_solution(12049825846306530970)
XLA Ops:
  0.0 4.0 %shard_map.109 = (bf16[48,1024]{1,0:T(8,128)(2,1)S(1)}, bf16[768,48]{1,0:T(8,128)(2,1)S(1)}, bf16[256,3200]{1,0:T(8,128)(2,1)}) custom-call(bf16[48,1024]{1,0:T(8,128)(2,1)} %q_hbm.1, bf16[1536,128]{1,0:T(8,128)(2,1)} %bitcast.33, bf16[1536,128]{1,0:T(8,128)(2,1)} %bitcast.34, bf16[48,128]{1,0:T(8,128)(2,1)} %nk_hbm.1, bf16[48,128]{1,0:T(8,128)(2,1)} %nv_hbm.1, ...), custom_call_target="tpu_custom_call" | custom-call | tf_op jit(solution)/shard_map/pallas_call | solution.py:249
  4.0 11.4 %all-to-all-start = ((bf16[32,8,3200]{2,1,0:T(8,128)(2,1)}), bf16[32,8,3200]{2,1,0:T(8,128)(2,1)S(1)}, u32[]{:S(2)}, u32[]{:S(2)}) async-start(bf16[32,8,3200]{2,1,0:T(8,128)(2,1)} %bitcast.5), calls=%async_computation | async-start | bytes 3276800 | tf_op jit(solution)/shard_map/all_to_all | solution.py:298
  15.4 5.8 %fusion.2 = f32[48,4096]{1,0:T(8,128)} fusion(bf16[48,1024]{1,0:T(8,128)(2,1)S(1)} %get-tuple-element.12.after, bf16[1024,4096]{1,0:T(8,128)(2,1)} %param.17), kind=kOutput, calls=%fused_computation.8 | convolution fusion | flops 402653184 | bytes 9273344 | tf_op jit(solution)/shard_map/dot_general | solution.py:311
  21.2 2.8 %reshape.31 = f32[48,4,2,512]{3,2,1,0:T(2,128)} reshape(f32[48,4096]{1,0:T(8,128)} %fusion.2) | data formatting | bytes 1572864 | tf_op jit(solution)/shard_map/reshape | solution.py:312
  24.0 2.2 %fusion.1 = (f32[48,4,1,512]{3,2,1,0:T(1,128)S(1)}, f32[48,4,1,512]{3,2,1,0:T(1,128)S(1)}) fusion(f32[48,4,2,512]{3,2,1,0:T(2,128)} %reshape.31), kind=kLoop, calls=%fused_computation.7 | loop fusion | bytes 1572864 | tf_op jit(solution)/shard_map/slice | solution.py:313
  26.2 0.8 copy-done.2
  26.9 0.8 fusion
  27.8 1.8 %collective-permute-done = bf16[48,4,512]{2,1,0:T(4,128)(2,1)} collective-permute-done((bf16[48,4,512]{2,1,0:T(4,128)(2,1)}, bf16[48,4,512]{2,1,0:T(4,128)(2,1)}, u32[]{:S(2)}, u32[]{:S(2)}) %collective-permute-start) | collective-permute-done | bytes 196640 | tf_op jit(solution)/shard_map/ppermute | solution.py:305
  29.6 1.3 %bitcast_add_fusion = f32[48,4,512]{2,1,0:T(4,128)S(1)} fusion(bf16[48,4,512]{2,1,0:T(4,128)(2,1)} %collective-permute-done, f32[48,4,1,512]{3,2,1,0:T(1,128)S(1)} %get-tuple-element.17, f32[48,4,1,512]{3,2,1,0:T(1,128)} %copy-done.2, pred[]{:T(512)S(6)} %eq.9), kind=kLoop, calls=%fused_computation | loop fusion | flops 294912 | bytes 1376257 | tf_op jit(solution)/shard_map/add | solution.py:316
  31.0 0.6 constant_dynamic-slice_fusion.2
  31.7 2.8 %collective-permute-start.3 = (bf16[48,512]{1,0:T(8,128)(2,1)}, bf16[48,512]{1,0:T(8,128)(2,1)}, u32[]{:S(2)}, u32[]{:S(2)}) collective-permute-start(bf16[48,512]{1,0:T(8,128)(2,1)} %get-tuple-element.20), channel_id=1, source_target_pairs={{0,6},{1,7},{2,0},{3,1},{4,2},{5,3},{6,4},{7,5},{8,14},{9,15},{10,... | collective-permute-start | bytes 147464 | tf_op jit(solution)/shard_map/ppermute | solution.py:305
  34.4 0.8 collective-permute-start.2
  35.2 0.9 collective-permute-start.1
  36.4 0.3 collective-permute-done.3
  36.7 3.4 %collective-permute-done.2 = bf16[48,512]{1,0:T(8,128)(2,1)} collective-permute-done((bf16[48,512]{1,0:T(8,128)(2,1)S(1)}, bf16[48,512]{1,0:T(8,128)(2,1)}, u32[]{:S(2)}, u32[]{:S(2)}) %collective-permute-start.2) | collective-permute-done | bytes 49184 | tf_op jit(solution)/shard_map/ppermute | solution.py:305
  40.1 0.5 collective-permute-done.1
  40.7 0.9 convert_add_fusion.frozen
  41.5 14.1 %all-to-all-done = bf16[32,8,3200]{2,1,0:T(8,128)(2,1)S(1)} async-done(((bf16[32,8,3200]{2,1,0:T(8,128)(2,1)}), bf16[32,8,3200]{2,1,0:T(8,128)(2,1)S(1)}, u32[]{:S(2)}, u32[]{:S(2)}) %all-to-all-start) | async-done | bytes 1638432 | tf_op jit(solution)/shard_map/all_to_all | solution.py:298
  55.6 4.0 %shard_map.111 = bf16[256,256]{1,0:T(8,128)(2,1)S(1)} custom-call(bf16[256,3200]{1,0:T(8,128)(2,1)S(1)} %bitcast.21, bf16[1024,1024]{1,0:T(8,128)(2,1)} %down.1), custom_call_target="tpu_custom_call" | custom-call | tf_op jit(solution)/shard_map/pallas_call | solution.py:273
  59.7 15.6 %all_to_all.45 = bf16[32,8,256]{2,1,0:T(8,128)(2,1)S(1)} all-to-all(bf16[32,8,256]{2,1,0:T(8,128)(2,1)S(1)} %bitcast.27), channel_id=1, replica_groups=mesh['adapter'=32,'tensor'=8] {'adapter'}, dimensions={0} | all-to-all | bytes 262144 | tf_op jit(solution)/shard_map/all_to_all | solution.py:298
  75.3 0.3 shard_map.112
  75.8 1.2 collective-permute-done.4
  76.9 1.4 %collective-permute-start.5 = (f32[24,128]{1,0:T(8,128)S(1)}, f32[24,128]{1,0:T(8,128)S(1)}, u32[]{:S(2)}, u32[]{:S(2)}) collective-permute-start(f32[24,128]{1,0:T(8,128)S(1)} %add.65.own), channel_id=1, source_target_pairs={{0,2},{1,3},{2,4},{3,5},{4,6},{5,7},{6,0},{7,1},{8,10},{9,11},{10,... | collective-permute-start | bytes 36872 | tf_op jit(solution)/shard_map/ppermute | solution.py:305
  78.3 1.8 %collective-permute-start.6 = (f32[24,128]{1,0:T(8,128)S(1)}, f32[24,128]{1,0:T(8,128)S(1)}, u32[]{:S(2)}, u32[]{:S(2)}) collective-permute-start(f32[24,128]{1,0:T(8,128)S(1)} %add.65.own), channel_id=1, source_target_pairs={{0,6},{1,7},{2,0},{3,1},{4,2},{5,3},{6,4},{7,5},{8,14},{9,15},{10,... | collective-permute-start | bytes 36872 | tf_op jit(solution)/shard_map/ppermute | solution.py:305
  80.2 1.8 %collective-permute-start.7 = (f32[24,128]{1,0:T(8,128)S(1)}, f32[24,128]{1,0:T(8,128)S(1)}, u32[]{:S(2)}, u32[]{:S(2)}) collective-permute-start(f32[24,128]{1,0:T(8,128)S(1)} %add.65.own), channel_id=1, source_target_pairs={{0,4},{1,5},{2,6},{3,7},{4,0},{5,1},{6,2},{7,3},{8,12},{9,13},{10,... | collective-permute-start | bytes 36872 | tf_op jit(solution)/shard_map/ppermute | solution.py:305
  82.0 3.3 %collective-permute-done.7.across = f32[24,128]{1,0:T(8,128)S(1)} collective-permute-done((f32[24,128]{1,0:T(8,128)S(1)}, f32[24,128]{1,0:T(8,128)S(1)}, u32[]{:S(2)}, u32[]{:S(2)}) %collective-permute-start.7) | collective-permute-done | bytes 12320 | tf_op jit(solution)/shard_map/ppermute | solution.py:305
  85.4 0.9 shard_map.113
  86.3 4.4 %all-to-all-start.2 = ((bf16[32,8,256]{2,1,0:T(8,128)(2,1)}), bf16[32,8,256]{2,1,0:T(8,128)(2,1)S(1)}, u32[]{:S(2)}, u32[]{:S(2)}) async-start(bf16[32,8,256]{2,1,0:T(8,128)(2,1)} %bitcast.11), calls=%async_computation.2 | async-start | bytes 262144 | tf_op jit(solution)/shard_map/all_to_all | solution.py:298
  90.7 9.8 %all-to-all-done.2 = bf16[32,8,256]{2,1,0:T(8,128)(2,1)S(1)} async-done(((bf16[32,8,256]{2,1,0:T(8,128)(2,1)}), bf16[32,8,256]{2,1,0:T(8,128)(2,1)S(1)}, u32[]{:S(2)}, u32[]{:S(2)}) %all-to-all-start.2) | async-done | bytes 131104 | tf_op jit(solution)/shard_map/all_to_all | solution.py:298
  100.5 1.7 %shard_map.114 = bf16[256,1536]{1,0:T(8,128)(2,1)S(1)} custom-call(bf16[256,256]{1,0:T(8,128)(2,1)S(1)} %bitcast.25, bf16[256,128]{1,0:T(8,128)(2,1)S(1)} %slice.13.meta, bf16[1024,512]{1,0:T(8,128)(2,1)S(1)} %copy-done), custom_call_target="tpu_custom_call" | custom-call | tf_op jit(solution)/shard_map/pallas_call | solution.py:286
  102.2 25.1 %all_to_all.46 = bf16[32,8,1536]{2,1,0:T(8,128)(2,1)S(1)} all-to-all(bf16[32,8,1536]{2,1,0:T(8,128)(2,1)S(1)} %bitcast.24), channel_id=1, replica_groups=mesh['adapter'=32,'tensor'=8] {'adapter'}, dimensions={0} | all-to-all | bytes 1572864 | tf_op jit(solution)/shard_map/all_to_all | solution.py:298
  127.4 0.9 shard_map.115
  (14 shorter events, 0.7 us)
Async XLA Ops:
  4.0 51.6 %all-to-all-start = ((bf16[32,8,3200]{2,1,0:T(8,128)(2,1)}), bf16[32,8,3200]{2,1,0:T(8,128)(2,1)S(1)}, u32[]{:S(2)}, u32[]{:S(2)}) async-start(bf16[32,8,3200]{2,1,0:T(8,128)(2,1)} %bitcast.5), calls=%async_computation | async-start | bytes 3276800 | tf_op jit(solution)/shard_map/all_to_all | solution.py:298
  15.4 20.7 %copy-start.1 = (s32[48,4]{0,1:T(4,128)S(1)}, s32[48,4]{0,1:T(4,128)}, u32[]{:S(2)}) copy-start(s32[48,4]{0,1:T(4,128)} %param.20) | copy-start | bytes 2308
  21.2 79.3 %copy-start = (bf16[1024,512]{1,0:T(8,128)(2,1)S(1)}, bf16[1024,512]{1,0:T(8,128)(2,1)}, u32[]{:S(2)}) copy-start(bf16[1024,512]{1,0:T(8,128)(2,1)} %up.1) | copy-start | bytes 3145732
  26.2 0.8 copy-start.2
  27.8 1.8 %collective-permute-start = (bf16[48,4,512]{2,1,0:T(4,128)(2,1)}, bf16[48,4,512]{2,1,0:T(4,128)(2,1)}, u32[]{:S(2)}, u32[]{:S(2)}) collective-permute-start(bf16[48,4,512]{2,1,0:T(4,128)(2,1)} %fusion), channel_id=1, source_target_pairs={{0,1},{1,0},{2,3},{3,2},{4,5},{5,4},{6,7},{7,6},{8,9},{9,8},{10,11... | collective-permute-start | bytes 589832 | tf_op jit(solution)/shard_map/ppermute | solution.py:305
  31.7 5.0 %collective-permute-start.3 = (bf16[48,512]{1,0:T(8,128)(2,1)}, bf16[48,512]{1,0:T(8,128)(2,1)}, u32[]{:S(2)}, u32[]{:S(2)}) collective-permute-start(bf16[48,512]{1,0:T(8,128)(2,1)} %get-tuple-element.20), channel_id=1, source_target_pairs={{0,6},{1,7},{2,0},{3,1},{4,2},{5,3},{6,4},{7,5},{8,14},{9,15},{10,... | collective-permute-start | bytes 147464 | tf_op jit(solution)/shard_map/ppermute | solution.py:305
  34.4 5.7 %collective-permute-start.2 = (bf16[48,512]{1,0:T(8,128)(2,1)S(1)}, bf16[48,512]{1,0:T(8,128)(2,1)}, u32[]{:S(2)}, u32[]{:S(2)}) collective-permute-start(bf16[48,512]{1,0:T(8,128)(2,1)S(1)} %get-tuple-element.21), channel_id=1, source_target_pairs={{0,4},{1,5},{2,6},{3,7},{4,0},{5,1},{6,2},{7,3},{8,12},{9,13},{10,... | collective-permute-start | bytes 147464 | tf_op jit(solution)/shard_map/ppermute | solution.py:305
  35.2 5.4 %collective-permute-start.1 = (bf16[48,512]{1,0:T(8,128)(2,1)S(1)}, bf16[48,512]{1,0:T(8,128)(2,1)}, u32[]{:S(2)}, u32[]{:S(2)}) collective-permute-start(bf16[48,512]{1,0:T(8,128)(2,1)S(1)} %get-tuple-element.19), channel_id=1, source_target_pairs={{0,2},{1,3},{2,4},{3,5},{4,6},{5,7},{6,0},{7,1},{8,10},{9,11},{10,... | collective-permute-start | bytes 147464 | tf_op jit(solution)/shard_map/ppermute | solution.py:305
  75.5 1.4 %collective-permute-start.4 = (f32[24,128]{1,0:T(8,128)S(1)}, f32[24,128]{1,0:T(8,128)S(1)}, u32[]{:S(2)}, u32[]{:S(2)}) collective-permute-start(f32[24,128]{1,0:T(8,128)S(1)} %shard_map.112), channel_id=1, source_target_pairs={{0,1},{1,0},{2,3},{3,2},{4,5},{5,4},{6,7},{7,6},{8,9},{9,8},{10,11... | collective-permute-start | bytes 36872 | tf_op jit(solution)/shard_map/ppermute | solution.py:305
  76.9 5.0 %collective-permute-start.5 = (f32[24,128]{1,0:T(8,128)S(1)}, f32[24,128]{1,0:T(8,128)S(1)}, u32[]{:S(2)}, u32[]{:S(2)}) collective-permute-start(f32[24,128]{1,0:T(8,128)S(1)} %add.65.own), channel_id=1, source_target_pairs={{0,2},{1,3},{2,4},{3,5},{4,6},{5,7},{6,0},{7,1},{8,10},{9,11},{10,... | collective-permute-start | bytes 36872 | tf_op jit(solution)/shard_map/ppermute | solution.py:305
  78.3 3.7 %collective-permute-start.6 = (f32[24,128]{1,0:T(8,128)S(1)}, f32[24,128]{1,0:T(8,128)S(1)}, u32[]{:S(2)}, u32[]{:S(2)}) collective-permute-start(f32[24,128]{1,0:T(8,128)S(1)} %add.65.own), channel_id=1, source_target_pairs={{0,6},{1,7},{2,0},{3,1},{4,2},{5,3},{6,4},{7,5},{8,14},{9,15},{10,... | collective-permute-start | bytes 36872 | tf_op jit(solution)/shard_map/ppermute | solution.py:305
  80.2 5.2 %collective-permute-start.7 = (f32[24,128]{1,0:T(8,128)S(1)}, f32[24,128]{1,0:T(8,128)S(1)}, u32[]{:S(2)}, u32[]{:S(2)}) collective-permute-start(f32[24,128]{1,0:T(8,128)S(1)} %add.65.own), channel_id=1, source_target_pairs={{0,4},{1,5},{2,6},{3,7},{4,0},{5,1},{6,2},{7,3},{8,12},{9,13},{10,... | collective-permute-start | bytes 36872 | tf_op jit(solution)/shard_map/ppermute | solution.py:305
  86.3 14.2 %all-to-all-start.2 = ((bf16[32,8,256]{2,1,0:T(8,128)(2,1)}), bf16[32,8,256]{2,1,0:T(8,128)(2,1)S(1)}, u32[]{:S(2)}, u32[]{:S(2)}) async-start(bf16[32,8,256]{2,1,0:T(8,128)(2,1)} %bitcast.11), calls=%async_computation.2 | async-start | bytes 262144 | tf_op jit(solution)/shard_map/all_to_all | solution.py:298

commit v4 on v3

--- a/solution.py
+++ b/solution.py
@@ -27,6 +27,9 @@
 CORES = 2
 CHIPS = 4
 DOWN_STEPS = 4
+DEPTH = 8
+SIDES = 4
+COLUMNS = [[y * DEPTH + z for z in range(DEPTH)] for y in range(SIDES)]
 CHUNK = 16
 BF = jnp.bfloat16
 F32 = jnp.float32
@@ -53,8 +56,8 @@
 
 def attend_kernel(
     q_hbm, ck_hbm, cv_hbm, nk_hbm, nv_hbm, lens_hbm, ids_hbm, hub_hbm,
-    att, picks, pay,
-    q, ck, cv, nk, nv, lens, ids, hub, sems, made, out_sems,
+    att, pay,
+    picks, q, ck, cv, nk, nv, lens, ids, hub, sems, made, out_sems,
 ):
     def leave(g, start, width):
         cols = pl.ds(start, width)
@@ -172,12 +175,20 @@
     out[...] = join_parts(pieces).astype(BF)
 
 
-def pick_kernel(ids, after, picks):
+def pick_kernel(ids, hub, after, picks, record):
     owner_of_line = iota((ROWS, LINES), 1) >> 3
     named = jnp.zeros((ROWS, LINES), jnp.bool_)
+    lane = iota((ROWS, 128), 1) - RANK
+    kept = jnp.zeros((ROWS, 128), F32)
     for j in range(TOPA):
-        owner = column(ids[j : j + 1, :].astype(F32)).astype(jnp.int32) >> 4
+        adapter = column(ids[j : j + 1, :].astype(F32)).astype(jnp.int32)
+        owner = adapter >> 4
         named = named | (owner == owner_of_line)
+        high, low = split_parts(column(hub[j : j + 1, :]))
+        fields = (owner.astype(F32), (adapter & (ADP_DEV - 1)).astype(F32), high.astype(F32), low.astype(F32))
+        for k, field in enumerate(fields):
+            kept = jnp.where(lane == k * TOPA + j, field, kept)
+    record[...] = kept.astype(BF)
     earlier = (iota((ROWS, ROWS), 1) < iota((ROWS, ROWS), 0)).astype(BF)
     place = dot(earlier, named.astype(BF)).astype(jnp.int32)
     place = jnp.where(named, place, -1)
@@ -186,7 +197,14 @@
         picks[pl.ds(g * ROWS, ROWS), :] = (place == spot + g * PART).astype(BF)
 
 
-def home_kernel(got, picks, out):
+def home_kernel(got, picks, ahead, behind, out, far_low, far_high, sems):
+    half = far_low.shape[0]
+    copies = [
+        pltpu.make_async_copy(ahead.at[pl.ds(0, half), :], far_low, sems.at[0]),
+        pltpu.make_async_copy(behind.at[pl.ds(half, half), :], far_high, sems.at[1]),
+    ]
+    for copy in copies:
+        copy.start()
     lane = iota((ROWS, 256), 1)
     total = jnp.zeros((ROWS, 256), F32)
     for g in range(PARTS):
@@ -194,55 +212,103 @@
         total = total + jnp.where((lane >> 6) == g, part, 0.0)
     folded = total[:, :128] + total[:, 128:]
     folded = folded + pltpu.roll(folded, RANK, 1)
-    half = ROWS // 2
-    lane = iota((half, 128), 1)
-    out[...] = jnp.where(lane < RANK, folded[:half, :], folded[half:, :])
-
-
-def mix_kernel(own, ahead, behind, across, picks, out):
+    few = ROWS // 2
+    lane = iota((few, 128), 1)
+    out[...] = jnp.where(lane < RANK, folded[:few, :], folded[few:, :])
+    for copy in copies:
+        copy.wait()
+
+
+def mix_kernel(own, ahead, behind, across, record, out):
     half = ROWS // 2
     total = (own[...] + ahead[...]) + (behind[...] + across[...])
     other = pltpu.roll(total, RANK, 1)
-    lane = iota((half, 128), 1)
-    first = jnp.where(lane < RANK, total, other)
-    second = jnp.where(lane < RANK, other, total)
-    mixed = jnp.concatenate([first, second], axis=0).astype(BF)
-    pieces = [dot(picks[pl.ds(g * LINES, LINES), :], mixed) for g in range(PARTS)]
-    out[...] = join_parts(pieces).astype(BF)
-
-
-def raise_kernel(got, meta, up, out):
-    lane = iota((LINES, 128), 1)
-    first = got[:, :128].astype(F32)
-    second = got[:, 128:].astype(F32)
-    turned = pltpu.roll(first, RANK, 1)
-    pairs = (
-        jnp.where(lane < RANK, first, turned),
-        jnp.where(lane < RANK, turned, first),
-        jnp.where(lane < RANK, second, pltpu.roll(second, RANK, 1)),
-    )
-    blocks = []
-    for g in range(PARTS):
-        coefs = coefs_of(meta[...], g)
-        blocks.append(
-            jnp.concatenate(
-                [
-                    (coefs[:, p * 128 : (p + 1) * 128] * pairs[g]).astype(BF)
-                    for p in range(ADP_DEV * RANK // 128)
-                ],
-                axis=1,
-            )
+    mixed = jnp.concatenate([total, other], axis=0)
+    lane = iota((ROWS, 128), 1)
+    sent = jnp.where(lane < RANK, mixed, record[...].astype(F32)).astype(BF)
+    for z in range(DEPTH):
+        out[pl.ds(z * ROWS, ROWS), :] = sent
+
+
+def raise_kernel(place, got, *refs):
+    ups, (out, held, sems) = refs[: SIDES + 1], refs[SIDES + 1 :]
+    half = held.shape[1] // 2
+    copies = []
+    for b in range(SIDES + 1):
+        if b < SIDES - 1:
+            target = held.at[b]
+        else:
+            target = held.at[SIDES - 1, pl.ds((b - SIDES + 1) * half, half), :]
+        copies.append(pltpu.make_async_copy(ups[b], target, sems.at[b]))
+        copies[-1].start()
+    me = place[0, 0]
+    y, z = me >> 3, me & (DEPTH - 1)
+    rows = DEPTH * ROWS
+    lane = iota((1, 128), 1)
+    spot = lane & (RANK - 1)
+    side = spot >> 4
+    away = jnp.where(side == 3, 2, jnp.where(side == 2, 3, side))
+    wanted = ((((y + away) & (SIDES - 1)) * DEPTH + z) * ADP_DEV + (spot & (ADP_DEV - 1))).astype(F32)
+    record = got[...].astype(F32)
+    lanes = iota((rows, 128), 1)
+    coef = jnp.zeros((rows, 128), F32)
+    for j in range(TOPA):
+        owner, local, high, low = (
+            record[:, RANK + k * TOPA + j : RANK + k * TOPA + j + 1] for k in range(4)
         )
-    raised = dot(jnp.concatenate(blocks, axis=0), up[...]).astype(BF)
-    for g in range(PARTS):
-        out[:, g * COLS : (g + 1) * COLS] = raised[g * LINES : (g + 1) * LINES, :]
-
-
-def final_kernel(got, picks, frozen, out):
+        weight = jnp.where(lanes < RANK, high, low)
+        coef = jnp.where(owner * ADP_DEV + local == wanted, weight, coef)
+    coef = coef.astype(BF)
+    mixed = jnp.where(lanes < RANK, record, pltpu.roll(record, RANK, 1))
+    shape = (128, ADP_DEV * RANK)
+    line = iota(shape, 0) & (RANK - 1)
+    adapter = iota(shape, 1) >> 6
+    total = jnp.zeros((rows, COLS), F32)
+    for b in range(SIDES):
+        coefs = dot(coef, (line == adapter + b * ADP_DEV).astype(BF))
+        expanded = jnp.concatenate(
+            [(coefs[:, p * 128 : (p + 1) * 128] * mixed).astype(BF) for p in range(ADP_DEV * RANK // 128)],
+            axis=1,
+        )
+        copies[b].wait()
+        if b == SIDES - 1:
+            copies[SIDES].wait()
+        total = total + dot(expanded, held[b])
+    out[...] = total.astype(BF)
+
+
+def final_kernel(got, frozen, out):
     total = frozen[...]
-    for g in range(PARTS):
-        total = total + dot(picks[pl.ds(g * ROWS, ROWS), :], got[:, g * COLS : (g + 1) * COLS])
+    for z in range(DEPTH):
+        total = total + got[pl.ds(z * ROWS, ROWS), :].astype(F32)
     out[...] = total.astype(BF)
+
+
+def home(got, picks, ahead, behind):
+    half = shape_of(ahead.shape[0] // 2, ahead.shape[1])
+    vmem, hbm = (pl.BlockSpec(memory_space=space) for space in (pltpu.VMEM, pltpu.HBM))
+    return pl.pallas_call(
+        home_kernel,
+        out_shape=(shape_of(ROWS // 2, 128, dtype=F32), half, half),
+        in_specs=[vmem, vmem, hbm, hbm],
+        out_specs=(vmem, hbm, hbm),
+        scratch_shapes=[pltpu.SemaphoreType.DMA((2,))],
+        compiler_params=pltpu.CompilerParams(vmem_limit_bytes=24 * 1024 * 1024),
+    )(got, picks, *[pltpu.with_memory_space_constraint(x, pltpu.HBM) for x in (ahead, behind)])
+
+
+def lift(place, got, ups):
+    return pl.pallas_call(
+        raise_kernel,
+        out_shape=shape_of(DEPTH * ROWS, COLS),
+        in_specs=[pl.BlockSpec(memory_space=pltpu.SMEM), pl.BlockSpec(memory_space=pltpu.VMEM)]
+        + [pl.BlockSpec(memory_space=pltpu.HBM)] * len(ups),
+        scratch_shapes=[
+            pltpu.VMEM((SIDES, *ups[0].shape), BF),
+            pltpu.SemaphoreType.DMA((len(ups),)),
+        ],
+        compiler_params=pltpu.CompilerParams(vmem_limit_bytes=32 * 1024 * 1024),
+    )(place, got, *[pltpu.with_memory_space_constraint(up, pltpu.HBM) for up in ups])
 
 
 def attend(*args):
@@ -250,16 +316,15 @@
         attend_kernel,
         out_shape=(
             shape_of(ROWS, FEATS),
-            shape_of(PARTS * LINES, ROWS),
             shape_of(LINES, PARTS * FEATS + 128),
         ),
         in_specs=[pl.BlockSpec(memory_space=pltpu.HBM)] * len(args),
         out_specs=(
             pl.BlockSpec(memory_space=pltpu.VMEM),
-            pl.BlockSpec(memory_space=pltpu.VMEM),
             pl.BlockSpec(memory_space=pltpu.HBM),
         ),
-        scratch_shapes=[pltpu.VMEM(x.shape, x.dtype) for x in args]
+        scratch_shapes=[pltpu.VMEM((PARTS * LINES, ROWS), BF)]
+        + [pltpu.VMEM(x.shape, x.dtype) for x in args]
         + [
             pltpu.SemaphoreType.DMA((len(args),)),
             pltpu.VMEM((LINES, PARTS * FEATS + 128), BF),
@@ -294,8 +359,15 @@
     return jax.ShapeDtypeStruct(shape, dtype)
 
 
-def swap(x, axis):
-    return lax.all_to_all(x, axis, split_axis=0, concat_axis=0, tiled=True)
+def swap(x, axis, groups=None):
+    return lax.all_to_all(
+        x, axis, split_axis=0, concat_axis=0, axis_index_groups=groups, tiled=True
+    )
+
+
+def beside(x, steps):
+    pairs = [(i, (i // DEPTH - steps) % SIDES * DEPTH + i % DEPTH) for i in range(OWNERS)]
+    return lax.ppermute(x, "adapter", pairs)
 
 
 def turn(x, chips, cores):
@@ -335,7 +407,7 @@
     adapter_ids,
     hub_weights,
 ):
-    attended, picks_out, payload = attend(
+    attended, payload = attend(
         queries,
         cache_keys.reshape(-1, HEAD_DIM),
         cache_values.reshape(-1, HEAD_DIM),
@@ -347,19 +419,27 @@
     )
     got = swap(payload, "adapter")
     frozen = frozen_sum(attended, out_weight)
-    picks = call(pick_kernel, shape_of(PARTS * ROWS, LINES), adapter_ids.T, attended)
-    got, frozen, picks = lax.optimization_barrier((got, frozen, picks))
+    picks, record = call(
+        pick_kernel,
+        (shape_of(PARTS * ROWS, LINES), shape_of(ROWS, 128)),
+        adapter_ids.T,
+        hub_weights.T,
+        attended,
+    )
+    later_up, attended = lax.optimization_barrier((adapter_up, attended))
+    ahead, behind = beside(later_up, 1), beside(later_up, SIDES - 1)
+    got, frozen, picks, record = lax.optimization_barrier((got, frozen, picks, record))
     lowered = lower(got, adapter_down)
     lowered = swap(lowered, "adapter")
-    share = call(home_kernel, shape_of(ROWS // 2, 128, dtype=F32), lowered, picks)
+    share, far_low, far_high = home(lowered, picks, ahead, behind)
+    ups = (adapter_up, ahead, behind, beside(far_low, 1), beside(far_high, SIDES - 1))
     share = share + turn(share, 0, 1)
     shares = [turn(share, step, 0) for step in (1, CHIPS - 1, 2)]
-    mixed = call(mix_kernel, shape_of(LINES, 256), share, *shares, picks_out)
-    mixed = swap(mixed, "adapter")
-    meta = got[:, PARTS * FEATS :]
-    raised = call(raise_kernel, shape_of(LINES, PARTS * COLS), mixed, meta, adapter_up)
-    raised = swap(raised, "adapter")
-    return call(final_kernel, shape_of(ROWS, COLS), raised, picks, frozen)
+    mixed = call(mix_kernel, shape_of(DEPTH * ROWS, 128), share, *shares, record)
+    mixed = swap(mixed, "adapter", COLUMNS)
+    place = lax.axis_index("adapter").reshape(1, 1)
+    raised = swap(lift(place, mixed, ups), "adapter", COLUMNS)
+    return call(final_kernel, shape_of(ROWS, COLS), raised, frozen)
 
 
 def solution(mesh):

time: 129 us -> 124 us (0.961)
  blocking collectives: 40.8 us -> 14.9 us
  starting transfers between devices: 25.5 us -> 37.4 us
  waiting for transfers between devices: 34.5 us -> 41.2 us
  Pallas kernels: 12 us -> 16 us
  local copies, waits for them, and re-layouts: 6.48 us -> 4.94 us
    all_to_all x2 -> x1, blocking collectives: 40.8 us -> 14.9 us  [swap(): lax.all_to_all(x, axis, split_axis=0, concat_axis=0, axis_index_groups=gr...]
    all_to_all x2 -> x3, waiting for transfers between devices: 23.9 us -> 34.2 us  [swap(): lax.all_to_all(x, axis, split_axis=0, concat_axis=0, axis_index_groups=gr...]
    all_to_all x2 -> x3, starting transfers between devices: 15.8 us -> 21.7 us  [swap(): lax.all_to_all(x, axis, split_axis=0, concat_axis=0, axis_index_groups=gr...]
    pallas_call x0 -> x2, Pallas kernels: none -> 5.4 us  [the longest x1 4.17 us: lift(): pl.pallas_call(raise_kernel, out_shape=shape_of(DEPTH * ROWS, COLS), in_s...]
    ppermute x0 -> x4, starting transfers between devices: none -> 4.83 us  [beside(): return lax.ppermute(x, 'adapter', pairs)]
    ppermute x8, waiting for transfers between devices: 10.6 us -> 7.04 us  [turn(): return lax.ppermute(x, 'tensor', pairs)]
    pallas_call x5 -> x3, Pallas kernels: 4.01 us -> 1.63 us  [call(): pl.pallas_call(kernel, out_shape=out_shape, compiler_params=pltpu.Compile...]
  transfers between devices with their start and end apart: 10 -> 15, of which waited for: 9 -> 8; matrix products, arithmetic and copies ran while one was open for 11% -> 10% of each run, Pallas kernels for 0% -> 5%
where the time goes in v4:
time: 124 us; the launch traced here: 123 us
  waiting for transfers between devices  41.2 us (33%)
  starting transfers between devices  37.4 us (30%)
  Pallas kernels  16 us (13%)
  blocking collectives  14.9 us (12%)
  matrix products  4.95 us (4%)
  local copies, waits for them, and re-layouts  4.94 us (4%)
  other arithmetic  2.9 us (2%)
    all_to_all x3, waiting for transfers between devices, swap(): lax.all_to_all(x, axis, split_axis=0, concat_axis=0, axis_index_groups=gr...  34.2 us
    all_to_all x3, starting transfers between devices, swap(): lax.all_to_all(x, axis, split_axis=0, concat_axis=0, axis_index_groups=gr...  21.7 us
    all_to_all x1, blocking collectives, swap(): lax.all_to_all(x, axis, split_axis=0, concat_axis=0, axis_index_groups=gr...  14.9 us
    ppermute x8, starting transfers between devices, turn(): return lax.ppermute(x, 'tensor', pairs)  10.8 us
    ppermute x8, waiting for transfers between devices, turn(): return lax.ppermute(x, 'tensor', pairs)  7.04 us
    pallas_call x1, Pallas kernels, lower(): pl.pallas_call(lower_kernel, out_shape=shape_of(LINES, 256), in_specs=[pl...  5.01 us
    dot_general x1, matrix products, frozen_sum(): part = jnp.dot(attended, out_weight, preferred_element_type=F32)  4.95 us
    ppermute x4, starting transfers between devices, beside(): return lax.ppermute(x, 'adapter', pairs)  4.83 us
  transfers between devices with their start and end apart: 15, of which 8 were waited for; matrix products, arithmetic and copies ran while one was open for 10% of the time, Pallas kernels for 5%

profile of v4, /device:TPU:32, one launch (start us, length us, event | category | flops | bytes accessed | tf_op | source)
XLA Modules:
  0.0 122.5 jit_solution(13734448972615965693)
XLA Ops:
  0.0 4.0 %shard_map.109 = (bf16[48,1024]{1,0:T(8,128)(2,1)S(1)}, bf16[256,3200]{1,0:T(8,128)(2,1)}) custom-call(bf16[48,1024]{1,0:T(8,128)(2,1)} %q_hbm.1, bf16[1536,128]{1,0:T(8,128)(2,1)} %bitcast.34, bf16[1536,128]{1,0:T(8,128)(2,1)} %bitcast.35, bf16[48,128]{1,0:T(8,128)(2,1)} %nk_hbm.1, bf16[48,128]{1,0:T(8,128)(2,1)} %nv_hbm.1, s32[1,48]{1,0:T(1,128)} %bitcast.36, ...), custom_call_target="tpu_custom_call" | custom-call | tf_op jit(solution)/shard_map/pallas_call | solution.py:315
  4.0 11.4 %all-to-all-start = ((bf16[32,8,3200]{2,1,0:T(8,128)(2,1)}), bf16[32,8,3200]{2,1,0:T(8,128)(2,1)S(1)}, u32[]{:S(2)}, u32[]{:S(2)}) async-start(bf16[32,8,3200]{2,1,0:T(8,128)(2,1)} %bitcast.6), calls=%async_computation | async-start | bytes 3276800 | tf_op jit(solution)/shard_map/all_to_all | solution.py:363
  15.4 5.0 %fusion.2 = f32[48,4096]{1,0:T(8,128)S(1)} fusion(bf16[48,1024]{1,0:T(8,128)(2,1)S(1)} %get-tuple-element.18.after, bf16[1024,4096]{1,0:T(8,128)(2,1)} %param.17), kind=kOutput, calls=%fused_computation.8 | convolution fusion | flops 402653184 | bytes 9273344 | tf_op jit(solution)/shard_map/dot_general | solution.py:383
  20.4 1.6 %reshape.35 = f32[48,4,2,512]{3,2,1,0:T(2,128)} reshape(f32[48,4096]{1,0:T(8,128)S(1)} %fusion.2) | data formatting | bytes 1572864 | tf_op jit(solution)/shard_map/reshape | solution.py:384
  22.0 2.2 %fusion.1 = (f32[48,4,1,512]{3,2,1,0:T(1,128)S(1)}, f32[48,4,1,512]{3,2,1,0:T(1,128)S(1)}) fusion(f32[48,4,2,512]{3,2,1,0:T(2,128)} %reshape.35), kind=kLoop, calls=%fused_computation.7 | loop fusion | bytes 1572864 | tf_op jit(solution)/shard_map/slice | solution.py:385
  24.2 0.8 fusion
  25.0 2.7 %collective-permute-start.4 = (bf16[1024,512]{1,0:T(8,128)(2,1)}, bf16[1024,512]{1,0:T(8,128)(2,1)S(1)}, u32[]{:S(2)}, u32[]{:S(2)}) collective-permute-start(bf16[1024,512]{1,0:T(8,128)(2,1)} %refs_0_.1), channel_id=1, source_target_pairs={{0,192},{8,200},{16,208},{24,216},{32,224},{40,232},{48,240},{56,2... | collective-permute-start | bytes 3145736 | tf_op jit(solution)/shard_map/ppermute | solution.py:370
  27.8 1.2 bitcast_add_fusion
  29.2 1.6 %collective-permute-start.1 = (bf16[48,512]{1,0:T(8,128)(2,1)S(1)}, bf16[48,512]{1,0:T(8,128)(2,1)S(1)}, u32[]{:S(2)}, u32[]{:S(2)}) collective-permute-start(bf16[48,512]{1,0:T(8,128)(2,1)S(1)} %get-tuple-element.31), channel_id=1, source_target_pairs={{0,2},{1,3},{2,4},{3,5},{4,6},{5,7},{6,0},{7,1},{8,10},{9,11},{10,... | collective-permute-start | bytes 147464 | tf_op jit(solution)/shard_map/ppermute | solution.py:377
  30.8 2.7 %collective-permute-start.2 = (bf16[48,512]{1,0:T(8,128)(2,1)S(1)}, bf16[48,512]{1,0:T(8,128)(2,1)S(1)}, u32[]{:S(2)}, u32[]{:S(2)}) collective-permute-start(bf16[48,512]{1,0:T(8,128)(2,1)S(1)} %get-tuple-element.33), channel_id=1, source_target_pairs={{0,4},{1,5},{2,6},{3,7},{4,0},{5,1},{6,2},{7,3},{8,12},{9,13},{10,... | collective-permute-start | bytes 147464 | tf_op jit(solution)/shard_map/ppermute | solution.py:377
  33.5 1.4 %collective-permute-start.3 = (bf16[48,512]{1,0:T(8,128)(2,1)S(1)}, bf16[48,512]{1,0:T(8,128)(2,1)}, u32[]{:S(2)}, u32[]{:S(2)}) collective-permute-start(bf16[48,512]{1,0:T(8,128)(2,1)S(1)} %get-tuple-element.32), channel_id=1, source_target_pairs={{0,6},{1,7},{2,0},{3,1},{4,2},{5,3},{6,4},{7,5},{8,14},{9,15},{10,... | collective-permute-start | bytes 147464 | tf_op jit(solution)/shard_map/ppermute | solution.py:377
  35.2 1.2 collective-permute-done.2
  36.4 1.3 %collective-permute-done.3 = bf16[48,512]{1,0:T(8,128)(2,1)} collective-permute-done((bf16[48,512]{1,0:T(8,128)(2,1)S(1)}, bf16[48,512]{1,0:T(8,128)(2,1)}, u32[]{:S(2)}, u32[]{:S(2)}) %collective-permute-start.3) | collective-permute-done | bytes 49184 | tf_op jit(solution)/shard_map/ppermute | solution.py:377
  37.7 0.8 convert_add_fusion.frozen
  38.5 17.1 %all-to-all-done = bf16[32,8,3200]{2,1,0:T(8,128)(2,1)S(1)} async-done(((bf16[32,8,3200]{2,1,0:T(8,128)(2,1)}), bf16[32,8,3200]{2,1,0:T(8,128)(2,1)S(1)}, u32[]{:S(2)}, u32[]{:S(2)}) %all-to-all-start) | async-done | bytes 1638432 | tf_op jit(solution)/shard_map/all_to_all | solution.py:363
  55.6 5.0 %shard_map.111 = bf16[256,256]{1,0:T(8,128)(2,1)} custom-call(bf16[256,3200]{1,0:T(8,128)(2,1)S(1)} %bitcast.22, bf16[1024,1024]{1,0:T(8,128)(2,1)} %down.1), custom_call_target="tpu_custom_call" | custom-call | tf_op jit(solution)/shard_map/pallas_call | solution.py:338
  60.7 6.2 %all-to-all-start.1 = ((bf16[32,8,256]{2,1,0:T(8,128)(2,1)}), bf16[32,8,256]{2,1,0:T(8,128)(2,1)S(1)}, u32[]{:S(2)}, u32[]{:S(2)}) async-start(bf16[32,8,256]{2,1,0:T(8,128)(2,1)} %bitcast.10), calls=%async_computation.1 | async-start | bytes 262144 | tf_op jit(solution)/shard_map/all_to_all | solution.py:363
  66.9 9.7 %all-to-all-done.1 = bf16[32,8,256]{2,1,0:T(8,128)(2,1)S(1)} async-done(((bf16[32,8,256]{2,1,0:T(8,128)(2,1)}), bf16[32,8,256]{2,1,0:T(8,128)(2,1)S(1)}, u32[]{:S(2)}, u32[]{:S(2)}) %all-to-all-start.1) | async-done | bytes 131104 | tf_op jit(solution)/shard_map/all_to_all | solution.py:363
  76.6 1.2 %shard_map.112 = (f32[24,128]{1,0:T(8,128)S(1)}, bf16[512,512]{1,0:T(8,128)(2,1)S(1)}, bf16[512,512]{1,0:T(8,128)(2,1)S(1)}) custom-call(bf16[256,256]{1,0:T(8,128)(2,1)S(1)} %bitcast.25, bf16[144,256]{1,0:T(8,128)(2,1)S(1)} %get-tuple-element.22.picks, bf16[1024,512]{1,0:T(8,128)(2,1)} %copy-done.2, bf16[1024,512]{1,0:T(8,128)(2,1)} %collective-permute-done.5.behind.refs_2_), custom_call_target="tpu_custom_call" | custom-call | tf_op jit(solution)/shard_map/pallas_call | solution.py:290
  77.9 1.1 collective-permute-start.10
  79.0 1.0 collective-permute-start.11
  80.0 1.2 collective-permute-done.6
  81.1 1.5 %collective-permute-start.7 = (f32[24,128]{1,0:T(8,128)S(1)}, f32[24,128]{1,0:T(8,128)S(1)}, u32[]{:S(2)}, u32[]{:S(2)}) collective-permute-start(f32[24,128]{1,0:T(8,128)S(1)} %add.65.own), channel_id=1, source_target_pairs={{0,2},{1,3},{2,4},{3,5},{4,6},{5,7},{6,0},{7,1},{8,10},{9,11},{10,... | collective-permute-start | bytes 36872 | tf_op jit(solution)/shard_map/ppermute | solution.py:377
  82.6 1.7 %collective-permute-start.8 = (f32[24,128]{1,0:T(8,128)S(1)}, f32[24,128]{1,0:T(8,128)S(1)}, u32[]{:S(2)}, u32[]{:S(2)}) collective-permute-start(f32[24,128]{1,0:T(8,128)S(1)} %add.65.own), channel_id=1, source_target_pairs={{0,6},{1,7},{2,0},{3,1},{4,2},{5,3},{6,4},{7,5},{8,14},{9,15},{10,... | collective-permute-start | bytes 36872 | tf_op jit(solution)/shard_map/ppermute | solution.py:377
  84.4 1.8 %collective-permute-start.9 = (f32[24,128]{1,0:T(8,128)S(1)}, f32[24,128]{1,0:T(8,128)S(1)}, u32[]{:S(2)}, u32[]{:S(2)}) collective-permute-start(f32[24,128]{1,0:T(8,128)S(1)} %add.65.own), channel_id=1, source_target_pairs={{0,4},{1,5},{2,6},{3,7},{4,0},{5,1},{6,2},{7,3},{8,12},{9,13},{10,... | collective-permute-start | bytes 36872 | tf_op jit(solution)/shard_map/ppermute | solution.py:377
  86.3 3.2 %collective-permute-done.9.across = f32[24,128]{1,0:T(8,128)S(1)} collective-permute-done((f32[24,128]{1,0:T(8,128)S(1)}, f32[24,128]{1,0:T(8,128)S(1)}, u32[]{:S(2)}, u32[]{:S(2)}) %collective-permute-start.9) | collective-permute-done | bytes 12320 | tf_op jit(solution)/shard_map/ppermute | solution.py:377
  89.6 0.7 shard_map.113
  90.3 4.2 %all-to-all-start.2 = ((bf16[8,48,128]{2,1,0:T(8,128)(2,1)}), bf16[8,48,128]{2,1,0:T(8,128)(2,1)S(1)}, u32[]{:S(2)}, u32[]{:S(2)}) async-start(bf16[8,48,128]{2,1,0:T(8,128)(2,1)} %bitcast.12), calls=%async_computation.2 | async-start | bytes 196608 | tf_op jit(solution)/shard_map/all_to_all | solution.py:363
  94.5 7.3 %all-to-all-done.2 = bf16[8,48,128]{2,1,0:T(8,128)(2,1)S(1)} async-done(((bf16[8,48,128]{2,1,0:T(8,128)(2,1)}), bf16[8,48,128]{2,1,0:T(8,128)(2,1)S(1)}, u32[]{:S(2)}, u32[]{:S(2)}) %all-to-all-start.2) | async-done | bytes 98336 | tf_op jit(solution)/shard_map/all_to_all | solution.py:363
  101.8 0.8 copy-done.4
  102.8 4.2 %shard_map.114 = bf16[384,512]{1,0:T(8,128)(2,1)S(1)} custom-call(s32[1,1]{1,0:T(1,128)} %bitcast.place, bf16[384,128]{1,0:T(8,128)(2,1)S(1)} %bitcast.26, bf16[1024,512]{1,0:T(8,128)(2,1)} %refs_0_.1, bf16[1024,512]{1,0:T(8,128)(2,1)} %copy-done.2, bf16[1024,512]{1,0:T(8,128)(2,1)} %collective-permute-done.5.behind.refs_2_, bf16[512,512]{1,0:T(8,128)(2,1)} %copy-done.4, ...), custom_call_target="tpu_custom_call" | custom-call | tf_op jit(solution)/shard_map/pallas_call | solution.py:301
  106.9 14.9 %all_to_all.45 = bf16[8,48,512]{2,1,0:T(8,128)(2,1)S(1)} all-to-all(bf16[8,48,512]{2,1,0:T(8,128)(2,1)S(1)} %bitcast.23), channel_id=1, replica_groups={{0,8,16,24,32,40,48,56},{64,72,80,88,96,104,112,120},{128,136,144,152,1..., dimensions={0} | all-to-all | bytes 786432 | tf_op jit(solution)/shard_map/all_to_all | solution.py:363
  (28 shorter events, 1.5 us)
Async XLA Ops:
  4.0 51.6 %all-to-all-start = ((bf16[32,8,3200]{2,1,0:T(8,128)(2,1)}), bf16[32,8,3200]{2,1,0:T(8,128)(2,1)S(1)}, u32[]{:S(2)}, u32[]{:S(2)}) async-start(bf16[32,8,3200]{2,1,0:T(8,128)(2,1)} %bitcast.6), calls=%async_computation | async-start | bytes 3276800 | tf_op jit(solution)/shard_map/all_to_all | solution.py:363
  15.4 19.5 %copy-start = (s32[48,4]{0,1:T(4,128)S(1)}, s32[48,4]{0,1:T(4,128)}, u32[]{:S(2)}) copy-start(s32[48,4]{0,1:T(4,128)} %param.20) | copy-start | bytes 2308
  15.4 19.5 %copy-start.1 = (f32[48,4]{0,1:T(4,128)S(1)}, f32[48,4]{0,1:T(4,128)}, u32[]{:S(2)}) copy-start(f32[48,4]{0,1:T(4,128)} %param.21) | copy-start | bytes 2308
  24.2 0.8 copy-start.3
  25.0 2.7 %collective-permute-start = (bf16[48,4,512]{2,1,0:T(4,128)(2,1)}, bf16[48,4,512]{2,1,0:T(4,128)(2,1)S(1)}, u32[]{:S(2)}, u32[]{:S(2)}) collective-permute-start(bf16[48,4,512]{2,1,0:T(4,128)(2,1)} %fusion), channel_id=1, source_target_pairs={{0,1},{1,0},{2,3},{3,2},{4,5},{5,4},{6,7},{7,6},{8,9},{9,8},{10,11... | collective-permute-start | bytes 589832 | tf_op jit(solution)/shard_map/ppermute | solution.py:377
  25.0 41.8 %collective-permute-start.4 = (bf16[1024,512]{1,0:T(8,128)(2,1)}, bf16[1024,512]{1,0:T(8,128)(2,1)S(1)}, u32[]{:S(2)}, u32[]{:S(2)}) collective-permute-start(bf16[1024,512]{1,0:T(8,128)(2,1)} %refs_0_.1), channel_id=1, source_target_pairs={{0,192},{8,200},{16,208},{24,216},{32,224},{40,232},{48,240},{56,2... | collective-permute-start | bytes 3145736 | tf_op jit(solution)/shard_map/ppermute | solution.py:370
  27.8 39.1 %collective-permute-start.5 = (bf16[1024,512]{1,0:T(8,128)(2,1)}, bf16[1024,512]{1,0:T(8,128)(2,1)}, u32[]{:S(2)}, u32[]{:S(2)}) collective-permute-start(bf16[1024,512]{1,0:T(8,128)(2,1)} %refs_0_.1), channel_id=1, source_target_pairs={{0,64},{8,72},{16,80},{24,88},{32,96},{40,104},{48,112},{56,120},{... | collective-permute-start | bytes 3145736 | tf_op jit(solution)/shard_map/ppermute | solution.py:370
  29.2 6.0 %collective-permute-start.1 = (bf16[48,512]{1,0:T(8,128)(2,1)S(1)}, bf16[48,512]{1,0:T(8,128)(2,1)S(1)}, u32[]{:S(2)}, u32[]{:S(2)}) collective-permute-start(bf16[48,512]{1,0:T(8,128)(2,1)S(1)} %get-tuple-element.31), channel_id=1, source_target_pairs={{0,2},{1,3},{2,4},{3,5},{4,6},{5,7},{6,0},{7,1},{8,10},{9,11},{10,... | collective-permute-start | bytes 147464 | tf_op jit(solution)/shard_map/ppermute | solution.py:377
  30.8 5.6 %collective-permute-start.2 = (bf16[48,512]{1,0:T(8,128)(2,1)S(1)}, bf16[48,512]{1,0:T(8,128)(2,1)S(1)}, u32[]{:S(2)}, u32[]{:S(2)}) collective-permute-start(bf16[48,512]{1,0:T(8,128)(2,1)S(1)} %get-tuple-element.33), channel_id=1, source_target_pairs={{0,4},{1,5},{2,6},{3,7},{4,0},{5,1},{6,2},{7,3},{8,12},{9,13},{10,... | collective-permute-start | bytes 147464 | tf_op jit(solution)/shard_map/ppermute | solution.py:377
  33.5 4.2 %collective-permute-start.3 = (bf16[48,512]{1,0:T(8,128)(2,1)S(1)}, bf16[48,512]{1,0:T(8,128)(2,1)}, u32[]{:S(2)}, u32[]{:S(2)}) collective-permute-start(bf16[48,512]{1,0:T(8,128)(2,1)S(1)} %get-tuple-element.32), channel_id=1, source_target_pairs={{0,6},{1,7},{2,0},{3,1},{4,2},{5,3},{6,4},{7,5},{8,14},{9,15},{10,... | collective-permute-start | bytes 147464 | tf_op jit(solution)/shard_map/ppermute | solution.py:377
  60.7 15.9 %all-to-all-start.1 = ((bf16[32,8,256]{2,1,0:T(8,128)(2,1)}), bf16[32,8,256]{2,1,0:T(8,128)(2,1)S(1)}, u32[]{:S(2)}, u32[]{:S(2)}) async-start(bf16[32,8,256]{2,1,0:T(8,128)(2,1)} %bitcast.10), calls=%async_computation.1 | async-start | bytes 262144 | tf_op jit(solution)/shard_map/all_to_all | solution.py:363
  66.9 9.7 %copy-start.2 = (bf16[1024,512]{1,0:T(8,128)(2,1)}, bf16[1024,512]{1,0:T(8,128)(2,1)S(1)}, u32[]{:S(2)}) copy-start(bf16[1024,512]{1,0:T(8,128)(2,1)S(1)} %collective-permute-done.4.ahead.refs_1_) | copy-start | bytes 3145732
  77.9 23.9 %collective-permute-start.10 = (bf16[512,512]{1,0:T(8,128)(2,1)S(1)}, bf16[512,512]{1,0:T(8,128)(2,1)S(1)}, u32[]{:S(2)}, u32[]{:S(2)}) collective-permute-start(bf16[512,512]{1,0:T(8,128)(2,1)S(1)} %get-tuple-element.26), channel_id=1, source_target_pairs={{0,192},{8,200},{16,208},{24,216},{32,224},{40,232},{48,240},{56,2... | collective-permute-start | bytes 1572872 | tf_op jit(solution)/shard_map/ppermute | solution.py:370
  79.0 22.8 %collective-permute-start.11 = (bf16[512,512]{1,0:T(8,128)(2,1)S(1)}, bf16[512,512]{1,0:T(8,128)(2,1)S(1)}, u32[]{:S(2)}, u32[]{:S(2)}) collective-permute-start(bf16[512,512]{1,0:T(8,128)(2,1)S(1)} %get-tuple-element.27), channel_id=1, source_target_pairs={{0,64},{8,72},{16,80},{24,88},{32,96},{40,104},{48,112},{56,120},{... | collective-permute-start | bytes 1572872 | tf_op jit(solution)/shard_map/ppermute | solution.py:370
  80.0 1.2 collective-permute-start.6
  81.1 5.1 %collective-permute-start.7 = (f32[24,128]{1,0:T(8,128)S(1)}, f32[24,128]{1,0:T(8,128)S(1)}, u32[]{:S(2)}, u32[]{:S(2)}) collective-permute-start(f32[24,128]{1,0:T(8,128)S(1)} %add.65.own), channel_id=1, source_target_pairs={{0,2},{1,3},{2,4},{3,5},{4,6},{5,7},{6,0},{7,1},{8,10},{9,11},{10,... | collective-permute-start | bytes 36872 | tf_op jit(solution)/shard_map/ppermute | solution.py:377
  82.6 3.7 %collective-permute-start.8 = (f32[24,128]{1,0:T(8,128)S(1)}, f32[24,128]{1,0:T(8,128)S(1)}, u32[]{:S(2)}, u32[]{:S(2)}) collective-permute-start(f32[24,128]{1,0:T(8,128)S(1)} %add.65.own), channel_id=1, source_target_pairs={{0,6},{1,7},{2,0},{3,1},{4,2},{5,3},{6,4},{7,5},{8,14},{9,15},{10,... | collective-permute-start | bytes 36872 | tf_op jit(solution)/shard_map/ppermute | solution.py:377
  84.4 5.2 %collective-permute-start.9 = (f32[24,128]{1,0:T(8,128)S(1)}, f32[24,128]{1,0:T(8,128)S(1)}, u32[]{:S(2)}, u32[]{:S(2)}) collective-permute-start(f32[24,128]{1,0:T(8,128)S(1)} %add.65.own), channel_id=1, source_target_pairs={{0,4},{1,5},{2,6},{3,7},{4,0},{5,1},{6,2},{7,3},{8,12},{9,13},{10,... | collective-permute-start | bytes 36872 | tf_op jit(solution)/shard_map/ppermute | solution.py:377
  90.3 11.5 %all-to-all-start.2 = ((bf16[8,48,128]{2,1,0:T(8,128)(2,1)}), bf16[8,48,128]{2,1,0:T(8,128)(2,1)S(1)}, u32[]{:S(2)}, u32[]{:S(2)}) async-start(bf16[8,48,128]{2,1,0:T(8,128)(2,1)} %bitcast.12), calls=%async_computation.2 | async-start | bytes 196608 | tf_op jit(solution)/shard_map/all_to_all | solution.py:363
  101.8 0.8 copy-start.4
  101.8 1.0 copy-start.5

commit v5 on v4

--- a/solution.py
+++ b/solution.py
@@ -197,7 +197,7 @@
         picks[pl.ds(g * ROWS, ROWS), :] = (place == spot + g * PART).astype(BF)
 
 
-def home_kernel(got, picks, ahead, behind, out, far_low, far_high, sems):
+def split_kernel(ahead, behind, far_low, far_high, sems):
     half = far_low.shape[0]
     copies = [
         pltpu.make_async_copy(ahead.at[pl.ds(0, half), :], far_low, sems.at[0]),
@@ -205,6 +205,11 @@
     ]
     for copy in copies:
         copy.start()
+    for copy in copies:
+        copy.wait()
+
+
+def home_kernel(got, picks, out):
     lane = iota((ROWS, 256), 1)
     total = jnp.zeros((ROWS, 256), F32)
     for g in range(PARTS):
@@ -212,11 +217,9 @@
         total = total + jnp.where((lane >> 6) == g, part, 0.0)
     folded = total[:, :128] + total[:, 128:]
     folded = folded + pltpu.roll(folded, RANK, 1)
-    few = ROWS // 2
-    lane = iota((few, 128), 1)
-    out[...] = jnp.where(lane < RANK, folded[:few, :], folded[few:, :])
-    for copy in copies:
-        copy.wait()
+    half = ROWS // 2
+    lane = iota((half, 128), 1)
+    out[...] = jnp.where(lane < RANK, folded[:half, :], folded[half:, :])
 
 
 def mix_kernel(own, ahead, behind, across, record, out):
@@ -284,17 +287,17 @@
     out[...] = total.astype(BF)
 
 
-def home(got, picks, ahead, behind):
+def split(ahead, behind):
     half = shape_of(ahead.shape[0] // 2, ahead.shape[1])
-    vmem, hbm = (pl.BlockSpec(memory_space=space) for space in (pltpu.VMEM, pltpu.HBM))
+    hbm = pl.BlockSpec(memory_space=pltpu.HBM)
     return pl.pallas_call(
-        home_kernel,
-        out_shape=(shape_of(ROWS // 2, 128, dtype=F32), half, half),
-        in_specs=[vmem, vmem, hbm, hbm],
-        out_specs=(vmem, hbm, hbm),
+        split_kernel,
+        out_shape=(half, half),
+        in_specs=[hbm, hbm],
+        out_specs=(hbm, hbm),
         scratch_shapes=[pltpu.SemaphoreType.DMA((2,))],
         compiler_params=pltpu.CompilerParams(vmem_limit_bytes=24 * 1024 * 1024),
-    )(got, picks, *[pltpu.with_memory_space_constraint(x, pltpu.HBM) for x in (ahead, behind)])
+    )(*[pltpu.with_memory_space_constraint(x, pltpu.HBM) for x in (ahead, behind)])
 
 
 def lift(place, got, ups):
@@ -302,13 +305,14 @@
         raise_kernel,
         out_shape=shape_of(DEPTH * ROWS, COLS),
         in_specs=[pl.BlockSpec(memory_space=pltpu.SMEM), pl.BlockSpec(memory_space=pltpu.VMEM)]
-        + [pl.BlockSpec(memory_space=pltpu.HBM)] * len(ups),
+        + [pl.BlockSpec(memory_space=pltpu.HBM)] * 3
+        + [pl.BlockSpec(memory_space=pl.ANY)] * 2,
         scratch_shapes=[
             pltpu.VMEM((SIDES, *ups[0].shape), BF),
             pltpu.SemaphoreType.DMA((len(ups),)),
         ],
         compiler_params=pltpu.CompilerParams(vmem_limit_bytes=32 * 1024 * 1024),
-    )(place, got, *[pltpu.with_memory_space_constraint(up, pltpu.HBM) for up in ups])
+    )(place, got, *[pltpu.with_memory_space_constraint(up, pltpu.HBM) for up in ups[:3]], *ups[3:])
 
 
 def attend(*args):
@@ -431,10 +435,13 @@
     got, frozen, picks, record = lax.optimization_barrier((got, frozen, picks, record))
     lowered = lower(got, adapter_down)
     lowered = swap(lowered, "adapter")
-    share, far_low, far_high = home(lowered, picks, ahead, behind)
+    far_low, far_high = split(ahead, behind)
+    lowered, far_low, far_high = lax.optimization_barrier((lowered, far_low, far_high))
+    share = call(home_kernel, shape_of(ROWS // 2, 128, dtype=F32), lowered, picks)
+    share = share + turn(share, 0, 1)
+    share, far_low, far_high = lax.optimization_barrier((share, far_low, far_high))
+    shares = [turn(share, step, 0) for step in (1, CHIPS - 1, 2)]
     ups = (adapter_up, ahead, behind, beside(far_low, 1), beside(far_high, SIDES - 1))
-    share = share + turn(share, 0, 1)
-    shares = [turn(share, step, 0) for step in (1, CHIPS - 1, 2)]
     mixed = call(mix_kernel, shape_of(DEPTH * ROWS, 128), share, *shares, record)
     mixed = swap(mixed, "adapter", COLUMNS)
     place = lax.axis_index("adapter").reshape(1, 1)

time: 124 us -> 121 us (0.976)
  waiting for transfers between devices: 41.2 us -> 39.1 us
    all_to_all x3, waiting for transfers between devices: 34.2 us -> 32 us  [swap(): lax.all_to_all(x, axis, split_axis=0, concat_axis=0, axis_index_groups=gr...]
  transfers between devices with their start and end apart: 15 -> 15, of which waited for: 8 -> 8; matrix products, arithmetic and copies ran while one was open for 10% -> 10% of each run, Pallas kernels for 5% -> 6%
where the time goes in v5:
time: 121 us; the launch traced here: 120 us
  waiting for transfers between devices  39.1 us (32%)
  starting transfers between devices  37.3 us (31%)
  Pallas kernels  16.3 us (13%)
  blocking collectives  14.1 us (12%)
  matrix products  4.95 us (4%)
  local copies, waits for them, and re-layouts  4.9 us (4%)
  other arithmetic  2.91 us (2%)
    all_to_all x3, waiting for transfers between devices, swap(): lax.all_to_all(x, axis, split_axis=0, concat_axis=0, axis_index_groups=gr...  32 us
    all_to_all x3, starting transfers between devices, swap(): lax.all_to_all(x, axis, split_axis=0, concat_axis=0, axis_index_groups=gr...  21.8 us
    all_to_all x1, blocking collectives, swap(): lax.all_to_all(x, axis, split_axis=0, concat_axis=0, axis_index_groups=gr...  14.1 us
    ppermute x8, starting transfers between devices, turn(): return lax.ppermute(x, 'tensor', pairs)  10.8 us
    ppermute x8, waiting for transfers between devices, turn(): return lax.ppermute(x, 'tensor', pairs)  7.05 us
    pallas_call x1, Pallas kernels, lower(): pl.pallas_call(lower_kernel, out_shape=shape_of(LINES, 256), in_specs=[pl...  5.01 us
    dot_general x1, matrix products, frozen_sum(): part = jnp.dot(attended, out_weight, preferred_element_type=F32)  4.95 us
    ppermute x4, starting transfers between devices, beside(): return lax.ppermute(x, 'adapter', pairs)  4.75 us
  transfers between devices with their start and end apart: 15, of which 8 were waited for; matrix products, arithmetic and copies ran while one was open for 10% of the time, Pallas kernels for 6%

profile of v5, /device:TPU:32, one launch (start us, length us, event | category | flops | bytes accessed | tf_op | source)
XLA Modules:
  0.0 119.7 jit_solution(7121696506901270900)
XLA Ops:
  0.0 4.0 %shard_map.109 = (bf16[48,1024]{1,0:T(8,128)(2,1)S(1)}, bf16[256,3200]{1,0:T(8,128)(2,1)}) custom-call(bf16[48,1024]{1,0:T(8,128)(2,1)} %q_hbm.1, bf16[1536,128]{1,0:T(8,128)(2,1)} %bitcast.34, bf16[1536,128]{1,0:T(8,128)(2,1)} %bitcast.35, bf16[48,128]{1,0:T(8,128)(2,1)} %nk_hbm.1, bf16[48,128]{1,0:T(8,128)(2,1)} %nv_hbm.1, s32[1,48]{1,0:T(1,128)} %bitcast.36, ...), custom_call_target="tpu_custom_call" | custom-call | tf_op jit(solution)/shard_map/pallas_call | solution.py:319
  4.0 11.4 %all-to-all-start = ((bf16[32,8,3200]{2,1,0:T(8,128)(2,1)}), bf16[32,8,3200]{2,1,0:T(8,128)(2,1)S(1)}, u32[]{:S(2)}, u32[]{:S(2)}) async-start(bf16[32,8,3200]{2,1,0:T(8,128)(2,1)} %bitcast.6), calls=%async_computation | async-start | bytes 3276800 | tf_op jit(solution)/shard_map/all_to_all | solution.py:367
  15.4 5.0 %fusion.2 = f32[48,4096]{1,0:T(8,128)S(1)} fusion(bf16[48,1024]{1,0:T(8,128)(2,1)S(1)} %get-tuple-element.23.after, bf16[1024,4096]{1,0:T(8,128)(2,1)} %param.17), kind=kOutput, calls=%fused_computation.8 | convolution fusion | flops 402653184 | bytes 9273344 | tf_op jit(solution)/shard_map/dot_general | solution.py:387
  20.4 1.6 %reshape.35 = f32[48,4,2,512]{3,2,1,0:T(2,128)} reshape(f32[48,4096]{1,0:T(8,128)S(1)} %fusion.2) | data formatting | bytes 1572864 | tf_op jit(solution)/shard_map/reshape | solution.py:388
  21.9 2.2 %fusion.1 = (f32[48,4,1,512]{3,2,1,0:T(1,128)S(1)}, f32[48,4,1,512]{3,2,1,0:T(1,128)S(1)}) fusion(f32[48,4,2,512]{3,2,1,0:T(2,128)} %reshape.35), kind=kLoop, calls=%fused_computation.7 | loop fusion | bytes 1572864 | tf_op jit(solution)/shard_map/slice | solution.py:389
  24.1 0.8 fusion
  25.0 2.7 %collective-permute-start.4 = (bf16[1024,512]{1,0:T(8,128)(2,1)}, bf16[1024,512]{1,0:T(8,128)(2,1)S(1)}, u32[]{:S(2)}, u32[]{:S(2)}) collective-permute-start(bf16[1024,512]{1,0:T(8,128)(2,1)} %refs_0_.1), channel_id=1, source_target_pairs={{0,192},{8,200},{16,208},{24,216},{32,224},{40,232},{48,240},{56,2... | collective-permute-start | bytes 3145736 | tf_op jit(solution)/shard_map/ppermute | solution.py:374
  27.7 1.2 %bitcast_add_fusion = f32[48,4,512]{2,1,0:T(4,128)S(1)} fusion(bf16[48,4,512]{2,1,0:T(4,128)(2,1)S(1)} %collective-permute-done, f32[48,4,1,512]{3,2,1,0:T(1,128)S(1)} %get-tuple-element.39, f32[48,4,1,512]{3,2,1,0:T(1,128)} %copy-done.3, pred[]{:T(512)S(6)} %eq.9), kind=kLoop, calls=%fused_computation | loop fusion | flops 294912 | bytes 1376257 | tf_op jit(solution)/shard_map/add | solution.py:392
  29.1 1.6 %collective-permute-start.1 = (bf16[48,512]{1,0:T(8,128)(2,1)S(1)}, bf16[48,512]{1,0:T(8,128)(2,1)S(1)}, u32[]{:S(2)}, u32[]{:S(2)}) collective-permute-start(bf16[48,512]{1,0:T(8,128)(2,1)S(1)} %get-tuple-element.41), channel_id=1, source_target_pairs={{0,2},{1,3},{2,4},{3,5},{4,6},{5,7},{6,0},{7,1},{8,10},{9,11},{10,... | collective-permute-start | bytes 147464 | tf_op jit(solution)/shard_map/ppermute | solution.py:381
  30.7 2.7 %collective-permute-start.2 = (bf16[48,512]{1,0:T(8,128)(2,1)S(1)}, bf16[48,512]{1,0:T(8,128)(2,1)S(1)}, u32[]{:S(2)}, u32[]{:S(2)}) collective-permute-start(bf16[48,512]{1,0:T(8,128)(2,1)S(1)} %get-tuple-element.43), channel_id=1, source_target_pairs={{0,4},{1,5},{2,6},{3,7},{4,0},{5,1},{6,2},{7,3},{8,12},{9,13},{10,... | collective-permute-start | bytes 147464 | tf_op jit(solution)/shard_map/ppermute | solution.py:381
  33.4 1.4 %collective-permute-start.3 = (bf16[48,512]{1,0:T(8,128)(2,1)S(1)}, bf16[48,512]{1,0:T(8,128)(2,1)}, u32[]{:S(2)}, u32[]{:S(2)}) collective-permute-start(bf16[48,512]{1,0:T(8,128)(2,1)S(1)} %get-tuple-element.42), channel_id=1, source_target_pairs={{0,6},{1,7},{2,0},{3,1},{4,2},{5,3},{6,4},{7,5},{8,14},{9,15},{10,... | collective-permute-start | bytes 147464 | tf_op jit(solution)/shard_map/ppermute | solution.py:381
  35.1 1.2 collective-permute-done.2
  36.3 1.3 %collective-permute-done.3 = bf16[48,512]{1,0:T(8,128)(2,1)} collective-permute-done((bf16[48,512]{1,0:T(8,128)(2,1)S(1)}, bf16[48,512]{1,0:T(8,128)(2,1)}, u32[]{:S(2)}, u32[]{:S(2)}) %collective-permute-start.3) | collective-permute-done | bytes 49184 | tf_op jit(solution)/shard_map/ppermute | solution.py:381
  37.6 0.8 convert_add_fusion.frozen
  38.4 17.2 %all-to-all-done = bf16[32,8,3200]{2,1,0:T(8,128)(2,1)S(1)} async-done(((bf16[32,8,3200]{2,1,0:T(8,128)(2,1)}), bf16[32,8,3200]{2,1,0:T(8,128)(2,1)S(1)}, u32[]{:S(2)}, u32[]{:S(2)}) %all-to-all-start) | async-done | bytes 1638432 | tf_op jit(solution)/shard_map/all_to_all | solution.py:367
  55.6 5.0 %shard_map.111 = bf16[256,256]{1,0:T(8,128)(2,1)} custom-call(bf16[256,3200]{1,0:T(8,128)(2,1)S(1)} %bitcast.22, bf16[1024,1024]{1,0:T(8,128)(2,1)} %down.1), custom_call_target="tpu_custom_call" | custom-call | tf_op jit(solution)/shard_map/pallas_call | solution.py:342
  60.7 6.2 %all-to-all-start.1 = ((bf16[32,8,256]{2,1,0:T(8,128)(2,1)}), bf16[32,8,256]{2,1,0:T(8,128)(2,1)S(1)}, u32[]{:S(2)}, u32[]{:S(2)}) async-start(bf16[32,8,256]{2,1,0:T(8,128)(2,1)} %bitcast.10), calls=%async_computation.1 | async-start | bytes 262144 | tf_op jit(solution)/shard_map/all_to_all | solution.py:367
  66.9 1.0 copy-done.2
  67.9 1.2 %shard_map.112 = (bf16[512,512]{1,0:T(8,128)(2,1)S(1)}, bf16[512,512]{1,0:T(8,128)(2,1)S(1)}) custom-call(bf16[1024,512]{1,0:T(8,128)(2,1)} %copy-done.2, bf16[1024,512]{1,0:T(8,128)(2,1)} %collective-permute-done.5.behind.refs_2_), custom_call_target="tpu_custom_call" | custom-call | tf_op jit(solution)/shard_map/pallas_call | solution.py:293
  69.1 7.5 %all-to-all-done.1 = bf16[32,8,256]{2,1,0:T(8,128)(2,1)S(1)} async-done(((bf16[32,8,256]{2,1,0:T(8,128)(2,1)}), bf16[32,8,256]{2,1,0:T(8,128)(2,1)S(1)}, u32[]{:S(2)}, u32[]{:S(2)}) %all-to-all-start.1) | async-done | bytes 131104 | tf_op jit(solution)/shard_map/all_to_all | solution.py:367
  76.9 1.2 collective-permute-done.6
  78.1 1.1 collective-permute-start.10
  79.2 1.0 collective-permute-start.11
  80.1 1.5 %collective-permute-start.7 = (f32[24,128]{1,0:T(8,128)S(1)}, f32[24,128]{1,0:T(8,128)S(1)}, u32[]{:S(2)}, u32[]{:S(2)}) collective-permute-start(f32[24,128]{1,0:T(8,128)S(1)} %add.65.own), channel_id=1, source_target_pairs={{0,2},{1,3},{2,4},{3,5},{4,6},{5,7},{6,0},{7,1},{8,10},{9,11},{10,... | collective-permute-start | bytes 36872 | tf_op jit(solution)/shard_map/ppermute | solution.py:381
  81.6 1.8 %collective-permute-start.8 = (f32[24,128]{1,0:T(8,128)S(1)}, f32[24,128]{1,0:T(8,128)S(1)}, u32[]{:S(2)}, u32[]{:S(2)}) collective-permute-start(f32[24,128]{1,0:T(8,128)S(1)} %add.65.own), channel_id=1, source_target_pairs={{0,6},{1,7},{2,0},{3,1},{4,2},{5,3},{6,4},{7,5},{8,14},{9,15},{10,... | collective-permute-start | bytes 36872 | tf_op jit(solution)/shard_map/ppermute | solution.py:381
  83.4 1.8 %collective-permute-start.9 = (f32[24,128]{1,0:T(8,128)S(1)}, f32[24,128]{1,0:T(8,128)S(1)}, u32[]{:S(2)}, u32[]{:S(2)}) collective-permute-start(f32[24,128]{1,0:T(8,128)S(1)} %add.65.own), channel_id=1, source_target_pairs={{0,4},{1,5},{2,6},{3,7},{4,0},{5,1},{6,2},{7,3},{8,12},{9,13},{10,... | collective-permute-start | bytes 36872 | tf_op jit(solution)/shard_map/ppermute | solution.py:381
  85.3 3.3 %collective-permute-done.9.across = f32[24,128]{1,0:T(8,128)S(1)} collective-permute-done((f32[24,128]{1,0:T(8,128)S(1)}, f32[24,128]{1,0:T(8,128)S(1)}, u32[]{:S(2)}, u32[]{:S(2)}) %collective-permute-start.9) | collective-permute-done | bytes 12320 | tf_op jit(solution)/shard_map/ppermute | solution.py:381
  88.6 0.7 shard_map.114
  89.3 4.2 %all-to-all-start.2 = ((bf16[8,48,128]{2,1,0:T(8,128)(2,1)}), bf16[8,48,128]{2,1,0:T(8,128)(2,1)S(1)}, u32[]{:S(2)}, u32[]{:S(2)}) async-start(bf16[8,48,128]{2,1,0:T(8,128)(2,1)} %bitcast.12), calls=%async_computation.2 | async-start | bytes 196608 | tf_op jit(solution)/shard_map/all_to_all | solution.py:367
  93.5 7.3 %all-to-all-done.2 = bf16[8,48,128]{2,1,0:T(8,128)(2,1)S(1)} async-done(((bf16[8,48,128]{2,1,0:T(8,128)(2,1)}), bf16[8,48,128]{2,1,0:T(8,128)(2,1)S(1)}, u32[]{:S(2)}, u32[]{:S(2)}) %all-to-all-start.2) | async-done | bytes 98336 | tf_op jit(solution)/shard_map/all_to_all | solution.py:367
  100.8 4.2 %shard_map.115 = bf16[384,512]{1,0:T(8,128)(2,1)S(1)} custom-call(s32[1,1]{1,0:T(1,128)} %bitcast.place, bf16[384,128]{1,0:T(8,128)(2,1)S(1)} %bitcast.26, bf16[1024,512]{1,0:T(8,128)(2,1)} %refs_0_.1, bf16[1024,512]{1,0:T(8,128)(2,1)} %copy-done.2, bf16[1024,512]{1,0:T(8,128)(2,1)} %collective-permute-done.5.behind.refs_2_, ...), custom_call_target="tpu_custom_call" | custom-call | tf_op jit(solution)/shard_map/pallas_call | solution.py:304
  105.0 14.1 %all_to_all.46 = bf16[8,48,512]{2,1,0:T(8,128)(2,1)S(1)} all-to-all(bf16[8,48,512]{2,1,0:T(8,128)(2,1)S(1)} %bitcast.23), channel_id=1, replica_groups={{0,8,16,24,32,40,48,56},{64,72,80,88,96,104,112,120},{128,136,144,152,1..., dimensions={0} | all-to-all | bytes 786432 | tf_op jit(solution)/shard_map/all_to_all | solution.py:367
  (25 shorter events, 1.6 us)
Async XLA Ops:
  4.0 51.6 %all-to-all-start = ((bf16[32,8,3200]{2,1,0:T(8,128)(2,1)}), bf16[32,8,3200]{2,1,0:T(8,128)(2,1)S(1)}, u32[]{:S(2)}, u32[]{:S(2)}) async-start(bf16[32,8,3200]{2,1,0:T(8,128)(2,1)} %bitcast.6), calls=%async_computation | async-start | bytes 3276800 | tf_op jit(solution)/shard_map/all_to_all | solution.py:367
  15.4 19.5 %copy-start = (s32[48,4]{0,1:T(4,128)S(1)}, s32[48,4]{0,1:T(4,128)}, u32[]{:S(2)}) copy-start(s32[48,4]{0,1:T(4,128)} %param.20) | copy-start | bytes 2308
  15.4 19.5 %copy-start.1 = (f32[48,4]{0,1:T(4,128)S(1)}, f32[48,4]{0,1:T(4,128)}, u32[]{:S(2)}) copy-start(f32[48,4]{0,1:T(4,128)} %param.21) | copy-start | bytes 2308
  24.1 0.9 copy-start.3
  25.0 2.7 %collective-permute-start = (bf16[48,4,512]{2,1,0:T(4,128)(2,1)}, bf16[48,4,512]{2,1,0:T(4,128)(2,1)S(1)}, u32[]{:S(2)}, u32[]{:S(2)}) collective-permute-start(bf16[48,4,512]{2,1,0:T(4,128)(2,1)} %fusion), channel_id=1, source_target_pairs={{0,1},{1,0},{2,3},{3,2},{4,5},{5,4},{6,7},{7,6},{8,9},{9,8},{10,11... | collective-permute-start | bytes 589832 | tf_op jit(solution)/shard_map/ppermute | solution.py:381
  25.0 41.9 %collective-permute-start.4 = (bf16[1024,512]{1,0:T(8,128)(2,1)}, bf16[1024,512]{1,0:T(8,128)(2,1)S(1)}, u32[]{:S(2)}, u32[]{:S(2)}) collective-permute-start(bf16[1024,512]{1,0:T(8,128)(2,1)} %refs_0_.1), channel_id=1, source_target_pairs={{0,192},{8,200},{16,208},{24,216},{32,224},{40,232},{48,240},{56,2... | collective-permute-start | bytes 3145736 | tf_op jit(solution)/shard_map/ppermute | solution.py:374
  27.7 39.2 %collective-permute-start.5 = (bf16[1024,512]{1,0:T(8,128)(2,1)}, bf16[1024,512]{1,0:T(8,128)(2,1)}, u32[]{:S(2)}, u32[]{:S(2)}) collective-permute-start(bf16[1024,512]{1,0:T(8,128)(2,1)} %refs_0_.1), channel_id=1, source_target_pairs={{0,64},{8,72},{16,80},{24,88},{32,96},{40,104},{48,112},{56,120},{... | collective-permute-start | bytes 3145736 | tf_op jit(solution)/shard_map/ppermute | solution.py:374
  29.1 6.0 %collective-permute-start.1 = (bf16[48,512]{1,0:T(8,128)(2,1)S(1)}, bf16[48,512]{1,0:T(8,128)(2,1)S(1)}, u32[]{:S(2)}, u32[]{:S(2)}) collective-permute-start(bf16[48,512]{1,0:T(8,128)(2,1)S(1)} %get-tuple-element.41), channel_id=1, source_target_pairs={{0,2},{1,3},{2,4},{3,5},{4,6},{5,7},{6,0},{7,1},{8,10},{9,11},{10,... | collective-permute-start | bytes 147464 | tf_op jit(solution)/shard_map/ppermute | solution.py:381
  30.7 5.6 %collective-permute-start.2 = (bf16[48,512]{1,0:T(8,128)(2,1)S(1)}, bf16[48,512]{1,0:T(8,128)(2,1)S(1)}, u32[]{:S(2)}, u32[]{:S(2)}) collective-permute-start(bf16[48,512]{1,0:T(8,128)(2,1)S(1)} %get-tuple-element.43), channel_id=1, source_target_pairs={{0,4},{1,5},{2,6},{3,7},{4,0},{5,1},{6,2},{7,3},{8,12},{9,13},{10,... | collective-permute-start | bytes 147464 | tf_op jit(solution)/shard_map/ppermute | solution.py:381
  33.4 4.2 %collective-permute-start.3 = (bf16[48,512]{1,0:T(8,128)(2,1)S(1)}, bf16[48,512]{1,0:T(8,128)(2,1)}, u32[]{:S(2)}, u32[]{:S(2)}) collective-permute-start(bf16[48,512]{1,0:T(8,128)(2,1)S(1)} %get-tuple-element.42), channel_id=1, source_target_pairs={{0,6},{1,7},{2,0},{3,1},{4,2},{5,3},{6,4},{7,5},{8,14},{9,15},{10,... | collective-permute-start | bytes 147464 | tf_op jit(solution)/shard_map/ppermute | solution.py:381
  60.7 16.0 %all-to-all-start.1 = ((bf16[32,8,256]{2,1,0:T(8,128)(2,1)}), bf16[32,8,256]{2,1,0:T(8,128)(2,1)S(1)}, u32[]{:S(2)}, u32[]{:S(2)}) async-start(bf16[32,8,256]{2,1,0:T(8,128)(2,1)} %bitcast.10), calls=%async_computation.1 | async-start | bytes 262144 | tf_op jit(solution)/shard_map/all_to_all | solution.py:367
  66.9 1.0 copy-start.2
  76.9 1.2 %collective-permute-start.6 = (f32[24,128]{1,0:T(8,128)S(1)}, f32[24,128]{1,0:T(8,128)S(1)}, u32[]{:S(2)}, u32[]{:S(2)}) collective-permute-start(f32[24,128]{1,0:T(8,128)S(1)} %shard_map.113), channel_id=1, source_target_pairs={{0,1},{1,0},{2,3},{3,2},{4,5},{5,4},{6,7},{7,6},{8,9},{9,8},{10,11... | collective-permute-start | bytes 36872 | tf_op jit(solution)/shard_map/ppermute | solution.py:381
  78.1 22.7 %collective-permute-start.10 = (bf16[512,512]{1,0:T(8,128)(2,1)S(1)}, bf16[512,512]{1,0:T(8,128)(2,1)S(1)}, u32[]{:S(2)}, u32[]{:S(2)}) collective-permute-start(bf16[512,512]{1,0:T(8,128)(2,1)S(1)} %get-tuple-element.36), channel_id=1, source_target_pairs={{0,192},{8,200},{16,208},{24,216},{32,224},{40,232},{48,240},{56,2... | collective-permute-start | bytes 1572872 | tf_op jit(solution)/shard_map/ppermute | solution.py:374
  79.2 21.6 %collective-permute-start.11 = (bf16[512,512]{1,0:T(8,128)(2,1)S(1)}, bf16[512,512]{1,0:T(8,128)(2,1)S(1)}, u32[]{:S(2)}, u32[]{:S(2)}) collective-permute-start(bf16[512,512]{1,0:T(8,128)(2,1)S(1)} %get-tuple-element.37), channel_id=1, source_target_pairs={{0,64},{8,72},{16,80},{24,88},{32,96},{40,104},{48,112},{56,120},{... | collective-permute-start | bytes 1572872 | tf_op jit(solution)/shard_map/ppermute | solution.py:374
  80.1 5.0 %collective-permute-start.7 = (f32[24,128]{1,0:T(8,128)S(1)}, f32[24,128]{1,0:T(8,128)S(1)}, u32[]{:S(2)}, u32[]{:S(2)}) collective-permute-start(f32[24,128]{1,0:T(8,128)S(1)} %add.65.own), channel_id=1, source_target_pairs={{0,2},{1,3},{2,4},{3,5},{4,6},{5,7},{6,0},{7,1},{8,10},{9,11},{10,... | collective-permute-start | bytes 36872 | tf_op jit(solution)/shard_map/ppermute | solution.py:381
  81.6 3.7 %collective-permute-start.8 = (f32[24,128]{1,0:T(8,128)S(1)}, f32[24,128]{1,0:T(8,128)S(1)}, u32[]{:S(2)}, u32[]{:S(2)}) collective-permute-start(f32[24,128]{1,0:T(8,128)S(1)} %add.65.own), channel_id=1, source_target_pairs={{0,6},{1,7},{2,0},{3,1},{4,2},{5,3},{6,4},{7,5},{8,14},{9,15},{10,... | collective-permute-start | bytes 36872 | tf_op jit(solution)/shard_map/ppermute | solution.py:381
  83.4 5.2 %collective-permute-start.9 = (f32[24,128]{1,0:T(8,128)S(1)}, f32[24,128]{1,0:T(8,128)S(1)}, u32[]{:S(2)}, u32[]{:S(2)}) collective-permute-start(f32[24,128]{1,0:T(8,128)S(1)} %add.65.own), channel_id=1, source_target_pairs={{0,4},{1,5},{2,6},{3,7},{4,0},{5,1},{6,2},{7,3},{8,12},{9,13},{10,... | collective-permute-start | bytes 36872 | tf_op jit(solution)/shard_map/ppermute | solution.py:381
  89.3 11.5 %all-to-all-start.2 = ((bf16[8,48,128]{2,1,0:T(8,128)(2,1)}), bf16[8,48,128]{2,1,0:T(8,128)(2,1)S(1)}, u32[]{:S(2)}, u32[]{:S(2)}) async-start(bf16[8,48,128]{2,1,0:T(8,128)(2,1)} %bitcast.12), calls=%async_computation.2 | async-start | bytes 196608 | tf_op jit(solution)/shard_map/all_to_all | solution.py:367

commit v6 on v5

--- a/solution.py
+++ b/solution.py
@@ -26,7 +26,7 @@
 TENSOR = 8
 CORES = 2
 CHIPS = 4
-DOWN_STEPS = 4
+DOWN_STEPS = 2
 DEPTH = 8
 SIDES = 4
 COLUMNS = [[y * DEPTH + z for z in range(DEPTH)] for y in range(SIDES)]
@@ -266,17 +266,14 @@
     shape = (128, ADP_DEV * RANK)
     line = iota(shape, 0) & (RANK - 1)
     adapter = iota(shape, 1) >> 6
-    total = jnp.zeros((rows, COLS), F32)
+    blocks = []
     for b in range(SIDES):
         coefs = dot(coef, (line == adapter + b * ADP_DEV).astype(BF))
-        expanded = jnp.concatenate(
-            [(coefs[:, p * 128 : (p + 1) * 128] * mixed).astype(BF) for p in range(ADP_DEV * RANK // 128)],
-            axis=1,
-        )
-        copies[b].wait()
-        if b == SIDES - 1:
-            copies[SIDES].wait()
-        total = total + dot(expanded, held[b])
+        for p in range(ADP_DEV * RANK // 128):
+            blocks.append((coefs[:, p * 128 : (p + 1) * 128] * mixed).astype(BF))
+    for copy in copies:
+        copy.wait()
+    total = dot(jnp.concatenate(blocks, axis=1), held[...].reshape(SIDES * ADP_DEV * RANK, COLS))
     out[...] = total.astype(BF)
 
 

time: 121 us -> 120 us (level)
  transfers between devices with their start and end apart: 15 -> 15, of which waited for: 8 -> 8; matrix products, arithmetic and copies ran while one was open for 10% -> 10% of each run, Pallas kernels for 6% -> 5%
where the time goes in v6:
time: 120 us; the launch traced here: 119 us
  waiting for transfers between devices  39.1 us (33%)
  starting transfers between devices  37.3 us (31%)
  Pallas kernels  15.1 us (13%)
  blocking collectives  14.1 us (12%)
  matrix products  4.95 us (4%)
  local copies, waits for them, and re-layouts  4.9 us (4%)
  other arithmetic  2.91 us (2%)
    all_to_all x3, waiting for transfers between devices, swap(): lax.all_to_all(x, axis, split_axis=0, concat_axis=0, axis_index_groups=gr...  32 us
    all_to_all x3, starting transfers between devices, swap(): lax.all_to_all(x, axis, split_axis=0, concat_axis=0, axis_index_groups=gr...  21.8 us
    all_to_all x1, blocking collectives, swap(): lax.all_to_all(x, axis, split_axis=0, concat_axis=0, axis_index_groups=gr...  14.1 us
    ppermute x8, starting transfers between devices, turn(): return lax.ppermute(x, 'tensor', pairs)  10.8 us
    ppermute x8, waiting for transfers between devices, turn(): return lax.ppermute(x, 'tensor', pairs)  7.04 us
    dot_general x1, matrix products, frozen_sum(): part = jnp.dot(attended, out_weight, preferred_element_type=F32)  4.95 us
    ppermute x4, starting transfers between devices, beside(): return lax.ppermute(x, 'adapter', pairs)  4.75 us
    pallas_call x1, Pallas kernels, lower(): pl.pallas_call(lower_kernel, out_shape=shape_of(LINES, 256), in_specs=[pl...  4.29 us
  transfers between devices with their start and end apart: 15, of which 8 were waited for; matrix products, arithmetic and copies ran while one was open for 10% of the time, Pallas kernels for 5%

profile of v6, /device:TPU:32, one launch (start us, length us, event | category | flops | bytes accessed | tf_op | source)
XLA Modules:
  0.0 118.5 jit_solution(8211328195498415962)
XLA Ops:
  0.0 4.0 %shard_map.109 = (bf16[48,1024]{1,0:T(8,128)(2,1)S(1)}, bf16[256,3200]{1,0:T(8,128)(2,1)}) custom-call(bf16[48,1024]{1,0:T(8,128)(2,1)} %q_hbm.1, bf16[1536,128]{1,0:T(8,128)(2,1)} %bitcast.34, bf16[1536,128]{1,0:T(8,128)(2,1)} %bitcast.35, bf16[48,128]{1,0:T(8,128)(2,1)} %nk_hbm.1, bf16[48,128]{1,0:T(8,128)(2,1)} %nv_hbm.1, s32[1,48]{1,0:T(1,128)} %bitcast.36, ...), custom_call_target="tpu_custom_call" | custom-call | tf_op jit(solution)/shard_map/pallas_call | solution.py:316
  4.0 11.4 %all-to-all-start = ((bf16[32,8,3200]{2,1,0:T(8,128)(2,1)}), bf16[32,8,3200]{2,1,0:T(8,128)(2,1)S(1)}, u32[]{:S(2)}, u32[]{:S(2)}) async-start(bf16[32,8,3200]{2,1,0:T(8,128)(2,1)} %bitcast.6), calls=%async_computation | async-start | bytes 3276800 | tf_op jit(solution)/shard_map/all_to_all | solution.py:364
  15.4 5.0 %fusion.2 = f32[48,4096]{1,0:T(8,128)S(1)} fusion(bf16[48,1024]{1,0:T(8,128)(2,1)S(1)} %get-tuple-element.23.after, bf16[1024,4096]{1,0:T(8,128)(2,1)} %param.17), kind=kOutput, calls=%fused_computation.8 | convolution fusion | flops 402653184 | bytes 9273344 | tf_op jit(solution)/shard_map/dot_general | solution.py:384
  20.4 1.6 %reshape.35 = f32[48,4,2,512]{3,2,1,0:T(2,128)} reshape(f32[48,4096]{1,0:T(8,128)S(1)} %fusion.2) | data formatting | bytes 1572864 | tf_op jit(solution)/shard_map/reshape | solution.py:385
  21.9 2.2 %fusion.1 = (f32[48,4,1,512]{3,2,1,0:T(1,128)S(1)}, f32[48,4,1,512]{3,2,1,0:T(1,128)S(1)}) fusion(f32[48,4,2,512]{3,2,1,0:T(2,128)} %reshape.35), kind=kLoop, calls=%fused_computation.7 | loop fusion | bytes 1572864 | tf_op jit(solution)/shard_map/slice | solution.py:386
  24.1 0.8 fusion
  25.0 2.7 %collective-permute-start.4 = (bf16[1024,512]{1,0:T(8,128)(2,1)}, bf16[1024,512]{1,0:T(8,128)(2,1)S(1)}, u32[]{:S(2)}, u32[]{:S(2)}) collective-permute-start(bf16[1024,512]{1,0:T(8,128)(2,1)} %refs_0_.1), channel_id=1, source_target_pairs={{0,192},{8,200},{16,208},{24,216},{32,224},{40,232},{48,240},{56,2... | collective-permute-start | bytes 3145736 | tf_op jit(solution)/shard_map/ppermute | solution.py:371
  27.7 1.2 %bitcast_add_fusion = f32[48,4,512]{2,1,0:T(4,128)S(1)} fusion(bf16[48,4,512]{2,1,0:T(4,128)(2,1)S(1)} %collective-permute-done, f32[48,4,1,512]{3,2,1,0:T(1,128)S(1)} %get-tuple-element.39, f32[48,4,1,512]{3,2,1,0:T(1,128)} %copy-done.3, pred[]{:T(512)S(6)} %eq.9), kind=kLoop, calls=%fused_computation | loop fusion | flops 294912 | bytes 1376257 | tf_op jit(solution)/shard_map/add | solution.py:389
  29.1 1.6 %collective-permute-start.1 = (bf16[48,512]{1,0:T(8,128)(2,1)S(1)}, bf16[48,512]{1,0:T(8,128)(2,1)S(1)}, u32[]{:S(2)}, u32[]{:S(2)}) collective-permute-start(bf16[48,512]{1,0:T(8,128)(2,1)S(1)} %get-tuple-element.41), channel_id=1, source_target_pairs={{0,2},{1,3},{2,4},{3,5},{4,6},{5,7},{6,0},{7,1},{8,10},{9,11},{10,... | collective-permute-start | bytes 147464 | tf_op jit(solution)/shard_map/ppermute | solution.py:378
  30.7 2.7 %collective-permute-start.2 = (bf16[48,512]{1,0:T(8,128)(2,1)S(1)}, bf16[48,512]{1,0:T(8,128)(2,1)S(1)}, u32[]{:S(2)}, u32[]{:S(2)}) collective-permute-start(bf16[48,512]{1,0:T(8,128)(2,1)S(1)} %get-tuple-element.43), channel_id=1, source_target_pairs={{0,4},{1,5},{2,6},{3,7},{4,0},{5,1},{6,2},{7,3},{8,12},{9,13},{10,... | collective-permute-start | bytes 147464 | tf_op jit(solution)/shard_map/ppermute | solution.py:378
  33.4 1.4 %collective-permute-start.3 = (bf16[48,512]{1,0:T(8,128)(2,1)S(1)}, bf16[48,512]{1,0:T(8,128)(2,1)}, u32[]{:S(2)}, u32[]{:S(2)}) collective-permute-start(bf16[48,512]{1,0:T(8,128)(2,1)S(1)} %get-tuple-element.42), channel_id=1, source_target_pairs={{0,6},{1,7},{2,0},{3,1},{4,2},{5,3},{6,4},{7,5},{8,14},{9,15},{10,... | collective-permute-start | bytes 147464 | tf_op jit(solution)/shard_map/ppermute | solution.py:378
  35.1 1.2 %collective-permute-done.2 = bf16[48,512]{1,0:T(8,128)(2,1)S(1)} collective-permute-done((bf16[48,512]{1,0:T(8,128)(2,1)S(1)}, bf16[48,512]{1,0:T(8,128)(2,1)S(1)}, u32[]{:S(2)}, u32[]{:S(2)}) %collective-permute-start.2) | collective-permute-done | bytes 49184 | tf_op jit(solution)/shard_map/ppermute | solution.py:378
  36.3 1.3 %collective-permute-done.3 = bf16[48,512]{1,0:T(8,128)(2,1)} collective-permute-done((bf16[48,512]{1,0:T(8,128)(2,1)S(1)}, bf16[48,512]{1,0:T(8,128)(2,1)}, u32[]{:S(2)}, u32[]{:S(2)}) %collective-permute-start.3) | collective-permute-done | bytes 49184 | tf_op jit(solution)/shard_map/ppermute | solution.py:378
  37.6 0.8 convert_add_fusion.frozen
  38.4 17.2 %all-to-all-done = bf16[32,8,3200]{2,1,0:T(8,128)(2,1)S(1)} async-done(((bf16[32,8,3200]{2,1,0:T(8,128)(2,1)}), bf16[32,8,3200]{2,1,0:T(8,128)(2,1)S(1)}, u32[]{:S(2)}, u32[]{:S(2)}) %all-to-all-start) | async-done | bytes 1638432 | tf_op jit(solution)/shard_map/all_to_all | solution.py:364
  55.6 4.3 %shard_map.111 = bf16[256,256]{1,0:T(8,128)(2,1)} custom-call(bf16[256,3200]{1,0:T(8,128)(2,1)S(1)} %bitcast.22, bf16[1024,1024]{1,0:T(8,128)(2,1)} %down.1), custom_call_target="tpu_custom_call" | custom-call | tf_op jit(solution)/shard_map/pallas_call | solution.py:339
  59.9 6.2 %all-to-all-start.1 = ((bf16[32,8,256]{2,1,0:T(8,128)(2,1)}), bf16[32,8,256]{2,1,0:T(8,128)(2,1)S(1)}, u32[]{:S(2)}, u32[]{:S(2)}) async-start(bf16[32,8,256]{2,1,0:T(8,128)(2,1)} %bitcast.10), calls=%async_computation.1 | async-start | bytes 262144 | tf_op jit(solution)/shard_map/all_to_all | solution.py:364
  66.2 1.0 copy-done.2
  67.2 1.2 %shard_map.112 = (bf16[512,512]{1,0:T(8,128)(2,1)S(1)}, bf16[512,512]{1,0:T(8,128)(2,1)S(1)}) custom-call(bf16[1024,512]{1,0:T(8,128)(2,1)} %copy-done.2, bf16[1024,512]{1,0:T(8,128)(2,1)} %collective-permute-done.5.behind.refs_2_), custom_call_target="tpu_custom_call" | custom-call | tf_op jit(solution)/shard_map/pallas_call | solution.py:290
  68.4 7.5 %all-to-all-done.1 = bf16[32,8,256]{2,1,0:T(8,128)(2,1)S(1)} async-done(((bf16[32,8,256]{2,1,0:T(8,128)(2,1)}), bf16[32,8,256]{2,1,0:T(8,128)(2,1)S(1)}, u32[]{:S(2)}, u32[]{:S(2)}) %all-to-all-start.1) | async-done | bytes 131104 | tf_op jit(solution)/shard_map/all_to_all | solution.py:364
  76.2 1.2 collective-permute-done.6
  77.4 1.1 collective-permute-start.10
  78.5 1.0 collective-permute-start.11
  79.4 1.5 %collective-permute-start.7 = (f32[24,128]{1,0:T(8,128)S(1)}, f32[24,128]{1,0:T(8,128)S(1)}, u32[]{:S(2)}, u32[]{:S(2)}) collective-permute-start(f32[24,128]{1,0:T(8,128)S(1)} %add.65.own), channel_id=1, source_target_pairs={{0,2},{1,3},{2,4},{3,5},{4,6},{5,7},{6,0},{7,1},{8,10},{9,11},{10,... | collective-permute-start | bytes 36872 | tf_op jit(solution)/shard_map/ppermute | solution.py:378
  80.9 1.8 %collective-permute-start.8 = (f32[24,128]{1,0:T(8,128)S(1)}, f32[24,128]{1,0:T(8,128)S(1)}, u32[]{:S(2)}, u32[]{:S(2)}) collective-permute-start(f32[24,128]{1,0:T(8,128)S(1)} %add.65.own), channel_id=1, source_target_pairs={{0,6},{1,7},{2,0},{3,1},{4,2},{5,3},{6,4},{7,5},{8,14},{9,15},{10,... | collective-permute-start | bytes 36872 | tf_op jit(solution)/shard_map/ppermute | solution.py:378
  82.6 1.8 %collective-permute-start.9 = (f32[24,128]{1,0:T(8,128)S(1)}, f32[24,128]{1,0:T(8,128)S(1)}, u32[]{:S(2)}, u32[]{:S(2)}) collective-permute-start(f32[24,128]{1,0:T(8,128)S(1)} %add.65.own), channel_id=1, source_target_pairs={{0,4},{1,5},{2,6},{3,7},{4,0},{5,1},{6,2},{7,3},{8,12},{9,13},{10,... | collective-permute-start | bytes 36872 | tf_op jit(solution)/shard_map/ppermute | solution.py:378
  84.6 3.3 %collective-permute-done.9.across = f32[24,128]{1,0:T(8,128)S(1)} collective-permute-done((f32[24,128]{1,0:T(8,128)S(1)}, f32[24,128]{1,0:T(8,128)S(1)}, u32[]{:S(2)}, u32[]{:S(2)}) %collective-permute-start.9) | collective-permute-done | bytes 12320 | tf_op jit(solution)/shard_map/ppermute | solution.py:378
  87.8 0.7 shard_map.114
  88.6 4.2 %all-to-all-start.2 = ((bf16[8,48,128]{2,1,0:T(8,128)(2,1)}), bf16[8,48,128]{2,1,0:T(8,128)(2,1)S(1)}, u32[]{:S(2)}, u32[]{:S(2)}) async-start(bf16[8,48,128]{2,1,0:T(8,128)(2,1)} %bitcast.12), calls=%async_computation.2 | async-start | bytes 196608 | tf_op jit(solution)/shard_map/all_to_all | solution.py:364
  92.8 7.3 %all-to-all-done.2 = bf16[8,48,128]{2,1,0:T(8,128)(2,1)S(1)} async-done(((bf16[8,48,128]{2,1,0:T(8,128)(2,1)}), bf16[8,48,128]{2,1,0:T(8,128)(2,1)S(1)}, u32[]{:S(2)}, u32[]{:S(2)}) %all-to-all-start.2) | async-done | bytes 98336 | tf_op jit(solution)/shard_map/all_to_all | solution.py:364
  100.1 3.7 %shard_map.115 = bf16[384,512]{1,0:T(8,128)(2,1)S(1)} custom-call(s32[1,1]{1,0:T(1,128)} %bitcast.place, bf16[384,128]{1,0:T(8,128)(2,1)S(1)} %bitcast.26, bf16[1024,512]{1,0:T(8,128)(2,1)} %refs_0_.1, bf16[1024,512]{1,0:T(8,128)(2,1)} %copy-done.2, bf16[1024,512]{1,0:T(8,128)(2,1)} %collective-permute-done.5.behind.refs_2_, ...), custom_call_target="tpu_custom_call" | custom-call | tf_op jit(solution)/shard_map/pallas_call | solution.py:301
  103.8 14.1 %all_to_all.46 = bf16[8,48,512]{2,1,0:T(8,128)(2,1)S(1)} all-to-all(bf16[8,48,512]{2,1,0:T(8,128)(2,1)S(1)} %bitcast.23), channel_id=1, replica_groups={{0,8,16,24,32,40,48,56},{64,72,80,88,96,104,112,120},{128,136,144,152,1..., dimensions={0} | all-to-all | bytes 786432 | tf_op jit(solution)/shard_map/all_to_all | solution.py:364
  (25 shorter events, 1.6 us)
Async XLA Ops:
  4.0 51.6 %all-to-all-start = ((bf16[32,8,3200]{2,1,0:T(8,128)(2,1)}), bf16[32,8,3200]{2,1,0:T(8,128)(2,1)S(1)}, u32[]{:S(2)}, u32[]{:S(2)}) async-start(bf16[32,8,3200]{2,1,0:T(8,128)(2,1)} %bitcast.6), calls=%async_computation | async-start | bytes 3276800 | tf_op jit(solution)/shard_map/all_to_all | solution.py:364
  15.4 19.5 %copy-start = (s32[48,4]{0,1:T(4,128)S(1)}, s32[48,4]{0,1:T(4,128)}, u32[]{:S(2)}) copy-start(s32[48,4]{0,1:T(4,128)} %param.20) | copy-start | bytes 2308
  15.4 19.5 %copy-start.1 = (f32[48,4]{0,1:T(4,128)S(1)}, f32[48,4]{0,1:T(4,128)}, u32[]{:S(2)}) copy-start(f32[48,4]{0,1:T(4,128)} %param.21) | copy-start | bytes 2308
  24.1 0.9 copy-start.3
  25.0 2.7 %collective-permute-start = (bf16[48,4,512]{2,1,0:T(4,128)(2,1)}, bf16[48,4,512]{2,1,0:T(4,128)(2,1)S(1)}, u32[]{:S(2)}, u32[]{:S(2)}) collective-permute-start(bf16[48,4,512]{2,1,0:T(4,128)(2,1)} %fusion), channel_id=1, source_target_pairs={{0,1},{1,0},{2,3},{3,2},{4,5},{5,4},{6,7},{7,6},{8,9},{9,8},{10,11... | collective-permute-start | bytes 589832 | tf_op jit(solution)/shard_map/ppermute | solution.py:378
  25.0 41.2 %collective-permute-start.4 = (bf16[1024,512]{1,0:T(8,128)(2,1)}, bf16[1024,512]{1,0:T(8,128)(2,1)S(1)}, u32[]{:S(2)}, u32[]{:S(2)}) collective-permute-start(bf16[1024,512]{1,0:T(8,128)(2,1)} %refs_0_.1), channel_id=1, source_target_pairs={{0,192},{8,200},{16,208},{24,216},{32,224},{40,232},{48,240},{56,2... | collective-permute-start | bytes 3145736 | tf_op jit(solution)/shard_map/ppermute | solution.py:371
  27.7 38.5 %collective-permute-start.5 = (bf16[1024,512]{1,0:T(8,128)(2,1)}, bf16[1024,512]{1,0:T(8,128)(2,1)}, u32[]{:S(2)}, u32[]{:S(2)}) collective-permute-start(bf16[1024,512]{1,0:T(8,128)(2,1)} %refs_0_.1), channel_id=1, source_target_pairs={{0,64},{8,72},{16,80},{24,88},{32,96},{40,104},{48,112},{56,120},{... | collective-permute-start | bytes 3145736 | tf_op jit(solution)/shard_map/ppermute | solution.py:371
  29.1 6.0 %collective-permute-start.1 = (bf16[48,512]{1,0:T(8,128)(2,1)S(1)}, bf16[48,512]{1,0:T(8,128)(2,1)S(1)}, u32[]{:S(2)}, u32[]{:S(2)}) collective-permute-start(bf16[48,512]{1,0:T(8,128)(2,1)S(1)} %get-tuple-element.41), channel_id=1, source_target_pairs={{0,2},{1,3},{2,4},{3,5},{4,6},{5,7},{6,0},{7,1},{8,10},{9,11},{10,... | collective-permute-start | bytes 147464 | tf_op jit(solution)/shard_map/ppermute | solution.py:378
  30.7 5.6 %collective-permute-start.2 = (bf16[48,512]{1,0:T(8,128)(2,1)S(1)}, bf16[48,512]{1,0:T(8,128)(2,1)S(1)}, u32[]{:S(2)}, u32[]{:S(2)}) collective-permute-start(bf16[48,512]{1,0:T(8,128)(2,1)S(1)} %get-tuple-element.43), channel_id=1, source_target_pairs={{0,4},{1,5},{2,6},{3,7},{4,0},{5,1},{6,2},{7,3},{8,12},{9,13},{10,... | collective-permute-start | bytes 147464 | tf_op jit(solution)/shard_map/ppermute | solution.py:378
  33.4 4.2 %collective-permute-start.3 = (bf16[48,512]{1,0:T(8,128)(2,1)S(1)}, bf16[48,512]{1,0:T(8,128)(2,1)}, u32[]{:S(2)}, u32[]{:S(2)}) collective-permute-start(bf16[48,512]{1,0:T(8,128)(2,1)S(1)} %get-tuple-element.42), channel_id=1, source_target_pairs={{0,6},{1,7},{2,0},{3,1},{4,2},{5,3},{6,4},{7,5},{8,14},{9,15},{10,... | collective-permute-start | bytes 147464 | tf_op jit(solution)/shard_map/ppermute | solution.py:378
  59.9 16.0 %all-to-all-start.1 = ((bf16[32,8,256]{2,1,0:T(8,128)(2,1)}), bf16[32,8,256]{2,1,0:T(8,128)(2,1)S(1)}, u32[]{:S(2)}, u32[]{:S(2)}) async-start(bf16[32,8,256]{2,1,0:T(8,128)(2,1)} %bitcast.10), calls=%async_computation.1 | async-start | bytes 262144 | tf_op jit(solution)/shard_map/all_to_all | solution.py:364
  66.2 1.0 copy-start.2
  76.2 1.2 %collective-permute-start.6 = (f32[24,128]{1,0:T(8,128)S(1)}, f32[24,128]{1,0:T(8,128)S(1)}, u32[]{:S(2)}, u32[]{:S(2)}) collective-permute-start(f32[24,128]{1,0:T(8,128)S(1)} %shard_map.113), channel_id=1, source_target_pairs={{0,1},{1,0},{2,3},{3,2},{4,5},{5,4},{6,7},{7,6},{8,9},{9,8},{10,11... | collective-permute-start | bytes 36872 | tf_op jit(solution)/shard_map/ppermute | solution.py:378
  77.4 22.7 %collective-permute-start.10 = (bf16[512,512]{1,0:T(8,128)(2,1)S(1)}, bf16[512,512]{1,0:T(8,128)(2,1)S(1)}, u32[]{:S(2)}, u32[]{:S(2)}) collective-permute-start(bf16[512,512]{1,0:T(8,128)(2,1)S(1)} %get-tuple-element.36), channel_id=1, source_target_pairs={{0,192},{8,200},{16,208},{24,216},{32,224},{40,232},{48,240},{56,2... | collective-permute-start | bytes 1572872 | tf_op jit(solution)/shard_map/ppermute | solution.py:371
  78.5 21.6 %collective-permute-start.11 = (bf16[512,512]{1,0:T(8,128)(2,1)S(1)}, bf16[512,512]{1,0:T(8,128)(2,1)S(1)}, u32[]{:S(2)}, u32[]{:S(2)}) collective-permute-start(bf16[512,512]{1,0:T(8,128)(2,1)S(1)} %get-tuple-element.37), channel_id=1, source_target_pairs={{0,64},{8,72},{16,80},{24,88},{32,96},{40,104},{48,112},{56,120},{... | collective-permute-start | bytes 1572872 | tf_op jit(solution)/shard_map/ppermute | solution.py:371
  79.4 5.1 %collective-permute-start.7 = (f32[24,128]{1,0:T(8,128)S(1)}, f32[24,128]{1,0:T(8,128)S(1)}, u32[]{:S(2)}, u32[]{:S(2)}) collective-permute-start(f32[24,128]{1,0:T(8,128)S(1)} %add.65.own), channel_id=1, source_target_pairs={{0,2},{1,3},{2,4},{3,5},{4,6},{5,7},{6,0},{7,1},{8,10},{9,11},{10,... | collective-permute-start | bytes 36872 | tf_op jit(solution)/shard_map/ppermute | solution.py:378
  80.9 3.7 %collective-permute-start.8 = (f32[24,128]{1,0:T(8,128)S(1)}, f32[24,128]{1,0:T(8,128)S(1)}, u32[]{:S(2)}, u32[]{:S(2)}) collective-permute-start(f32[24,128]{1,0:T(8,128)S(1)} %add.65.own), channel_id=1, source_target_pairs={{0,6},{1,7},{2,0},{3,1},{4,2},{5,3},{6,4},{7,5},{8,14},{9,15},{10,... | collective-permute-start | bytes 36872 | tf_op jit(solution)/shard_map/ppermute | solution.py:378
  82.6 5.2 %collective-permute-start.9 = (f32[24,128]{1,0:T(8,128)S(1)}, f32[24,128]{1,0:T(8,128)S(1)}, u32[]{:S(2)}, u32[]{:S(2)}) collective-permute-start(f32[24,128]{1,0:T(8,128)S(1)} %add.65.own), channel_id=1, source_target_pairs={{0,4},{1,5},{2,6},{3,7},{4,0},{5,1},{6,2},{7,3},{8,12},{9,13},{10,... | collective-permute-start | bytes 36872 | tf_op jit(solution)/shard_map/ppermute | solution.py:378
  88.6 11.5 %all-to-all-start.2 = ((bf16[8,48,128]{2,1,0:T(8,128)(2,1)}), bf16[8,48,128]{2,1,0:T(8,128)(2,1)S(1)}, u32[]{:S(2)}, u32[]{:S(2)}) async-start(bf16[8,48,128]{2,1,0:T(8,128)(2,1)} %bitcast.12), calls=%async_computation.2 | async-start | bytes 196608 | tf_op jit(solution)/shard_map/all_to_all | solution.py:364

commit v7 on v6

--- a/solution.py
+++ b/solution.py
@@ -27,6 +27,7 @@
 CORES = 2
 CHIPS = 4
 DOWN_STEPS = 2
+PIECES = 2
 DEPTH = 8
 SIDES = 4
 COLUMNS = [[y * DEPTH + z for z in range(DEPTH)] for y in range(SIDES)]
@@ -98,7 +99,7 @@
             coefs = coefs + dot((pick & hits[j]).astype(BF), spreads[j], ((1,), (1,)))
         meta = meta + (pltpu.roll(coefs, g * 2 * ADP_DEV, 1) if g else coefs)
     made[:, PARTS * FEATS :] = meta.astype(BF)
-    leaving = [leave(PARTS, PARTS * FEATS, 128)]
+    leaving = [leave(PARTS * PIECES, PARTS * FEATS, 128)]
 
     for copy in copies[2:]:
         copy.wait()
@@ -132,8 +133,12 @@
     everything = att[...]
     for g in range(PARTS):
         pick = picks[pl.ds(g * LINES, LINES), :]
-        made[:, g * FEATS : (g + 1) * FEATS] = dot(pick, everything).astype(BF)
-        leaving.append(leave(g, g * FEATS, FEATS))
+        for n in range(PIECES):
+            width = FEATS // PIECES
+            start = g * FEATS + n * width
+            piece = dot(pick, everything[:, n * width : (n + 1) * width])
+            made[:, start : start + width] = piece.astype(BF)
+            leaving.append(leave(g * PIECES + n, start, width))
     for copy in leaving:
         copy.wait()
 
@@ -329,7 +334,7 @@
         + [
             pltpu.SemaphoreType.DMA((len(args),)),
             pltpu.VMEM((LINES, PARTS * FEATS + 128), BF),
-            pltpu.SemaphoreType.DMA((PARTS + 1,)),
+            pltpu.SemaphoreType.DMA((PARTS * PIECES + 1,)),
         ],
         compiler_params=pltpu.CompilerParams(vmem_limit_bytes=32 * 1024 * 1024),
     )(*[pltpu.with_memory_space_constraint(x, pltpu.HBM) for x in args])

time: 120 us -> 120 us (level)
  no operation moved by 1% of the time
where the time goes in v7:
time: 120 us; the launch traced here: 119 us
  waiting for transfers between devices  39.1 us (33%)
  starting transfers between devices  37.3 us (31%)
  Pallas kernels  15.1 us (13%)
  blocking collectives  14.1 us (12%)
  matrix products  4.95 us (4%)
  local copies, waits for them, and re-layouts  4.9 us (4%)
  other arithmetic  2.91 us (2%)
    all_to_all x3, waiting for transfers between devices, swap(): lax.all_to_all(x, axis, split_axis=0, concat_axis=0, axis_index_groups=gr...  32 us
    all_to_all x3, starting transfers between devices, swap(): lax.all_to_all(x, axis, split_axis=0, concat_axis=0, axis_index_groups=gr...  21.8 us
    all_to_all x1, blocking collectives, swap(): lax.all_to_all(x, axis, split_axis=0, concat_axis=0, axis_index_groups=gr...  14.1 us
    ppermute x8, starting transfers between devices, turn(): return lax.ppermute(x, 'tensor', pairs)  10.8 us
    ppermute x8, waiting for transfers between devices, turn(): return lax.ppermute(x, 'tensor', pairs)  7.05 us
    dot_general x1, matrix products, frozen_sum(): part = jnp.dot(attended, out_weight, preferred_element_type=F32)  4.95 us
    ppermute x4, starting transfers between devices, beside(): return lax.ppermute(x, 'adapter', pairs)  4.75 us
    pallas_call x1, Pallas kernels, lower(): pl.pallas_call(lower_kernel, out_shape=shape_of(LINES, 256), in_specs=[pl...  4.29 us
  transfers between devices with their start and end apart: 15, of which 8 were waited for; matrix products, arithmetic and copies ran while one was open for 10% of the time, Pallas kernels for 5%

profile of v7, /device:TPU:32, one launch (start us, length us, event | category | flops | bytes accessed | tf_op | source)
XLA Modules:
  0.0 118.5 jit_solution(8924485113488920959)
XLA Ops:
  0.0 4.0 %shard_map.109 = (bf16[48,1024]{1,0:T(8,128)(2,1)S(1)}, bf16[256,3200]{1,0:T(8,128)(2,1)}) custom-call(bf16[48,1024]{1,0:T(8,128)(2,1)} %q_hbm.1, bf16[1536,128]{1,0:T(8,128)(2,1)} %bitcast.34, bf16[1536,128]{1,0:T(8,128)(2,1)} %bitcast.35, bf16[48,128]{1,0:T(8,128)(2,1)} %nk_hbm.1, bf16[48,128]{1,0:T(8,128)(2,1)} %nv_hbm.1, s32[1,48]{1,0:T(1,128)} %bitcast.36, ...), custom_call_target="tpu_custom_call" | custom-call | tf_op jit(solution)/shard_map/pallas_call | solution.py:321
  4.0 11.4 %all-to-all-start = ((bf16[32,8,3200]{2,1,0:T(8,128)(2,1)}), bf16[32,8,3200]{2,1,0:T(8,128)(2,1)S(1)}, u32[]{:S(2)}, u32[]{:S(2)}) async-start(bf16[32,8,3200]{2,1,0:T(8,128)(2,1)} %bitcast.6), calls=%async_computation | async-start | bytes 3276800 | tf_op jit(solution)/shard_map/all_to_all | solution.py:369
  15.4 5.0 %fusion.2 = f32[48,4096]{1,0:T(8,128)S(1)} fusion(bf16[48,1024]{1,0:T(8,128)(2,1)S(1)} %get-tuple-element.23.after, bf16[1024,4096]{1,0:T(8,128)(2,1)} %param.17), kind=kOutput, calls=%fused_computation.8 | convolution fusion | flops 402653184 | bytes 9273344 | tf_op jit(solution)/shard_map/dot_general | solution.py:389
  20.4 1.6 %reshape.35 = f32[48,4,2,512]{3,2,1,0:T(2,128)} reshape(f32[48,4096]{1,0:T(8,128)S(1)} %fusion.2) | data formatting | bytes 1572864 | tf_op jit(solution)/shard_map/reshape | solution.py:390
  21.9 2.2 %fusion.1 = (f32[48,4,1,512]{3,2,1,0:T(1,128)S(1)}, f32[48,4,1,512]{3,2,1,0:T(1,128)S(1)}) fusion(f32[48,4,2,512]{3,2,1,0:T(2,128)} %reshape.35), kind=kLoop, calls=%fused_computation.7 | loop fusion | bytes 1572864 | tf_op jit(solution)/shard_map/slice | solution.py:391
  24.1 0.8 fusion
  24.9 2.7 %collective-permute-start.4 = (bf16[1024,512]{1,0:T(8,128)(2,1)}, bf16[1024,512]{1,0:T(8,128)(2,1)S(1)}, u32[]{:S(2)}, u32[]{:S(2)}) collective-permute-start(bf16[1024,512]{1,0:T(8,128)(2,1)} %refs_0_.1), channel_id=1, source_target_pairs={{0,192},{8,200},{16,208},{24,216},{32,224},{40,232},{48,240},{56,2... | collective-permute-start | bytes 3145736 | tf_op jit(solution)/shard_map/ppermute | solution.py:376
  27.7 1.2 %bitcast_add_fusion = f32[48,4,512]{2,1,0:T(4,128)S(1)} fusion(bf16[48,4,512]{2,1,0:T(4,128)(2,1)S(1)} %collective-permute-done, f32[48,4,1,512]{3,2,1,0:T(1,128)S(1)} %get-tuple-element.39, f32[48,4,1,512]{3,2,1,0:T(1,128)} %copy-done.3, pred[]{:T(512)S(6)} %eq.9), kind=kLoop, calls=%fused_computation | loop fusion | flops 294912 | bytes 1376257 | tf_op jit(solution)/shard_map/add | solution.py:394
  29.1 1.6 %collective-permute-start.1 = (bf16[48,512]{1,0:T(8,128)(2,1)S(1)}, bf16[48,512]{1,0:T(8,128)(2,1)S(1)}, u32[]{:S(2)}, u32[]{:S(2)}) collective-permute-start(bf16[48,512]{1,0:T(8,128)(2,1)S(1)} %get-tuple-element.41), channel_id=1, source_target_pairs={{0,2},{1,3},{2,4},{3,5},{4,6},{5,7},{6,0},{7,1},{8,10},{9,11},{10,... | collective-permute-start | bytes 147464 | tf_op jit(solution)/shard_map/ppermute | solution.py:383
  30.7 2.7 %collective-permute-start.2 = (bf16[48,512]{1,0:T(8,128)(2,1)S(1)}, bf16[48,512]{1,0:T(8,128)(2,1)S(1)}, u32[]{:S(2)}, u32[]{:S(2)}) collective-permute-start(bf16[48,512]{1,0:T(8,128)(2,1)S(1)} %get-tuple-element.43), channel_id=1, source_target_pairs={{0,4},{1,5},{2,6},{3,7},{4,0},{5,1},{6,2},{7,3},{8,12},{9,13},{10,... | collective-permute-start | bytes 147464 | tf_op jit(solution)/shard_map/ppermute | solution.py:383
  33.4 1.4 %collective-permute-start.3 = (bf16[48,512]{1,0:T(8,128)(2,1)S(1)}, bf16[48,512]{1,0:T(8,128)(2,1)}, u32[]{:S(2)}, u32[]{:S(2)}) collective-permute-start(bf16[48,512]{1,0:T(8,128)(2,1)S(1)} %get-tuple-element.42), channel_id=1, source_target_pairs={{0,6},{1,7},{2,0},{3,1},{4,2},{5,3},{6,4},{7,5},{8,14},{9,15},{10,... | collective-permute-start | bytes 147464 | tf_op jit(solution)/shard_map/ppermute | solution.py:383
  35.1 1.2 %collective-permute-done.2 = bf16[48,512]{1,0:T(8,128)(2,1)S(1)} collective-permute-done((bf16[48,512]{1,0:T(8,128)(2,1)S(1)}, bf16[48,512]{1,0:T(8,128)(2,1)S(1)}, u32[]{:S(2)}, u32[]{:S(2)}) %collective-permute-start.2) | collective-permute-done | bytes 49184 | tf_op jit(solution)/shard_map/ppermute | solution.py:383
  36.3 1.3 %collective-permute-done.3 = bf16[48,512]{1,0:T(8,128)(2,1)} collective-permute-done((bf16[48,512]{1,0:T(8,128)(2,1)S(1)}, bf16[48,512]{1,0:T(8,128)(2,1)}, u32[]{:S(2)}, u32[]{:S(2)}) %collective-permute-start.3) | collective-permute-done | bytes 49184 | tf_op jit(solution)/shard_map/ppermute | solution.py:383
  37.6 0.8 convert_add_fusion.frozen
  38.4 17.2 %all-to-all-done = bf16[32,8,3200]{2,1,0:T(8,128)(2,1)S(1)} async-done(((bf16[32,8,3200]{2,1,0:T(8,128)(2,1)}), bf16[32,8,3200]{2,1,0:T(8,128)(2,1)S(1)}, u32[]{:S(2)}, u32[]{:S(2)}) %all-to-all-start) | async-done | bytes 1638432 | tf_op jit(solution)/shard_map/all_to_all | solution.py:369
  55.6 4.3 %shard_map.111 = bf16[256,256]{1,0:T(8,128)(2,1)} custom-call(bf16[256,3200]{1,0:T(8,128)(2,1)S(1)} %bitcast.22, bf16[1024,1024]{1,0:T(8,128)(2,1)} %down.1), custom_call_target="tpu_custom_call" | custom-call | tf_op jit(solution)/shard_map/pallas_call | solution.py:344
  59.9 6.2 %all-to-all-start.1 = ((bf16[32,8,256]{2,1,0:T(8,128)(2,1)}), bf16[32,8,256]{2,1,0:T(8,128)(2,1)S(1)}, u32[]{:S(2)}, u32[]{:S(2)}) async-start(bf16[32,8,256]{2,1,0:T(8,128)(2,1)} %bitcast.10), calls=%async_computation.1 | async-start | bytes 262144 | tf_op jit(solution)/shard_map/all_to_all | solution.py:369
  66.2 1.0 copy-done.2
  67.2 1.2 %shard_map.112 = (bf16[512,512]{1,0:T(8,128)(2,1)S(1)}, bf16[512,512]{1,0:T(8,128)(2,1)S(1)}) custom-call(bf16[1024,512]{1,0:T(8,128)(2,1)} %copy-done.2, bf16[1024,512]{1,0:T(8,128)(2,1)} %collective-permute-done.5.behind.refs_2_), custom_call_target="tpu_custom_call" | custom-call | tf_op jit(solution)/shard_map/pallas_call | solution.py:295
  68.4 7.5 %all-to-all-done.1 = bf16[32,8,256]{2,1,0:T(8,128)(2,1)S(1)} async-done(((bf16[32,8,256]{2,1,0:T(8,128)(2,1)}), bf16[32,8,256]{2,1,0:T(8,128)(2,1)S(1)}, u32[]{:S(2)}, u32[]{:S(2)}) %all-to-all-start.1) | async-done | bytes 131104 | tf_op jit(solution)/shard_map/all_to_all | solution.py:369
  76.2 1.2 collective-permute-done.6
  77.4 1.1 collective-permute-start.10
  78.4 1.0 collective-permute-start.11
  79.4 1.5 %collective-permute-start.7 = (f32[24,128]{1,0:T(8,128)S(1)}, f32[24,128]{1,0:T(8,128)S(1)}, u32[]{:S(2)}, u32[]{:S(2)}) collective-permute-start(f32[24,128]{1,0:T(8,128)S(1)} %add.65.own), channel_id=1, source_target_pairs={{0,2},{1,3},{2,4},{3,5},{4,6},{5,7},{6,0},{7,1},{8,10},{9,11},{10,... | collective-permute-start | bytes 36872 | tf_op jit(solution)/shard_map/ppermute | solution.py:383
  80.9 1.8 %collective-permute-start.8 = (f32[24,128]{1,0:T(8,128)S(1)}, f32[24,128]{1,0:T(8,128)S(1)}, u32[]{:S(2)}, u32[]{:S(2)}) collective-permute-start(f32[24,128]{1,0:T(8,128)S(1)} %add.65.own), channel_id=1, source_target_pairs={{0,6},{1,7},{2,0},{3,1},{4,2},{5,3},{6,4},{7,5},{8,14},{9,15},{10,... | collective-permute-start | bytes 36872 | tf_op jit(solution)/shard_map/ppermute | solution.py:383
  82.6 1.8 %collective-permute-start.9 = (f32[24,128]{1,0:T(8,128)S(1)}, f32[24,128]{1,0:T(8,128)S(1)}, u32[]{:S(2)}, u32[]{:S(2)}) collective-permute-start(f32[24,128]{1,0:T(8,128)S(1)} %add.65.own), channel_id=1, source_target_pairs={{0,4},{1,5},{2,6},{3,7},{4,0},{5,1},{6,2},{7,3},{8,12},{9,13},{10,... | collective-permute-start | bytes 36872 | tf_op jit(solution)/shard_map/ppermute | solution.py:383
  84.6 3.3 %collective-permute-done.9.across = f32[24,128]{1,0:T(8,128)S(1)} collective-permute-done((f32[24,128]{1,0:T(8,128)S(1)}, f32[24,128]{1,0:T(8,128)S(1)}, u32[]{:S(2)}, u32[]{:S(2)}) %collective-permute-start.9) | collective-permute-done | bytes 12320 | tf_op jit(solution)/shard_map/ppermute | solution.py:383
  87.8 0.7 shard_map.114
  88.5 4.2 %all-to-all-start.2 = ((bf16[8,48,128]{2,1,0:T(8,128)(2,1)}), bf16[8,48,128]{2,1,0:T(8,128)(2,1)S(1)}, u32[]{:S(2)}, u32[]{:S(2)}) async-start(bf16[8,48,128]{2,1,0:T(8,128)(2,1)} %bitcast.12), calls=%async_computation.2 | async-start | bytes 196608 | tf_op jit(solution)/shard_map/all_to_all | solution.py:369
  92.7 7.3 %all-to-all-done.2 = bf16[8,48,128]{2,1,0:T(8,128)(2,1)S(1)} async-done(((bf16[8,48,128]{2,1,0:T(8,128)(2,1)}), bf16[8,48,128]{2,1,0:T(8,128)(2,1)S(1)}, u32[]{:S(2)}, u32[]{:S(2)}) %all-to-all-start.2) | async-done | bytes 98336 | tf_op jit(solution)/shard_map/all_to_all | solution.py:369
  100.0 3.7 %shard_map.115 = bf16[384,512]{1,0:T(8,128)(2,1)S(1)} custom-call(s32[1,1]{1,0:T(1,128)} %bitcast.place, bf16[384,128]{1,0:T(8,128)(2,1)S(1)} %bitcast.26, bf16[1024,512]{1,0:T(8,128)(2,1)} %refs_0_.1, bf16[1024,512]{1,0:T(8,128)(2,1)} %copy-done.2, bf16[1024,512]{1,0:T(8,128)(2,1)} %collective-permute-done.5.behind.refs_2_, ...), custom_call_target="tpu_custom_call" | custom-call | tf_op jit(solution)/shard_map/pallas_call | solution.py:306
  103.7 14.1 %all_to_all.46 = bf16[8,48,512]{2,1,0:T(8,128)(2,1)S(1)} all-to-all(bf16[8,48,512]{2,1,0:T(8,128)(2,1)S(1)} %bitcast.23), channel_id=1, replica_groups={{0,8,16,24,32,40,48,56},{64,72,80,88,96,104,112,120},{128,136,144,152,1..., dimensions={0} | all-to-all | bytes 786432 | tf_op jit(solution)/shard_map/all_to_all | solution.py:369
  (25 shorter events, 1.6 us)
Async XLA Ops:
  4.0 51.6 %all-to-all-start = ((bf16[32,8,3200]{2,1,0:T(8,128)(2,1)}), bf16[32,8,3200]{2,1,0:T(8,128)(2,1)S(1)}, u32[]{:S(2)}, u32[]{:S(2)}) async-start(bf16[32,8,3200]{2,1,0:T(8,128)(2,1)} %bitcast.6), calls=%async_computation | async-start | bytes 3276800 | tf_op jit(solution)/shard_map/all_to_all | solution.py:369
  15.4 19.5 %copy-start = (s32[48,4]{0,1:T(4,128)S(1)}, s32[48,4]{0,1:T(4,128)}, u32[]{:S(2)}) copy-start(s32[48,4]{0,1:T(4,128)} %param.20) | copy-start | bytes 2308
  15.4 19.5 %copy-start.1 = (f32[48,4]{0,1:T(4,128)S(1)}, f32[48,4]{0,1:T(4,128)}, u32[]{:S(2)}) copy-start(f32[48,4]{0,1:T(4,128)} %param.21) | copy-start | bytes 2308
  24.1 0.9 copy-start.3
  24.9 2.7 %collective-permute-start = (bf16[48,4,512]{2,1,0:T(4,128)(2,1)}, bf16[48,4,512]{2,1,0:T(4,128)(2,1)S(1)}, u32[]{:S(2)}, u32[]{:S(2)}) collective-permute-start(bf16[48,4,512]{2,1,0:T(4,128)(2,1)} %fusion), channel_id=1, source_target_pairs={{0,1},{1,0},{2,3},{3,2},{4,5},{5,4},{6,7},{7,6},{8,9},{9,8},{10,11... | collective-permute-start | bytes 589832 | tf_op jit(solution)/shard_map/ppermute | solution.py:383
  24.9 41.2 %collective-permute-start.4 = (bf16[1024,512]{1,0:T(8,128)(2,1)}, bf16[1024,512]{1,0:T(8,128)(2,1)S(1)}, u32[]{:S(2)}, u32[]{:S(2)}) collective-permute-start(bf16[1024,512]{1,0:T(8,128)(2,1)} %refs_0_.1), channel_id=1, source_target_pairs={{0,192},{8,200},{16,208},{24,216},{32,224},{40,232},{48,240},{56,2... | collective-permute-start | bytes 3145736 | tf_op jit(solution)/shard_map/ppermute | solution.py:376
  27.7 38.5 %collective-permute-start.5 = (bf16[1024,512]{1,0:T(8,128)(2,1)}, bf16[1024,512]{1,0:T(8,128)(2,1)}, u32[]{:S(2)}, u32[]{:S(2)}) collective-permute-start(bf16[1024,512]{1,0:T(8,128)(2,1)} %refs_0_.1), channel_id=1, source_target_pairs={{0,64},{8,72},{16,80},{24,88},{32,96},{40,104},{48,112},{56,120},{... | collective-permute-start | bytes 3145736 | tf_op jit(solution)/shard_map/ppermute | solution.py:376
  29.1 6.0 %collective-permute-start.1 = (bf16[48,512]{1,0:T(8,128)(2,1)S(1)}, bf16[48,512]{1,0:T(8,128)(2,1)S(1)}, u32[]{:S(2)}, u32[]{:S(2)}) collective-permute-start(bf16[48,512]{1,0:T(8,128)(2,1)S(1)} %get-tuple-element.41), channel_id=1, source_target_pairs={{0,2},{1,3},{2,4},{3,5},{4,6},{5,7},{6,0},{7,1},{8,10},{9,11},{10,... | collective-permute-start | bytes 147464 | tf_op jit(solution)/shard_map/ppermute | solution.py:383
  30.7 5.6 %collective-permute-start.2 = (bf16[48,512]{1,0:T(8,128)(2,1)S(1)}, bf16[48,512]{1,0:T(8,128)(2,1)S(1)}, u32[]{:S(2)}, u32[]{:S(2)}) collective-permute-start(bf16[48,512]{1,0:T(8,128)(2,1)S(1)} %get-tuple-element.43), channel_id=1, source_target_pairs={{0,4},{1,5},{2,6},{3,7},{4,0},{5,1},{6,2},{7,3},{8,12},{9,13},{10,... | collective-permute-start | bytes 147464 | tf_op jit(solution)/shard_map/ppermute | solution.py:383
  33.4 4.2 %collective-permute-start.3 = (bf16[48,512]{1,0:T(8,128)(2,1)S(1)}, bf16[48,512]{1,0:T(8,128)(2,1)}, u32[]{:S(2)}, u32[]{:S(2)}) collective-permute-start(bf16[48,512]{1,0:T(8,128)(2,1)S(1)} %get-tuple-element.42), channel_id=1, source_target_pairs={{0,6},{1,7},{2,0},{3,1},{4,2},{5,3},{6,4},{7,5},{8,14},{9,15},{10,... | collective-permute-start | bytes 147464 | tf_op jit(solution)/shard_map/ppermute | solution.py:383
  59.9 16.0 %all-to-all-start.1 = ((bf16[32,8,256]{2,1,0:T(8,128)(2,1)}), bf16[32,8,256]{2,1,0:T(8,128)(2,1)S(1)}, u32[]{:S(2)}, u32[]{:S(2)}) async-start(bf16[32,8,256]{2,1,0:T(8,128)(2,1)} %bitcast.10), calls=%async_computation.1 | async-start | bytes 262144 | tf_op jit(solution)/shard_map/all_to_all | solution.py:369
  66.1 1.0 copy-start.2
  76.1 1.2 %collective-permute-start.6 = (f32[24,128]{1,0:T(8,128)S(1)}, f32[24,128]{1,0:T(8,128)S(1)}, u32[]{:S(2)}, u32[]{:S(2)}) collective-permute-start(f32[24,128]{1,0:T(8,128)S(1)} %shard_map.113), channel_id=1, source_target_pairs={{0,1},{1,0},{2,3},{3,2},{4,5},{5,4},{6,7},{7,6},{8,9},{9,8},{10,11... | collective-permute-start | bytes 36872 | tf_op jit(solution)/shard_map/ppermute | solution.py:383
  77.4 22.7 %collective-permute-start.10 = (bf16[512,512]{1,0:T(8,128)(2,1)S(1)}, bf16[512,512]{1,0:T(8,128)(2,1)S(1)}, u32[]{:S(2)}, u32[]{:S(2)}) collective-permute-start(bf16[512,512]{1,0:T(8,128)(2,1)S(1)} %get-tuple-element.36), channel_id=1, source_target_pairs={{0,192},{8,200},{16,208},{24,216},{32,224},{40,232},{48,240},{56,2... | collective-permute-start | bytes 1572872 | tf_op jit(solution)/shard_map/ppermute | solution.py:376
  78.4 21.6 %collective-permute-start.11 = (bf16[512,512]{1,0:T(8,128)(2,1)S(1)}, bf16[512,512]{1,0:T(8,128)(2,1)S(1)}, u32[]{:S(2)}, u32[]{:S(2)}) collective-permute-start(bf16[512,512]{1,0:T(8,128)(2,1)S(1)} %get-tuple-element.37), channel_id=1, source_target_pairs={{0,64},{8,72},{16,80},{24,88},{32,96},{40,104},{48,112},{56,120},{... | collective-permute-start | bytes 1572872 | tf_op jit(solution)/shard_map/ppermute | solution.py:376
  79.4 5.0 %collective-permute-start.7 = (f32[24,128]{1,0:T(8,128)S(1)}, f32[24,128]{1,0:T(8,128)S(1)}, u32[]{:S(2)}, u32[]{:S(2)}) collective-permute-start(f32[24,128]{1,0:T(8,128)S(1)} %add.65.own), channel_id=1, source_target_pairs={{0,2},{1,3},{2,4},{3,5},{4,6},{5,7},{6,0},{7,1},{8,10},{9,11},{10,... | collective-permute-start | bytes 36872 | tf_op jit(solution)/shard_map/ppermute | solution.py:383
  80.9 3.7 %collective-permute-start.8 = (f32[24,128]{1,0:T(8,128)S(1)}, f32[24,128]{1,0:T(8,128)S(1)}, u32[]{:S(2)}, u32[]{:S(2)}) collective-permute-start(f32[24,128]{1,0:T(8,128)S(1)} %add.65.own), channel_id=1, source_target_pairs={{0,6},{1,7},{2,0},{3,1},{4,2},{5,3},{6,4},{7,5},{8,14},{9,15},{10,... | collective-permute-start | bytes 36872 | tf_op jit(solution)/shard_map/ppermute | solution.py:383
  82.6 5.2 %collective-permute-start.9 = (f32[24,128]{1,0:T(8,128)S(1)}, f32[24,128]{1,0:T(8,128)S(1)}, u32[]{:S(2)}, u32[]{:S(2)}) collective-permute-start(f32[24,128]{1,0:T(8,128)S(1)} %add.65.own), channel_id=1, source_target_pairs={{0,4},{1,5},{2,6},{3,7},{4,0},{5,1},{6,2},{7,3},{8,12},{9,13},{10,... | collective-permute-start | bytes 36872 | tf_op jit(solution)/shard_map/ppermute | solution.py:383
  88.5 11.5 %all-to-all-start.2 = ((bf16[8,48,128]{2,1,0:T(8,128)(2,1)}), bf16[8,48,128]{2,1,0:T(8,128)(2,1)S(1)}, u32[]{:S(2)}, u32[]{:S(2)}) async-start(bf16[8,48,128]{2,1,0:T(8,128)(2,1)} %bitcast.12), calls=%async_computation.2 | async-start | bytes 196608 | tf_op jit(solution)/shard_map/all_to_all | solution.py:369

commit v8 on v7

--- a/solution.py
+++ b/solution.py
@@ -276,9 +276,16 @@
         coefs = dot(coef, (line == adapter + b * ADP_DEV).astype(BF))
         for p in range(ADP_DEV * RANK // 128):
             blocks.append((coefs[:, p * 128 : (p + 1) * 128] * mixed).astype(BF))
-    for copy in copies:
+    depth = SIDES * ADP_DEV * RANK // 2
+    middle = len(blocks) // 2
+    for copy in copies[: SIDES // 2]:
         copy.wait()
-    total = dot(jnp.concatenate(blocks, axis=1), held[...].reshape(SIDES * ADP_DEV * RANK, COLS))
+    near = held[pl.ds(0, SIDES // 2), :, :].reshape(depth, COLS)
+    total = dot(jnp.concatenate(blocks[:middle], axis=1), near)
+    for copy in copies[SIDES // 2 :]:
+        copy.wait()
+    rest = held[pl.ds(SIDES // 2, SIDES // 2), :, :].reshape(depth, COLS)
+    total = total + dot(jnp.concatenate(blocks[middle:], axis=1), rest)
     out[...] = total.astype(BF)
 
 

time: 120 us -> 120 us (level)
  no operation moved by 1% of the time
where the time goes in v8:
time: 120 us; the launch traced here: 119 us
  waiting for transfers between devices  39.1 us (33%)
  starting transfers between devices  37.3 us (31%)
  Pallas kernels  15.1 us (13%)
  blocking collectives  14.1 us (12%)
  matrix products  4.95 us (4%)
  local copies, waits for them, and re-layouts  4.9 us (4%)
  other arithmetic  2.91 us (2%)
    all_to_all x3, waiting for transfers between devices, swap(): lax.all_to_all(x, axis, split_axis=0, concat_axis=0, axis_index_groups=gr...  32 us
    all_to_all x3, starting transfers between devices, swap(): lax.all_to_all(x, axis, split_axis=0, concat_axis=0, axis_index_groups=gr...  21.8 us
    all_to_all x1, blocking collectives, swap(): lax.all_to_all(x, axis, split_axis=0, concat_axis=0, axis_index_groups=gr...  14.1 us
    ppermute x8, starting transfers between devices, turn(): return lax.ppermute(x, 'tensor', pairs)  10.8 us
    ppermute x8, waiting for transfers between devices, turn(): return lax.ppermute(x, 'tensor', pairs)  7.05 us
    dot_general x1, matrix products, frozen_sum(): part = jnp.dot(attended, out_weight, preferred_element_type=F32)  4.95 us
    ppermute x4, starting transfers between devices, beside(): return lax.ppermute(x, 'adapter', pairs)  4.75 us
    pallas_call x1, Pallas kernels, lower(): pl.pallas_call(lower_kernel, out_shape=shape_of(LINES, 256), in_specs=[pl...  4.29 us
  transfers between devices with their start and end apart: 15, of which 8 were waited for; matrix products, arithmetic and copies ran while one was open for 10% of the time, Pallas kernels for 5%

profile of v8, /device:TPU:32, one launch (start us, length us, event | category | flops | bytes accessed | tf_op | source)
XLA Modules:
  0.0 118.5 jit_solution(7080114615725722417)
XLA Ops:
  0.0 4.0 %shard_map.109 = (bf16[48,1024]{1,0:T(8,128)(2,1)S(1)}, bf16[256,3200]{1,0:T(8,128)(2,1)}) custom-call(bf16[48,1024]{1,0:T(8,128)(2,1)} %q_hbm.1, bf16[1536,128]{1,0:T(8,128)(2,1)} %bitcast.34, bf16[1536,128]{1,0:T(8,128)(2,1)} %bitcast.35, bf16[48,128]{1,0:T(8,128)(2,1)} %nk_hbm.1, bf16[48,128]{1,0:T(8,128)(2,1)} %nv_hbm.1, s32[1,48]{1,0:T(1,128)} %bitcast.36, ...), custom_call_target="tpu_custom_call" | custom-call | tf_op jit(solution)/shard_map/pallas_call | solution.py:328
  4.0 11.4 %all-to-all-start = ((bf16[32,8,3200]{2,1,0:T(8,128)(2,1)}), bf16[32,8,3200]{2,1,0:T(8,128)(2,1)S(1)}, u32[]{:S(2)}, u32[]{:S(2)}) async-start(bf16[32,8,3200]{2,1,0:T(8,128)(2,1)} %bitcast.6), calls=%async_computation | async-start | bytes 3276800 | tf_op jit(solution)/shard_map/all_to_all | solution.py:376
  15.4 5.0 %fusion.2 = f32[48,4096]{1,0:T(8,128)S(1)} fusion(bf16[48,1024]{1,0:T(8,128)(2,1)S(1)} %get-tuple-element.23.after, bf16[1024,4096]{1,0:T(8,128)(2,1)} %param.17), kind=kOutput, calls=%fused_computation.8 | convolution fusion | flops 402653184 | bytes 9273344 | tf_op jit(solution)/shard_map/dot_general | solution.py:396
  20.4 1.6 %reshape.35 = f32[48,4,2,512]{3,2,1,0:T(2,128)} reshape(f32[48,4096]{1,0:T(8,128)S(1)} %fusion.2) | data formatting | bytes 1572864 | tf_op jit(solution)/shard_map/reshape | solution.py:397
  21.9 2.2 %fusion.1 = (f32[48,4,1,512]{3,2,1,0:T(1,128)S(1)}, f32[48,4,1,512]{3,2,1,0:T(1,128)S(1)}) fusion(f32[48,4,2,512]{3,2,1,0:T(2,128)} %reshape.35), kind=kLoop, calls=%fused_computation.7 | loop fusion | bytes 1572864 | tf_op jit(solution)/shard_map/slice | solution.py:398
  24.1 0.8 fusion
  24.9 2.7 %collective-permute-start.4 = (bf16[1024,512]{1,0:T(8,128)(2,1)}, bf16[1024,512]{1,0:T(8,128)(2,1)S(1)}, u32[]{:S(2)}, u32[]{:S(2)}) collective-permute-start(bf16[1024,512]{1,0:T(8,128)(2,1)} %refs_0_.1), channel_id=1, source_target_pairs={{0,192},{8,200},{16,208},{24,216},{32,224},{40,232},{48,240},{56,2... | collective-permute-start | bytes 3145736 | tf_op jit(solution)/shard_map/ppermute | solution.py:383
  27.7 1.2 %bitcast_add_fusion = f32[48,4,512]{2,1,0:T(4,128)S(1)} fusion(bf16[48,4,512]{2,1,0:T(4,128)(2,1)S(1)} %collective-permute-done, f32[48,4,1,512]{3,2,1,0:T(1,128)S(1)} %get-tuple-element.39, f32[48,4,1,512]{3,2,1,0:T(1,128)} %copy-done.3, pred[]{:T(512)S(6)} %eq.9), kind=kLoop, calls=%fused_computation | loop fusion | flops 294912 | bytes 1376257 | tf_op jit(solution)/shard_map/add | solution.py:401
  29.1 1.6 %collective-permute-start.1 = (bf16[48,512]{1,0:T(8,128)(2,1)S(1)}, bf16[48,512]{1,0:T(8,128)(2,1)S(1)}, u32[]{:S(2)}, u32[]{:S(2)}) collective-permute-start(bf16[48,512]{1,0:T(8,128)(2,1)S(1)} %get-tuple-element.41), channel_id=1, source_target_pairs={{0,2},{1,3},{2,4},{3,5},{4,6},{5,7},{6,0},{7,1},{8,10},{9,11},{10,... | collective-permute-start | bytes 147464 | tf_op jit(solution)/shard_map/ppermute | solution.py:390
  30.7 2.7 %collective-permute-start.2 = (bf16[48,512]{1,0:T(8,128)(2,1)S(1)}, bf16[48,512]{1,0:T(8,128)(2,1)S(1)}, u32[]{:S(2)}, u32[]{:S(2)}) collective-permute-start(bf16[48,512]{1,0:T(8,128)(2,1)S(1)} %get-tuple-element.43), channel_id=1, source_target_pairs={{0,4},{1,5},{2,6},{3,7},{4,0},{5,1},{6,2},{7,3},{8,12},{9,13},{10,... | collective-permute-start | bytes 147464 | tf_op jit(solution)/shard_map/ppermute | solution.py:390
  33.4 1.4 %collective-permute-start.3 = (bf16[48,512]{1,0:T(8,128)(2,1)S(1)}, bf16[48,512]{1,0:T(8,128)(2,1)}, u32[]{:S(2)}, u32[]{:S(2)}) collective-permute-start(bf16[48,512]{1,0:T(8,128)(2,1)S(1)} %get-tuple-element.42), channel_id=1, source_target_pairs={{0,6},{1,7},{2,0},{3,1},{4,2},{5,3},{6,4},{7,5},{8,14},{9,15},{10,... | collective-permute-start | bytes 147464 | tf_op jit(solution)/shard_map/ppermute | solution.py:390
  35.1 1.2 %collective-permute-done.2 = bf16[48,512]{1,0:T(8,128)(2,1)S(1)} collective-permute-done((bf16[48,512]{1,0:T(8,128)(2,1)S(1)}, bf16[48,512]{1,0:T(8,128)(2,1)S(1)}, u32[]{:S(2)}, u32[]{:S(2)}) %collective-permute-start.2) | collective-permute-done | bytes 49184 | tf_op jit(solution)/shard_map/ppermute | solution.py:390
  36.3 1.3 %collective-permute-done.3 = bf16[48,512]{1,0:T(8,128)(2,1)} collective-permute-done((bf16[48,512]{1,0:T(8,128)(2,1)S(1)}, bf16[48,512]{1,0:T(8,128)(2,1)}, u32[]{:S(2)}, u32[]{:S(2)}) %collective-permute-start.3) | collective-permute-done | bytes 49184 | tf_op jit(solution)/shard_map/ppermute | solution.py:390
  37.6 0.8 convert_add_fusion.frozen
  38.4 17.2 %all-to-all-done = bf16[32,8,3200]{2,1,0:T(8,128)(2,1)S(1)} async-done(((bf16[32,8,3200]{2,1,0:T(8,128)(2,1)}), bf16[32,8,3200]{2,1,0:T(8,128)(2,1)S(1)}, u32[]{:S(2)}, u32[]{:S(2)}) %all-to-all-start) | async-done | bytes 1638432 | tf_op jit(solution)/shard_map/all_to_all | solution.py:376
  55.6 4.3 %shard_map.111 = bf16[256,256]{1,0:T(8,128)(2,1)} custom-call(bf16[256,3200]{1,0:T(8,128)(2,1)S(1)} %bitcast.22, bf16[1024,1024]{1,0:T(8,128)(2,1)} %down.1), custom_call_target="tpu_custom_call" | custom-call | tf_op jit(solution)/shard_map/pallas_call | solution.py:351
  59.9 6.2 %all-to-all-start.1 = ((bf16[32,8,256]{2,1,0:T(8,128)(2,1)}), bf16[32,8,256]{2,1,0:T(8,128)(2,1)S(1)}, u32[]{:S(2)}, u32[]{:S(2)}) async-start(bf16[32,8,256]{2,1,0:T(8,128)(2,1)} %bitcast.10), calls=%async_computation.1 | async-start | bytes 262144 | tf_op jit(solution)/shard_map/all_to_all | solution.py:376
  66.2 1.0 copy-done.2
  67.2 1.2 %shard_map.112 = (bf16[512,512]{1,0:T(8,128)(2,1)S(1)}, bf16[512,512]{1,0:T(8,128)(2,1)S(1)}) custom-call(bf16[1024,512]{1,0:T(8,128)(2,1)} %copy-done.2, bf16[1024,512]{1,0:T(8,128)(2,1)} %collective-permute-done.5.behind.refs_2_), custom_call_target="tpu_custom_call" | custom-call | tf_op jit(solution)/shard_map/pallas_call | solution.py:302
  68.4 7.5 %all-to-all-done.1 = bf16[32,8,256]{2,1,0:T(8,128)(2,1)S(1)} async-done(((bf16[32,8,256]{2,1,0:T(8,128)(2,1)}), bf16[32,8,256]{2,1,0:T(8,128)(2,1)S(1)}, u32[]{:S(2)}, u32[]{:S(2)}) %all-to-all-start.1) | async-done | bytes 131104 | tf_op jit(solution)/shard_map/all_to_all | solution.py:376
  76.2 1.2 collective-permute-done.6
  77.4 1.1 collective-permute-start.10
  78.4 1.0 collective-permute-start.11
  79.4 1.5 %collective-permute-start.7 = (f32[24,128]{1,0:T(8,128)S(1)}, f32[24,128]{1,0:T(8,128)S(1)}, u32[]{:S(2)}, u32[]{:S(2)}) collective-permute-start(f32[24,128]{1,0:T(8,128)S(1)} %add.65.own), channel_id=1, source_target_pairs={{0,2},{1,3},{2,4},{3,5},{4,6},{5,7},{6,0},{7,1},{8,10},{9,11},{10,... | collective-permute-start | bytes 36872 | tf_op jit(solution)/shard_map/ppermute | solution.py:390
  80.9 1.8 %collective-permute-start.8 = (f32[24,128]{1,0:T(8,128)S(1)}, f32[24,128]{1,0:T(8,128)S(1)}, u32[]{:S(2)}, u32[]{:S(2)}) collective-permute-start(f32[24,128]{1,0:T(8,128)S(1)} %add.65.own), channel_id=1, source_target_pairs={{0,6},{1,7},{2,0},{3,1},{4,2},{5,3},{6,4},{7,5},{8,14},{9,15},{10,... | collective-permute-start | bytes 36872 | tf_op jit(solution)/shard_map/ppermute | solution.py:390
  82.6 1.8 %collective-permute-start.9 = (f32[24,128]{1,0:T(8,128)S(1)}, f32[24,128]{1,0:T(8,128)S(1)}, u32[]{:S(2)}, u32[]{:S(2)}) collective-permute-start(f32[24,128]{1,0:T(8,128)S(1)} %add.65.own), channel_id=1, source_target_pairs={{0,4},{1,5},{2,6},{3,7},{4,0},{5,1},{6,2},{7,3},{8,12},{9,13},{10,... | collective-permute-start | bytes 36872 | tf_op jit(solution)/shard_map/ppermute | solution.py:390
  84.6 3.3 %collective-permute-done.9.across = f32[24,128]{1,0:T(8,128)S(1)} collective-permute-done((f32[24,128]{1,0:T(8,128)S(1)}, f32[24,128]{1,0:T(8,128)S(1)}, u32[]{:S(2)}, u32[]{:S(2)}) %collective-permute-start.9) | collective-permute-done | bytes 12320 | tf_op jit(solution)/shard_map/ppermute | solution.py:390
  87.8 0.7 shard_map.114
  88.5 4.2 %all-to-all-start.2 = ((bf16[8,48,128]{2,1,0:T(8,128)(2,1)}), bf16[8,48,128]{2,1,0:T(8,128)(2,1)S(1)}, u32[]{:S(2)}, u32[]{:S(2)}) async-start(bf16[8,48,128]{2,1,0:T(8,128)(2,1)} %bitcast.12), calls=%async_computation.2 | async-start | bytes 196608 | tf_op jit(solution)/shard_map/all_to_all | solution.py:376
  92.7 7.3 %all-to-all-done.2 = bf16[8,48,128]{2,1,0:T(8,128)(2,1)S(1)} async-done(((bf16[8,48,128]{2,1,0:T(8,128)(2,1)}), bf16[8,48,128]{2,1,0:T(8,128)(2,1)S(1)}, u32[]{:S(2)}, u32[]{:S(2)}) %all-to-all-start.2) | async-done | bytes 98336 | tf_op jit(solution)/shard_map/all_to_all | solution.py:376
  100.0 3.7 %shard_map.115 = bf16[384,512]{1,0:T(8,128)(2,1)S(1)} custom-call(s32[1,1]{1,0:T(1,128)} %bitcast.place, bf16[384,128]{1,0:T(8,128)(2,1)S(1)} %bitcast.26, bf16[1024,512]{1,0:T(8,128)(2,1)} %refs_0_.1, bf16[1024,512]{1,0:T(8,128)(2,1)} %copy-done.2, bf16[1024,512]{1,0:T(8,128)(2,1)} %collective-permute-done.5.behind.refs_2_, ...), custom_call_target="tpu_custom_call" | custom-call | tf_op jit(solution)/shard_map/pallas_call | solution.py:313
  103.7 14.1 %all_to_all.46 = bf16[8,48,512]{2,1,0:T(8,128)(2,1)S(1)} all-to-all(bf16[8,48,512]{2,1,0:T(8,128)(2,1)S(1)} %bitcast.23), channel_id=1, replica_groups={{0,8,16,24,32,40,48,56},{64,72,80,88,96,104,112,120},{128,136,144,152,1..., dimensions={0} | all-to-all | bytes 786432 | tf_op jit(solution)/shard_map/all_to_all | solution.py:376
  (25 shorter events, 1.6 us)
Async XLA Ops:
  4.0 51.6 %all-to-all-start = ((bf16[32,8,3200]{2,1,0:T(8,128)(2,1)}), bf16[32,8,3200]{2,1,0:T(8,128)(2,1)S(1)}, u32[]{:S(2)}, u32[]{:S(2)}) async-start(bf16[32,8,3200]{2,1,0:T(8,128)(2,1)} %bitcast.6), calls=%async_computation | async-start | bytes 3276800 | tf_op jit(solution)/shard_map/all_to_all | solution.py:376
  15.4 19.5 %copy-start = (s32[48,4]{0,1:T(4,128)S(1)}, s32[48,4]{0,1:T(4,128)}, u32[]{:S(2)}) copy-start(s32[48,4]{0,1:T(4,128)} %param.20) | copy-start | bytes 2308
  15.4 19.5 %copy-start.1 = (f32[48,4]{0,1:T(4,128)S(1)}, f32[48,4]{0,1:T(4,128)}, u32[]{:S(2)}) copy-start(f32[48,4]{0,1:T(4,128)} %param.21) | copy-start | bytes 2308
  24.1 0.9 copy-start.3
  24.9 2.7 %collective-permute-start = (bf16[48,4,512]{2,1,0:T(4,128)(2,1)}, bf16[48,4,512]{2,1,0:T(4,128)(2,1)S(1)}, u32[]{:S(2)}, u32[]{:S(2)}) collective-permute-start(bf16[48,4,512]{2,1,0:T(4,128)(2,1)} %fusion), channel_id=1, source_target_pairs={{0,1},{1,0},{2,3},{3,2},{4,5},{5,4},{6,7},{7,6},{8,9},{9,8},{10,11... | collective-permute-start | bytes 589832 | tf_op jit(solution)/shard_map/ppermute | solution.py:390
  24.9 41.2 %collective-permute-start.4 = (bf16[1024,512]{1,0:T(8,128)(2,1)}, bf16[1024,512]{1,0:T(8,128)(2,1)S(1)}, u32[]{:S(2)}, u32[]{:S(2)}) collective-permute-start(bf16[1024,512]{1,0:T(8,128)(2,1)} %refs_0_.1), channel_id=1, source_target_pairs={{0,192},{8,200},{16,208},{24,216},{32,224},{40,232},{48,240},{56,2... | collective-permute-start | bytes 3145736 | tf_op jit(solution)/shard_map/ppermute | solution.py:383
  27.7 38.5 %collective-permute-start.5 = (bf16[1024,512]{1,0:T(8,128)(2,1)}, bf16[1024,512]{1,0:T(8,128)(2,1)}, u32[]{:S(2)}, u32[]{:S(2)}) collective-permute-start(bf16[1024,512]{1,0:T(8,128)(2,1)} %refs_0_.1), channel_id=1, source_target_pairs={{0,64},{8,72},{16,80},{24,88},{32,96},{40,104},{48,112},{56,120},{... | collective-permute-start | bytes 3145736 | tf_op jit(solution)/shard_map/ppermute | solution.py:383
  29.1 6.0 %collective-permute-start.1 = (bf16[48,512]{1,0:T(8,128)(2,1)S(1)}, bf16[48,512]{1,0:T(8,128)(2,1)S(1)}, u32[]{:S(2)}, u32[]{:S(2)}) collective-permute-start(bf16[48,512]{1,0:T(8,128)(2,1)S(1)} %get-tuple-element.41), channel_id=1, source_target_pairs={{0,2},{1,3},{2,4},{3,5},{4,6},{5,7},{6,0},{7,1},{8,10},{9,11},{10,... | collective-permute-start | bytes 147464 | tf_op jit(solution)/shard_map/ppermute | solution.py:390
  30.7 5.6 %collective-permute-start.2 = (bf16[48,512]{1,0:T(8,128)(2,1)S(1)}, bf16[48,512]{1,0:T(8,128)(2,1)S(1)}, u32[]{:S(2)}, u32[]{:S(2)}) collective-permute-start(bf16[48,512]{1,0:T(8,128)(2,1)S(1)} %get-tuple-element.43), channel_id=1, source_target_pairs={{0,4},{1,5},{2,6},{3,7},{4,0},{5,1},{6,2},{7,3},{8,12},{9,13},{10,... | collective-permute-start | bytes 147464 | tf_op jit(solution)/shard_map/ppermute | solution.py:390
  33.4 4.2 %collective-permute-start.3 = (bf16[48,512]{1,0:T(8,128)(2,1)S(1)}, bf16[48,512]{1,0:T(8,128)(2,1)}, u32[]{:S(2)}, u32[]{:S(2)}) collective-permute-start(bf16[48,512]{1,0:T(8,128)(2,1)S(1)} %get-tuple-element.42), channel_id=1, source_target_pairs={{0,6},{1,7},{2,0},{3,1},{4,2},{5,3},{6,4},{7,5},{8,14},{9,15},{10,... | collective-permute-start | bytes 147464 | tf_op jit(solution)/shard_map/ppermute | solution.py:390
  59.9 16.0 %all-to-all-start.1 = ((bf16[32,8,256]{2,1,0:T(8,128)(2,1)}), bf16[32,8,256]{2,1,0:T(8,128)(2,1)S(1)}, u32[]{:S(2)}, u32[]{:S(2)}) async-start(bf16[32,8,256]{2,1,0:T(8,128)(2,1)} %bitcast.10), calls=%async_computation.1 | async-start | bytes 262144 | tf_op jit(solution)/shard_map/all_to_all | solution.py:376
  66.1 1.0 copy-start.2
  76.1 1.2 %collective-permute-start.6 = (f32[24,128]{1,0:T(8,128)S(1)}, f32[24,128]{1,0:T(8,128)S(1)}, u32[]{:S(2)}, u32[]{:S(2)}) collective-permute-start(f32[24,128]{1,0:T(8,128)S(1)} %shard_map.113), channel_id=1, source_target_pairs={{0,1},{1,0},{2,3},{3,2},{4,5},{5,4},{6,7},{7,6},{8,9},{9,8},{10,11... | collective-permute-start | bytes 36872 | tf_op jit(solution)/shard_map/ppermute | solution.py:390
  77.4 22.7 %collective-permute-start.10 = (bf16[512,512]{1,0:T(8,128)(2,1)S(1)}, bf16[512,512]{1,0:T(8,128)(2,1)S(1)}, u32[]{:S(2)}, u32[]{:S(2)}) collective-permute-start(bf16[512,512]{1,0:T(8,128)(2,1)S(1)} %get-tuple-element.36), channel_id=1, source_target_pairs={{0,192},{8,200},{16,208},{24,216},{32,224},{40,232},{48,240},{56,2... | collective-permute-start | bytes 1572872 | tf_op jit(solution)/shard_map/ppermute | solution.py:383
  78.4 21.6 %collective-permute-start.11 = (bf16[512,512]{1,0:T(8,128)(2,1)S(1)}, bf16[512,512]{1,0:T(8,128)(2,1)S(1)}, u32[]{:S(2)}, u32[]{:S(2)}) collective-permute-start(bf16[512,512]{1,0:T(8,128)(2,1)S(1)} %get-tuple-element.37), channel_id=1, source_target_pairs={{0,64},{8,72},{16,80},{24,88},{32,96},{40,104},{48,112},{56,120},{... | collective-permute-start | bytes 1572872 | tf_op jit(solution)/shard_map/ppermute | solution.py:383
  79.4 5.0 %collective-permute-start.7 = (f32[24,128]{1,0:T(8,128)S(1)}, f32[24,128]{1,0:T(8,128)S(1)}, u32[]{:S(2)}, u32[]{:S(2)}) collective-permute-start(f32[24,128]{1,0:T(8,128)S(1)} %add.65.own), channel_id=1, source_target_pairs={{0,2},{1,3},{2,4},{3,5},{4,6},{5,7},{6,0},{7,1},{8,10},{9,11},{10,... | collective-permute-start | bytes 36872 | tf_op jit(solution)/shard_map/ppermute | solution.py:390
  80.9 3.7 %collective-permute-start.8 = (f32[24,128]{1,0:T(8,128)S(1)}, f32[24,128]{1,0:T(8,128)S(1)}, u32[]{:S(2)}, u32[]{:S(2)}) collective-permute-start(f32[24,128]{1,0:T(8,128)S(1)} %add.65.own), channel_id=1, source_target_pairs={{0,6},{1,7},{2,0},{3,1},{4,2},{5,3},{6,4},{7,5},{8,14},{9,15},{10,... | collective-permute-start | bytes 36872 | tf_op jit(solution)/shard_map/ppermute | solution.py:390
  82.6 5.2 %collective-permute-start.9 = (f32[24,128]{1,0:T(8,128)S(1)}, f32[24,128]{1,0:T(8,128)S(1)}, u32[]{:S(2)}, u32[]{:S(2)}) collective-permute-start(f32[24,128]{1,0:T(8,128)S(1)} %add.65.own), channel_id=1, source_target_pairs={{0,4},{1,5},{2,6},{3,7},{4,0},{5,1},{6,2},{7,3},{8,12},{9,13},{10,... | collective-permute-start | bytes 36872 | tf_op jit(solution)/shard_map/ppermute | solution.py:390
  88.5 11.5 %all-to-all-start.2 = ((bf16[8,48,128]{2,1,0:T(8,128)(2,1)}), bf16[8,48,128]{2,1,0:T(8,128)(2,1)S(1)}, u32[]{:S(2)}, u32[]{:S(2)}) async-start(bf16[8,48,128]{2,1,0:T(8,128)(2,1)} %bitcast.12), calls=%async_computation.2 | async-start | bytes 196608 | tf_op jit(solution)/shard_map/all_to_all | solution.py:376
